TPU v7x, 32 devices: a whole 2x2x4 slice. The times are simulated.
32 devices in a mesh: seq: 8 (over z, x), tp: 4 (over y, core).
Axes of the slice: x: 2, y: 2, z: 4, core: 2. Of those that a mesh axis runs over, the one named last changes fastest.
Arguments:
- tokens: bfloat16 [4096, 2048], P('seq', 'tp'), may hold values from -6 to 6
- norm_gain: float32 [2048], replicated, may hold values from 0.1 to 1.9
- w_query: bfloat16 [2048, 2048], P(None, 'tp'), may hold values from -0.125 to 0.125
- w_keyval: bfloat16 [2048, 256], replicated, may hold values from -0.125 to 0.125
- w_out: bfloat16 [2048, 2048], P('tp'), may hold values from -0.5 to 0.5
- span_lens: int32 [8], P('seq'), may hold values from 1 to 512, 3072 in all
- cached_lens: int32 [8], P('seq'), may hold values from 1 to 1536, 6144 in all
- old_table: int32 [8, 8], P('seq'), may hold values from 0 to 7, each once within a row
- new_table: int32 [8, 8], P('seq'), may hold values from 0 to 7, each once within a row
- old_cache: bfloat16 [64, 256, 256], P('seq', 'tp'), may hold values from -720 to 720
Outputs:
- mixed: bfloat16 [4096, 2048], P('seq', 'tp')
- new_cache: bfloat16 [64, 256, 256], P('seq', 'tp')
Inputs may be any that keep to these rules, and one draw needn't show every extreme that they name: Request r's new tokens are the first span_lens[r] of its 512 rows. `old_table`: each row names every device once: each device holds exactly one block of every request. `new_table`: each row names every device once: each device receives exactly one block of every request.
All inputs are finite; a program needn't handle non-finite values. No bound on the sum of `span_lens` or of `cached_lens` on one device may be relied on, other than what follows from the above.
Results may differ from a plain program's by a relative error of at most 0.012.
The roundings to bfloat16 on the way count: a program that leaves them out, or rounds other values in their place, can miss the bound.
Values may be sent and summed in bfloat16 or wider, within the bound.
No kernel may reach another device: no remote copies, remote signals or barrier semaphores. Data moves between devices by JAX's collectives and lax.ppermute only.
A program may use at most 128 MiB of HBM per device.

v0:
```python
import functools
import math

import jax
import jax.numpy as jnp
from jax import lax
from jax.experimental import pallas as pl
from jax.experimental.pallas import tpu as pltpu
from jax.sharding import PartitionSpec as P

EPSILON = 1e-05
MASKED = -1e30
CHUNKS = 2
PART_ROWS = 256
ROW_TILE = 128
KEY_TILE = 128
NORM_ROWS = 128
MIB = 51
PROJECT_MIB = 50.375
LEAST = -3e38
ATTEND_MIB = 49
SAFE = 60.0
F32 = jnp.float32
BF16 = jnp.bfloat16

VMEM = pl.BlockSpec(memory_space=pltpu.VMEM)
SMEM = pl.BlockSpec(memory_space=pltpu.SMEM)
HBM = pl.BlockSpec(memory_space=pltpu.HBM)


def dot(a, b):
    return lax.dot_general(a, b, (((1,), (0,)), ((), ())), preferred_element_type=F32)


def dot_t(a, b):
    return lax.dot_general(a, b, (((1,), (1,)), ((), ())), preferred_element_type=F32)


def pair_kernel(keep_ref, got_ref, *pair_refs):
    for k, pair_ref in enumerate(pair_refs):
        pair_ref[0] = keep_ref[k]
        pair_ref[1] = got_ref[k]


def order_kernel(share, plan_ref, arrived_ref, out_ref):
    rows, count = out_ref.shape[0], arrived_ref.shape[0]
    if share % 16 == 0:
        for b in range(rows // share):
            at = pl.ds(pl.multiple_of(plan_ref[2 + b] * share, share), share)
            out_ref[pl.ds(b * share, share), :] = arrived_ref[at, :]
        return
    row = lax.broadcasted_iota(jnp.int32, (rows, 128), 0)
    block = row // share
    holder = jnp.zeros_like(block)
    for b in range(rows // share):
        holder = jnp.where(block == b, plan_ref[2 + b], holder)
    index = (holder * share + row % share)[:, :1]
    column = lax.broadcasted_iota(jnp.int32, (rows, count), 1)
    pick = jnp.where(column == index, 1.0, 0.0).astype(BF16)
    out_ref[...] = dot(pick, arrived_ref[...]).astype(BF16)


def extend_kernel(share, block_rows, plan_ref, kv_ref, arrived_ref, *out_refs):
    rows = arrived_ref.shape[0]
    groups = rows // share
    held, span = plan_ref[0], plan_ref[1]
    me = lax.axis_index("seq") if len(out_refs) > 1 else 0
    row = lax.broadcasted_iota(jnp.int32, (rows, 128), 0)
    target = row // share
    block, holder = jnp.zeros_like(row), jnp.zeros_like(row)
    for b in range(groups):
        hit = target == plan_ref[2 + groups + b] ^ me
        block = jnp.where(hit, b, block)
        holder = jnp.where(hit, plan_ref[2 + b], holder)
    position = block * block_rows + lax.axis_index("tp") * share + row % share
    old_row = jnp.where(position < held, holder * share + row % share, -1)[:, :1]
    fresh = position - held
    new_row = jnp.where((fresh >= 0) & (fresh < span), fresh, -1)[:, :1]
    column = lax.broadcasted_iota(jnp.int32, (rows, rows), 1)
    total = dot(jnp.where(column == old_row, 1.0, 0.0).astype(BF16), arrived_ref[...])
    column = lax.broadcasted_iota(jnp.int32, (rows, kv_ref.shape[0]), 1)
    total += dot(jnp.where(column == new_row, 1.0, 0.0).astype(BF16), kv_ref[...])
    total = total.astype(BF16)
    if len(out_refs) == 1:
        out_refs[0][...] = total
        return
    for slot in range(groups):
        out_refs[slot % 2][slot // 2] = total[slot * share : (slot + 1) * share]


def project_kernel(
    x0,
    x1,
    x2,
    x3,
    gain_ref,
    wq_hbm,
    wkv_hbm,
    q_ref,
    kv_ref,
    values_ref,
    limits_ref,
    normed,
    wq_ref,
    wkv_ref,
    sems,
):
    pieces = (x0, x1, x2, x3)
    me = lax.axis_index("tp")
    rows, width = x0.shape
    features = width * len(pieces)
    hd = kv_ref.shape[1] // 2
    heads = wq_ref.shape[1] // hd
    loads = []
    for hbm, to in ((wkv_hbm, wkv_ref), (wq_hbm, wq_ref)):
        for j in range(len(pieces)):
            at = pl.ds(j * width, width)
            loads.append(pltpu.make_async_copy(hbm.at[at], to.at[at], sems.at[len(loads)]))
            loads[-1].start()

    for step in range(0, rows, NORM_ROWS):
        at = pl.ds(step, NORM_ROWS)
        values = [piece[at, :].astype(F32) for piece in pieces]
        average = jnp.sum(sum(values), axis=1, keepdims=True) / features
        centred = [v - average for v in values]
        spread = jnp.sum(sum(v * v for v in centred), axis=1, keepdims=True) / features
        scale = lax.rsqrt(spread + EPSILON)
        for j, v in enumerate(centred):
            owner = me ^ j
            to = pl.ds(pl.multiple_of(owner * width, width), width)
            normed[at, to] = (v * scale * gain_ref[owner]).astype(BF16)
    for load in loads[: len(pieces)]:
        load.wait()
    keyval = dot(normed[...], wkv_ref[...]).astype(BF16)
    kv_ref[...] = keyval
    values_ref[:, hd:] = keyval[:, hd:]
    values_ref[:, :hd] = jnp.ones((rows, hd), BF16)
    limits_ref[0] = longest(keyval[:, :hd])
    for load in loads[len(pieces) :]:
        load.wait()
    query = dot(normed[...], wq_ref[...]).astype(BF16)
    for start in range(0, rows, ROW_TILE):
        for h in range(heads):
            q_ref[pl.ds(start * heads + h * ROW_TILE, ROW_TILE), :] = query[
                start : start + ROW_TILE, h * hd : (h + 1) * hd
            ]
    limits_ref[1] = longest(q_ref[...])


def longest(x):
    squares = dot(x * x, jnp.ones((x.shape[1], 128), BF16))
    return jnp.max(squares.reshape(-1, 8, 128), axis=0)


def attend_kernel(share, block_rows, start_row, rows, plan_ref, q_ref, kv_ref, new_ref, *refs):
    limits_ref, pieces, wout_hbm = refs[0], refs[1:5], refs[5]
    total, high, context, wout, sem = refs[-5:]
    if start_row:
        old_ref, old_limit_ref, before_ref, far0_ref, far1_ref, near0_ref, near1_ref = refs[6:13]
    else:
        far1_ref, near1_ref, context_out, old_ref, old_limit_ref = refs[6:11]
    me = lax.axis_index("tp")
    held, span = plan_ref[0], plan_ref[1]
    piece_rows, width = pieces[0].shape
    hd = width // 2
    heads = q_ref.shape[0] // kv_ref.shape[0]
    load = pltpu.make_async_copy(wout_hbm, wout, sem)
    load.start()

    group = KEY_TILE * len(pieces)
    most = piece_rows // KEY_TILE
    tiles = (held + group - 1) // group
    if not start_row:
        row = lax.broadcasted_iota(jnp.int32, (KEY_TILE, hd), 0)
        place = row // share * block_rows + row % share
        limit = jnp.zeros((8, 128), F32)

        def lay(i, whole):
            source = pl.ds(i * KEY_TILE, KEY_TILE)
            for j, piece in enumerate(pieces):
                at = pl.ds(i * group + j * KEY_TILE, KEY_TILE)
                if whole:
                    old_ref[at, hd:] = piece[source, hd:]
                    old_ref[at, :hd] = jnp.ones((KEY_TILE, hd), BF16)
                    continue
                used = place + (me ^ j) * share + i * group < held
                old_ref[at, hd:] = jnp.where(used, piece[source, hd:].astype(F32), 0.0).astype(BF16)
                old_ref[at, :hd] = jnp.where(used, 1.0, 0.0).astype(BF16)

        for i in range(most):
            pl.when(i < tiles - 1)(functools.partial(lay, i, True))
            pl.when(i == tiles - 1)(functools.partial(lay, i, False))
        for piece in pieces:
            limit = jnp.maximum(limit, longest(piece[:, :hd]))
        old_limit_ref[...] = limit

    factor = hd ** (-0.5) * math.log2(math.e)
    key_limit = jnp.max(jnp.maximum(old_limit_ref[...], limits_ref[0]))
    small = key_limit * jnp.max(limits_ref[1]) * (1.05 / hd) < SAFE * SAFE

    tile_rows = ROW_TILE * heads

    def queries(t):
        return q_ref[pl.ds(start_row * heads + t * tile_rows, tile_rows), :]

    def old_keys(i):
        source = pl.ds(i * KEY_TILE, KEY_TILE)
        return jnp.concatenate([piece[source, :hd] for piece in pieces], axis=0)

    def new_scores(t):
        known = start_row + t * ROW_TILE
        scores = dot_t(queries(t), kv_ref[pl.ds(0, known + ROW_TILE), :hd])
        to = lax.broadcasted_iota(jnp.int32, (tile_rows, ROW_TILE), 0) % ROW_TILE
        by = lax.broadcasted_iota(jnp.int32, (tile_rows, ROW_TILE), 1)
        last = jnp.where(by <= to, scores[:, known:], MASKED)
        return jnp.concatenate([scores[:, :known], last], axis=1) if known else last

    def new_values(t):
        return new_ref[pl.ds(0, start_row + (t + 1) * ROW_TILE), :]

    def put(t, both):
        sums = both[:, :hd]
        inverse = pl.reciprocal(sums, approx=True)
        inverse = inverse * (2.0 - sums * inverse)
        out = (both[:, hd:] * inverse).astype(BF16)
        for h in range(heads):
            context[pl.ds(t * ROW_TILE, ROW_TILE), h * hd : (h + 1) * hd] = out[
                h * ROW_TILE : (h + 1) * ROW_TILE
            ]

    def fast(used, begin):
        row_tiles = range(begin // ROW_TILE, min(begin + PART_ROWS, rows) // ROW_TILE)
        steps = [(t, i) for t in row_tiles for i in range(used + 1)]

        def score(t, i):
            return new_scores(t) if i == used else dot_t(queries(t), old_keys(i))

        ahead, both = score(*steps[0]), None
        for at, (t, i) in enumerate(steps):
            scores = ahead
            if at + 1 < len(steps):
                ahead = score(*steps[at + 1])
            weights = jnp.exp2(scores * factor).astype(BF16)
            values = new_values(t) if i == used else old_ref[pl.ds(i * group, group), :]
            part = dot(weights, values)
            both = part if i == 0 else both + part
            if i == used:
                put(t, both)

    def exact(t):
        column = lax.broadcasted_iota(jnp.int32, (tile_rows, group), 1)
        within = column % KEY_TILE
        owner = me ^ (column // KEY_TILE)
        place = within // share * block_rows + within % share + owner * share

        def old_scores(i):
            scores = dot_t(queries(t), old_keys(pl.multiple_of(i, 1)))
            return jnp.where(place + i * group < held, scores, MASKED)

        def raise_high(i, carry):
            top = jnp.max(old_scores(i), axis=1, keepdims=True)
            high[...] = jnp.maximum(high[...], top)
            return carry

        def add(i, carry):
            weights = jnp.exp2((old_scores(i) - high[:, :1]) * factor).astype(BF16)
            total[...] += dot(weights, old_ref[pl.ds(pl.multiple_of(i * group, group), group), :])
            return carry

        high[...] = jnp.zeros_like(high) + jnp.max(new_scores(t), axis=1, keepdims=True)
        lax.fori_loop(0, tiles, raise_high, 0)
        weights = jnp.exp2((new_scores(t) - high[:, :1]) * factor).astype(BF16)
        total[...] = dot(weights, new_values(t))
        lax.fori_loop(0, tiles, add, 0)
        put(t, total[...])

    for begin in range(0, rows, PART_ROWS):
        busy = start_row + begin < span
        for used in range(1, most + 1):
            pl.when(busy & small & (tiles == used))(functools.partial(fast, used, begin))

        @pl.when(busy & jnp.logical_not(small))
        def _():
            for t in range(begin // ROW_TILE, min(begin + PART_ROWS, rows) // ROW_TILE):
                exact(t)

        @pl.when(jnp.logical_not(busy))
        def _():
            context[pl.ds(begin, PART_ROWS), :] = jnp.zeros((PART_ROWS, context.shape[1]), BF16)

    load.wait()
    cols = wout.shape[1] // 4

    def partial_sums(rows_of, k):
        columns = pl.ds(pl.multiple_of((me ^ k) * cols, cols), cols)
        return dot(rows_of[...], wout[:, columns]).astype(BF16)

    far1_ref[...] = partial_sums(context, 3)
    near1_ref[...] = partial_sums(context, 2)
    if not start_row:
        context_out[...] = context[...]
        return
    for at, rows_of in ((0, before_ref), (start_row, context)):
        far0_ref[pl.ds(at, rows), :] = partial_sums(rows_of, 1)
        near0_ref[pl.ds(at, rows), :] = partial_sums(rows_of, 0)


def hand_on_kernel(in_ref, out_ref):
    pass


def finish_kernel(at, phased, plan_ref, tokens_ref, near_ref, got_ref, crossed_ref, *refs):
    out_hbm, done, sems = refs[0 if not at else -3 - phased], refs[-2], refs[-1]
    rows = crossed_ref.shape[0]
    half = rows // 2
    stores = []
    if at and phased:
        me = lax.axis_index("seq")
        for k, pair_ref in enumerate(refs[:4]):
            for j in range(2):
                sem = sems.at[2 + len(stores)]
                slot = refs[-3].at[me ^ (2 * k + j)]
                stores.append(pltpu.make_async_copy(pair_ref.at[j], slot, sem))
                stores[-1].start()
    for i in range(2):
        here = pl.ds(i * half, half)
        there = pl.ds(at + i * half, half)
        kept = near_ref[there, :].astype(F32) + got_ref[there, :].astype(F32)
        total = tokens_ref[there, :].astype(F32) + (kept + crossed_ref[here, :].astype(F32))
        row = lax.broadcasted_iota(jnp.int32, total.shape, 0) + (at + i * half)
        done[here, :] = jnp.where(row < plan_ref[1], total, 0.0).astype(BF16)
        stores.append(pltpu.make_async_copy(done.at[here], out_hbm.at[there], sems.at[i]))
        stores[-1].start()
    for store in stores:
        store.wait()


def call(
    kernel, out_shape, in_specs, args, flops, mib=MIB, scratch=(), exps=0, name=None, into=None
):
    outs = out_shape if isinstance(out_shape, (list, tuple)) else [out_shape]
    moved = sum(a.size * a.dtype.itemsize for a in list(args) + list(outs))
    return pl.pallas_call(
        kernel,
        out_shape=out_shape,
        in_specs=in_specs,
        out_specs=jax.tree.map(lambda _: VMEM if into is None else HBM, out_shape),
        input_output_aliases=into or {},
        scratch_shapes=list(scratch),
        cost_estimate=pl.CostEstimate(flops=flops, bytes_accessed=moved, transcendentals=exps),
        compiler_params=pltpu.CompilerParams(vmem_limit_bytes=int(mib * 1024 * 1024)),
        name=name,
    )(*args)


def body(
    tokens,
    norm_gain,
    w_query,
    w_keyval,
    w_out,
    span_lens,
    cached_lens,
    old_table,
    new_table,
    old_cache,
):
    tp = lax.axis_size("tp")
    groups, share, width = old_cache.shape
    block_rows = share * tp
    capacity = groups * block_rows
    rows, cols = tokens.shape
    q_cols = w_query.shape[1]
    features = w_query.shape[0]
    hd = width // 2
    most_held = capacity - rows
    piece_rows = most_held // tp

    def swap(x, bit, axis="tp"):
        size = lax.axis_size(axis)
        return lax.ppermute(x, axis, [(i, i ^ bit) for i in range(size)])

    def exchange(x):
        return lax.all_to_all(x, "seq", split_axis=0, concat_axis=0, tiled=True)

    phased = groups == 8

    with jax.named_scope("tokens_gather"):
        across = swap(tokens, 2)
        beside = swap(tokens, 1)

    with jax.named_scope("cache_gather"):
        gain = jnp.maximum(norm_gain, LEAST).reshape(tp, 1, cols)
        gain, stored = lax.optimization_barrier((gain, old_cache))
        arrived = exchange(stored).reshape(groups * share, width)
        own = jnp.maximum(tokens, jnp.asarray(LEAST, BF16))
        across, *lens = lax.optimization_barrier(
            (across, cached_lens, span_lens, old_table[0], new_table[0])
        )
        plan = jnp.concatenate(lens)
        arrived, across, own, plan = lax.optimization_barrier((arrived, across, own, plan))
        ordered = call(
            functools.partial(order_kernel, share),
            jax.ShapeDtypeStruct((piece_rows, width), BF16),
            [SMEM, VMEM],
            (plan, arrived),
            flops=2 * piece_rows * groups * share * width,
            name="order",
        )
        c_across = swap(ordered, 2)
        c_beside = swap(ordered, 1)

    with jax.named_scope("project"):
        corner = swap(across, 1)
        stacked = rows * (q_cols // hd)
        query, keyval, values, limits = call(
            project_kernel,
            [
                jax.ShapeDtypeStruct((stacked, hd), BF16),
                jax.ShapeDtypeStruct((rows, width), BF16),
                jax.ShapeDtypeStruct((rows, width), BF16),
                jax.ShapeDtypeStruct((2, 8, 128), F32),
            ],
            [VMEM] * 5 + [HBM] * 2,
            (
                own,
                beside,
                across,
                corner,
                gain,
                w_query,
                w_keyval,
            ),
            flops=2 * rows * features * (q_cols + width),
            mib=PROJECT_MIB,
            scratch=[
                pltpu.VMEM((rows, features), BF16),
                pltpu.VMEM(w_query.shape, BF16),
                pltpu.VMEM(w_keyval.shape, BF16),
                pltpu.SemaphoreType.DMA((2 * tp,)),
            ],
            name="project",
        )

    with jax.named_scope("extend"):
        sent = call(
            functools.partial(extend_kernel, share, block_rows),
            [jax.ShapeDtypeStruct((groups // 2, share, width), BF16)] * 2
            if phased
            else [jax.ShapeDtypeStruct((groups * share, width), BF16)],
            [SMEM] + [VMEM] * 2,
            (plan, keyval, arrived),
            flops=4 * groups * share * groups * share * width,
            name="extend",
        )
        *sent, c_across = lax.optimization_barrier((*sent, c_across))
        if phased:
            keep, got = sent[0], swap(sent[1], 1, "seq")
        cached = (ordered, c_beside, c_across, swap(c_across, 1))

    part = rows // CHUNKS
    tile_rows = ROW_TILE * (q_cols // hd)
    old = []
    mixed = None
    for c in range(CHUNKS):
        last = c == CHUNKS - 1
        with jax.named_scope("attend"):
            of_part = jax.ShapeDtypeStruct((part, cols), BF16)
            of_all = jax.ShapeDtypeStruct((rows, cols), BF16)
            outs = [of_all, of_part, of_all, of_part]
            if not last:
                outs = [
                    of_part,
                    of_part,
                    jax.ShapeDtypeStruct((part, q_cols), BF16),
                    jax.ShapeDtypeStruct((most_held, width), BF16),
                    jax.ShapeDtypeStruct((8, 128), F32),
                ]
            seen = most_held + (c + 1) * part
            sums = list(call(
                functools.partial(attend_kernel, share, block_rows, c * part, part),
                outs,
                [SMEM] + [VMEM] * 8 + [HBM] + [VMEM] * len(old),
                (plan, query, keyval, values, limits, *cached, w_out, *old),
                flops=4 * part * seen * q_cols + 2 * part * q_cols * features,
                exps=part * seen * (q_cols // hd),
                mib=ATTEND_MIB,
                scratch=[
                    pltpu.VMEM((tile_rows, width), F32),
                    pltpu.VMEM((tile_rows, hd), F32),
                    pltpu.VMEM((part, q_cols), BF16),
                    pltpu.VMEM(w_out.shape, BF16),
                    pltpu.SemaphoreType.DMA,
                ],
                name="attend",
            ))
            if last:
                far0, far1, near0, near1 = sums
            else:
                far1, near1, before_rows, *old = sums
                old.append(before_rows)
        with jax.named_scope("reduce"):
            if c == 0 and phased:
                far1, got = lax.optimization_barrier((far1, got))
            got1 = swap(far1, 1)
            if c and last:
                before = pl.pallas_call(
                    hand_on_kernel,
                    out_shape=jax.ShapeDtypeStruct(before.shape, BF16),
                    in_specs=[pl.BlockSpec(memory_space=pl.ANY)],
                    out_specs=pl.BlockSpec(memory_space=pl.ANY),
                    input_output_aliases={0: 0},
                    cost_estimate=pl.CostEstimate(
                        flops=1 << 34, bytes_accessed=1024, transcendentals=0
                    ),
                    compiler_params=pltpu.CompilerParams(vmem_limit_bytes=1 << 20),
                    name="hand_on",
                )(before)
                before, got1 = lax.optimization_barrier((before, got1))
            pair = (near1.astype(F32) + got1.astype(F32)).astype(BF16)
            if not last:
                query, pair = lax.optimization_barrier((query, pair))
            if last and phased:
                pair, got = lax.optimization_barrier((pair, got))
            crossed = swap(pair, 2)
            if not last:
                before = crossed

    with jax.named_scope("exchange"):
        if phased:
            pairs = list(call(
                pair_kernel,
                [jax.ShapeDtypeStruct((2, share, width), BF16)] * (groups // 2),
                [VMEM] * 2,
                (keep, got),
                flops=0,
                mib=8,
                name="pair",
            ))
            for k in range(len(pairs) - 1, 0, -1):
                pairs[k] = swap(pairs[k], 2 * k, "seq")
        else:
            pairs = []
            new_cache = exchange(sent[0].reshape(groups, share, width))

    with jax.named_scope("finish"):
        got0 = swap(far0, 1)
        ends = (plan, own, near0, got0)
        out = jax.ShapeDtypeStruct((rows, cols), BF16)
        scratch = [pltpu.VMEM((part, cols), BF16)]
        mixed = call(
            functools.partial(finish_kernel, 0, phased),
            out,
            [SMEM] + [VMEM] * 4,
            (*ends, before),
            flops=4 * part * cols,
            scratch=scratch + [pltpu.SemaphoreType.DMA((2,))],
            name="finish",
            into={},
        )
        finished = call(
            functools.partial(finish_kernel, part, phased),
            [out, jax.ShapeDtypeStruct(old_cache.shape, BF16)] if phased else out,
            [SMEM] + [VMEM] * (4 + len(pairs)) + [HBM],
            (*ends, crossed, *pairs, mixed),
            flops=4 * part * cols,
            scratch=scratch + [pltpu.SemaphoreType.DMA((2 + groups * phased,))],
            name="finish",
            into={5 + len(pairs): 0},
        )
    return tuple(finished) if phased else (finished, new_cache)


def solution(mesh):
    in_specs = (
        P("seq", "tp"),
        P(),
        P(None, "tp"),
        P(),
        P("tp", None),
        P("seq"),
        P("seq"),
        P("seq", None),
        P("seq", None),
        P("seq", "tp", None),
    )
    out_specs = (P("seq", "tp"), P("seq", "tp", None))
    return jax.shard_map(body, mesh=mesh, in_specs=in_specs, out_specs=out_specs, check_vma=False)
```

profile of v0, /device:TPU:0, one launch (start us, length us, event | category | flops | bytes accessed | tf_op | source)
XLA Modules:
  0.0 62.6 jit_solution(5769605322295530889)
XLA Ops:
  0.6 3.0 %collective-permute-start = (bf16[512,512]{1,0:T(8,128)(2,1)}, bf16[512,512]{1,0:T(8,128)(2,1)S(1)}, u32[]{:S(2)}, u32[]{:S(2)}) collective-permute-start(bf16[512,512]{1,0:T(8,128)(2,1)} %param.10), channel_id=1, source_target_pairs={{0,2},{1,3},{2,0},{3,1},{4,6},{5,7},{6,4},{7,5},{8,10},{9,11},{10,... | collective-permute-start | bytes 1572872 | tf_op jit(solution)/shard_map/tokens_gather/ppermute | solution.py:381
  3.7 0.7 %broadcast_maximum_fusion.1 = f32[2048]{0:T(1024)S(1)} fusion(f32[2048]{0:T(1024)} %param.11), kind=kLoop, calls=%fused_computation.3 | loop fusion | flops 2048 | bytes 16384 | tf_op jit(solution)/shard_map/cache_gather/max | solution.py:393
  4.4 5.8 %all-to-all-start = ((bf16[8,64,256]{2,1,0:T(8,128)(2,1)}), bf16[8,64,256]{2,1,0:T(8,128)(2,1)S(1)}, u32[]{:S(2)}, u32[]{:S(2)}) async-start(bf16[8,64,256]{2,1,0:T(8,128)(2,1)} %param.19), calls=%async_computation | async-start | bytes 524288 | tf_op jit(solution)/shard_map/cache_gather/all_to_all | solution.py:384
  11.5 1.1 %broadcast_maximum_fusion.x0.tokens_ref = bf16[512,512]{1,0:T(8,128)(2,1)S(1)} fusion(bf16[512,512]{1,0:T(8,128)(2,1)} %param.10), kind=kLoop, calls=%fused_computation.2 | loop fusion | flops 262144 | bytes 1048576 | tf_op jit(solution)/shard_map/cache_gather/max | solution.py:396
  12.6 3.2 %collective-permute-done.x2 = bf16[512,512]{1,0:T(8,128)(2,1)S(1)} collective-permute-done((bf16[512,512]{1,0:T(8,128)(2,1)}, bf16[512,512]{1,0:T(8,128)(2,1)S(1)}, u32[]{:S(2)}, u32[]{:S(2)}) %collective-permute-start) | collective-permute-done | bytes 524320 | tf_op jit(solution)/shard_map/tokens_gather/ppermute | solution.py:381
  15.8 0.7 %pad_add_fusion.plan_ref = s32[18]{0:T(128)S(1)} fusion(s32[8]{0:T(128)} %bitcast.7, s32[8]{0:T(128)} %bitcast.8, s32[1]{0:T(128)S(6)} %copy.16, s32[1]{0:T(128)S(6)} %copy.17), kind=kLoop, calls=%fused_computation.4 | loop fusion | flops 54 | bytes 144 | tf_op jit(solution)/shard_map/cache_gather/concatenate | solution.py:400
  16.5 2.3 %all-to-all-done = bf16[8,64,256]{2,1,0:T(8,128)(2,1)S(1)} async-done(((bf16[8,64,256]{2,1,0:T(8,128)(2,1)}), bf16[8,64,256]{2,1,0:T(8,128)(2,1)S(1)}, u32[]{:S(2)}, u32[]{:S(2)}) %all-to-all-start) | async-done | bytes 262176 | tf_op jit(solution)/shard_map/cache_gather/all_to_all | solution.py:384
  18.8 0.6 order.1.refs_1_
  19.4 0.6 collective-permute-start.4
  20.7 4.1 %project.1 = (bf16[2048,128]{1,0:T(8,128)(2,1)S(1)}, bf16[512,256]{1,0:T(8,128)(2,1)S(1)}, bf16[512,256]{1,0:T(8,128)(2,1)S(1)}, f32[2,8,128]{2,1,0:T(8,128)S(1)}) custom-call(bf16[512,512]{1,0:T(8,128)(2,1)S(1)} %broadcast_maximum_fusion.x0.tokens_ref, bf16[512,512]{1,0:T(8,128)(2,1)S(1)} %collective-permute-done.1.x1, ...), custom_call_target="tpu_custom_call" | custom-call | flops 1610612736 | bytes 6307840 | tf_op jit(solution)/shard_map/project/project/pallas_call | solution.py:343
  24.8 1.2 %extend.1 = (bf16[4,64,256]{2,1,0:T(8,128)(2,1)S(1)}, bf16[4,64,256]{2,1,0:T(8,128)(2,1)S(1)}) custom-call(s32[18]{0:T(128)S(1)} %pad_add_fusion.plan_ref, bf16[512,256]{1,0:T(8,128)(2,1)S(1)} %get-tuple-element.54.kv_ref, bf16[512,256]{1,0:T(8,128)(2,1)S(1)} %bitcast.5), custom_call_target="tpu_custom_call" | custom-call | flops 268435456 | bytes 786504 | tf_op jit(solution)/shard_map/extend/extend/pallas_call | solution.py:343
  26.0 0.7 %collective-permute-done.4.refs_3_ = bf16[384,256]{1,0:T(8,128)(2,1)S(1)} collective-permute-done((bf16[384,256]{1,0:T(8,128)(2,1)S(1)}, bf16[384,256]{1,0:T(8,128)(2,1)S(1)}, u32[]{:S(2)}, u32[]{:S(2)}) %collective-permute-start.4) | collective-permute-done | bytes 196640 | tf_op jit(solution)/shard_map/cache_gather/ppermute | solution.py:381
  26.8 1.5 %collective-permute-start.6 = (bf16[4,64,256]{2,1,0:T(8,128)(2,1)S(1)}, bf16[4,64,256]{2,1,0:T(8,128)(2,1)S(1)}, u32[]{:S(2)}, u32[]{:S(2)}) collective-permute-start(bf16[4,64,256]{2,1,0:T(8,128)(2,1)S(1)} %get-tuple-element.63), channel_id=1, source_target_pairs={{0,4},{4,0},{8,12},{12,8},{16,20},{20,16},{24,28},{28,24},{1,5},{5... | collective-permute-start | bytes 393224 | tf_op jit(solution)/shard_map/extend/ppermute | solution.py:381
  28.2 5.1 %attend.2 = (bf16[256,512]{1,0:T(8,128)(2,1)S(1)}, bf16[256,512]{1,0:T(8,128)(2,1)S(1)}, bf16[256,512]{1,0:T(8,128)(2,1)S(1)}, bf16[1536,256]{1,0:T(8,128)(2,1)S(1)}, f32[8,128]{1,0:T(8,128)S(1)}) custom-call(s32[18]{0:T(128)S(1)} %pad_add_fusion.plan_ref, bf16[2048,128]{1,0:T(8,128)(2,1)S(1)} %get-tuple-element.65.q_ref, ...), custom_call_target="tpu_custom_call" | custom-call | flops 1476395008 | bytes 5517384 | tf_op jit(solution)/shard_map/attend/attend/pallas_call | solution.py:343
  33.6 1.3 %collective-permute-done.7 = bf16[256,512]{1,0:T(8,128)(2,1)S(1)} collective-permute-done((bf16[256,512]{1,0:T(8,128)(2,1)S(1)}, bf16[256,512]{1,0:T(8,128)(2,1)S(1)}, u32[]{:S(2)}, u32[]{:S(2)}) %collective-permute-start.7) | collective-permute-done | bytes 262176 | tf_op jit(solution)/shard_map/reduce/ppermute | solution.py:381
  35.0 0.7 %collective-permute-start.9 = (bf16[256,512]{1,0:T(8,128)(2,1)S(1)}, bf16[256,512]{1,0:T(8,128)(2,1)S(1)}, u32[]{:S(2)}, u32[]{:S(2)}) collective-permute-start(bf16[256,512]{1,0:T(8,128)(2,1)S(1)} %add_convert_fusion.1), channel_id=1, source_target_pairs={{0,2},{1,3},{2,0},{3,1},{4,6},{5,7},{6,4},{7,5},{8,10},{9,11},{10,... | collective-permute-start | bytes 786440 | tf_op jit(solution)/shard_map/reduce/ppermute | solution.py:381
  35.7 5.5 %attend.3 = (bf16[512,512]{1,0:T(8,128)(2,1)S(1)}, bf16[256,512]{1,0:T(8,128)(2,1)S(1)}, bf16[512,512]{1,0:T(8,128)(2,1)S(1)}, bf16[256,512]{1,0:T(8,128)(2,1)S(1)}) custom-call(s32[18]{0:T(128)S(1)} %pad_add_fusion.plan_ref, bf16[2048,128]{1,0:T(8,128)(2,1)S(1)} %get-tuple-element.65.q_ref, bf16[512,256]{1,0:T(8,128)(2,1)S(1)} %get-tuple-element.54.kv_ref, ...), custom_call_target="tpu_custom_call" | custom-call | flops 1610612736 | bytes 6565960 | tf_op jit(solution)/shard_map/attend/attend/pallas_call | solution.py:343
  41.8 1.7 %collective-permute-done.9.in_ref = bf16[256,512]{1,0:T(8,128)(2,1)S(1)} collective-permute-done((bf16[256,512]{1,0:T(8,128)(2,1)S(1)}, bf16[256,512]{1,0:T(8,128)(2,1)S(1)}, u32[]{:S(2)}, u32[]{:S(2)}) %collective-permute-start.9) | collective-permute-done | bytes 262176 | tf_op jit(solution)/shard_map/reduce/ppermute | solution.py:381
  43.6 0.8 %collective-permute-start.11 = (bf16[256,512]{1,0:T(8,128)(2,1)S(1)}, bf16[256,512]{1,0:T(8,128)(2,1)S(1)}, u32[]{:S(2)}, u32[]{:S(2)}) collective-permute-start(bf16[256,512]{1,0:T(8,128)(2,1)S(1)} %add_convert_fusion), channel_id=1, source_target_pairs={{0,2},{1,3},{2,0},{3,1},{4,6},{5,7},{6,4},{7,5},{8,10},{9,11},{10,... | collective-permute-start | bytes 786440 | tf_op jit(solution)/shard_map/reduce/ppermute | solution.py:381
  44.4 8.7 %collective-permute-start.12 = (bf16[2,64,256]{2,1,0:T(8,128)(2,1)S(1)}, bf16[2,64,256]{2,1,0:T(8,128)(2,1)S(1)}, u32[]{:S(2)}, u32[]{:S(2)}) collective-permute-start(bf16[2,64,256]{2,1,0:T(8,128)(2,1)S(1)} %get-tuple-element.80), channel_id=1, source_target_pairs={{0,8},{4,12},{8,0},{12,4},{16,24},{20,28},{24,16},{28,20},{1,9},{5... | collective-permute-start | bytes 196616 | tf_op jit(solution)/shard_map/exchange/ppermute | solution.py:381
  53.2 2.4 %collective-permute-start.14 = (bf16[2,64,256]{2,1,0:T(8,128)(2,1)S(1)}, bf16[2,64,256]{2,1,0:T(8,128)(2,1)S(1)}, u32[]{:S(2)}, u32[]{:S(2)}) collective-permute-start(bf16[2,64,256]{2,1,0:T(8,128)(2,1)S(1)} %get-tuple-element.82), channel_id=1, source_target_pairs={{0,24},{4,28},{8,16},{12,20},{16,8},{20,12},{24,0},{28,4},{1,25},{... | collective-permute-start | bytes 196616 | tf_op jit(solution)/shard_map/exchange/ppermute | solution.py:381
  55.6 1.4 %finish.2.refs_4_ = bf16[512,512]{1,0:T(8,128)(2,1)} custom-call(s32[18]{0:T(128)S(1)} %pad_add_fusion.plan_ref, bf16[512,512]{1,0:T(8,128)(2,1)S(1)} %broadcast_maximum_fusion.x0.tokens_ref, bf16[512,512]{1,0:T(8,128)(2,1)S(1)} %get-tuple-element.69.near_ref, bf16[512,512]{1,0:T(8,128)(2,1)S(1)} %collective-permute-done.8.got_ref, ...), custom_call_target="tpu_custom_call" | custom-call | flops 524288 | bytes 2359368 | tf_op jit(solution)/shard_map/finish/finish/pallas_call | solution.py:343
  57.0 4.0 %collective-permute-done.13.refs_2_ = bf16[2,64,256]{2,1,0:T(8,128)(2,1)S(1)} collective-permute-done((bf16[2,64,256]{2,1,0:T(8,128)(2,1)S(1)}, bf16[2,64,256]{2,1,0:T(8,128)(2,1)S(1)}, u32[]{:S(2)}, u32[]{:S(2)}) %collective-permute-start.13) | collective-permute-done | bytes 65568 | tf_op jit(solution)/shard_map/exchange/ppermute | solution.py:381
  61.0 1.4 %finish.3 = (bf16[512,512]{1,0:T(8,128)(2,1)}, bf16[8,64,256]{2,1,0:T(8,128)(2,1)}) custom-call(s32[18]{0:T(128)S(1)} %pad_add_fusion.plan_ref, bf16[512,512]{1,0:T(8,128)(2,1)S(1)} %broadcast_maximum_fusion.x0.tokens_ref, bf16[512,512]{1,0:T(8,128)(2,1)S(1)} %get-tuple-element.69.near_ref, ...), custom_call_target="tpu_custom_call", output_to_operand_aliasing={{0}: (9, {})} | custom-call | flops 524288 | bytes 3407944 | tf_op jit(solution)/shard_map/finish/finish/pallas_call | solution.py:343
  (22 shorter events, 1.9 us)
Async XLA Ops:
  0.6 15.2 %collective-permute-start = (bf16[512,512]{1,0:T(8,128)(2,1)}, bf16[512,512]{1,0:T(8,128)(2,1)S(1)}, u32[]{:S(2)}, u32[]{:S(2)}) collective-permute-start(bf16[512,512]{1,0:T(8,128)(2,1)} %param.10), channel_id=1, source_target_pairs={{0,2},{1,3},{2,0},{3,1},{4,6},{5,7},{6,4},{7,5},{8,10},{9,11},{10,... | collective-permute-start | bytes 1572872 | tf_op jit(solution)/shard_map/tokens_gather/ppermute | solution.py:381
  4.4 14.4 %all-to-all-start = ((bf16[8,64,256]{2,1,0:T(8,128)(2,1)}), bf16[8,64,256]{2,1,0:T(8,128)(2,1)S(1)}, u32[]{:S(2)}, u32[]{:S(2)}) async-start(bf16[8,64,256]{2,1,0:T(8,128)(2,1)} %param.19), calls=%async_computation | async-start | bytes 524288 | tf_op jit(solution)/shard_map/cache_gather/all_to_all | solution.py:384
  10.2 10.0 %collective-permute-start.1 = (bf16[512,512]{1,0:T(8,128)(2,1)}, bf16[512,512]{1,0:T(8,128)(2,1)S(1)}, u32[]{:S(2)}, u32[]{:S(2)}) collective-permute-start(bf16[512,512]{1,0:T(8,128)(2,1)} %param.10), channel_id=1, source_target_pairs={{0,1},{1,0},{2,3},{3,2},{4,5},{5,4},{6,7},{7,6},{8,9},{9,8},{10,11... | collective-permute-start | bytes 1572872 | tf_op jit(solution)/shard_map/tokens_gather/ppermute | solution.py:381
  18.8 1.9 %collective-permute-start.2 = (bf16[512,512]{1,0:T(8,128)(2,1)S(1)}, bf16[512,512]{1,0:T(8,128)(2,1)S(1)}, u32[]{:S(2)}, u32[]{:S(2)}) collective-permute-start(bf16[512,512]{1,0:T(8,128)(2,1)S(1)} %collective-permute-done.x2), channel_id=1, source_target_pairs={{0,1},{1,0},{2,3},{3,2},{4,5},{5,4},{6,7},{7,6},{8,9},{9,8},{10,11... | collective-permute-start | bytes 1572872 | tf_op jit(solution)/shard_map/project/ppermute | solution.py:381
  19.4 7.4 %collective-permute-start.4 = (bf16[384,256]{1,0:T(8,128)(2,1)S(1)}, bf16[384,256]{1,0:T(8,128)(2,1)S(1)}, u32[]{:S(2)}, u32[]{:S(2)}) collective-permute-start(bf16[384,256]{1,0:T(8,128)(2,1)S(1)} %order.1.refs_1_), channel_id=1, source_target_pairs={{0,2},{1,3},{2,0},{3,1},{4,6},{5,7},{6,4},{7,5},{8,10},{9,11},{10,... | collective-permute-start | bytes 589832 | tf_op jit(solution)/shard_map/cache_gather/ppermute | solution.py:381
  19.9 8.3 %collective-permute-start.3 = (bf16[384,256]{1,0:T(8,128)(2,1)S(1)}, bf16[384,256]{1,0:T(8,128)(2,1)S(1)}, u32[]{:S(2)}, u32[]{:S(2)}) collective-permute-start(bf16[384,256]{1,0:T(8,128)(2,1)S(1)} %order.1.refs_1_), channel_id=1, source_target_pairs={{0,1},{1,0},{2,3},{3,2},{4,5},{5,4},{6,7},{7,6},{8,9},{9,8},{10,11... | collective-permute-start | bytes 589832 | tf_op jit(solution)/shard_map/cache_gather/ppermute | solution.py:381
  26.8 1.5 %collective-permute-start.5 = (bf16[384,256]{1,0:T(8,128)(2,1)S(1)}, bf16[384,256]{1,0:T(8,128)(2,1)S(1)}, u32[]{:S(2)}, u32[]{:S(2)}) collective-permute-start(bf16[384,256]{1,0:T(8,128)(2,1)S(1)} %collective-permute-done.4.refs_3_), channel_id=1, source_target_pairs={{0,1},{1,0},{2,3},{3,2},{4,5},{5,4},{6,7},{7,6},{8,9},{9,8},{10,11... | collective-permute-start | bytes 589832 | tf_op jit(solution)/shard_map/extend/ppermute | solution.py:381
  26.8 6.6 %collective-permute-start.6 = (bf16[4,64,256]{2,1,0:T(8,128)(2,1)S(1)}, bf16[4,64,256]{2,1,0:T(8,128)(2,1)S(1)}, u32[]{:S(2)}, u32[]{:S(2)}) collective-permute-start(bf16[4,64,256]{2,1,0:T(8,128)(2,1)S(1)} %get-tuple-element.63), channel_id=1, source_target_pairs={{0,4},{4,0},{8,12},{12,8},{16,20},{20,16},{24,28},{28,24},{1,5},{5... | collective-permute-start | bytes 393224 | tf_op jit(solution)/shard_map/extend/ppermute | solution.py:381
  33.3 1.6 %collective-permute-start.7 = (bf16[256,512]{1,0:T(8,128)(2,1)S(1)}, bf16[256,512]{1,0:T(8,128)(2,1)S(1)}, u32[]{:S(2)}, u32[]{:S(2)}) collective-permute-start(bf16[256,512]{1,0:T(8,128)(2,1)S(1)} %get-tuple-element.64), channel_id=1, source_target_pairs={{0,1},{1,0},{2,3},{3,2},{4,5},{5,4},{6,7},{7,6},{8,9},{9,8},{10,11... | collective-permute-start | bytes 786440 | tf_op jit(solution)/shard_map/reduce/ppermute | solution.py:381
  35.0 8.5 %collective-permute-start.9 = (bf16[256,512]{1,0:T(8,128)(2,1)S(1)}, bf16[256,512]{1,0:T(8,128)(2,1)S(1)}, u32[]{:S(2)}, u32[]{:S(2)}) collective-permute-start(bf16[256,512]{1,0:T(8,128)(2,1)S(1)} %add_convert_fusion.1), channel_id=1, source_target_pairs={{0,2},{1,3},{2,0},{3,1},{4,6},{5,7},{6,4},{7,5},{8,10},{9,11},{10,... | collective-permute-start | bytes 786440 | tf_op jit(solution)/shard_map/reduce/ppermute | solution.py:381
  41.2 2.3 %collective-permute-start.10 = (bf16[256,512]{1,0:T(8,128)(2,1)S(1)}, bf16[256,512]{1,0:T(8,128)(2,1)S(1)}, u32[]{:S(2)}, u32[]{:S(2)}) collective-permute-start(bf16[256,512]{1,0:T(8,128)(2,1)S(1)} %get-tuple-element.73), channel_id=1, source_target_pairs={{0,1},{1,0},{2,3},{3,2},{4,5},{5,4},{6,7},{7,6},{8,9},{9,8},{10,11... | collective-permute-start | bytes 786440 | tf_op jit(solution)/shard_map/reduce/ppermute | solution.py:381
  41.3 14.3 %collective-permute-start.8 = (bf16[512,512]{1,0:T(8,128)(2,1)S(1)}, bf16[512,512]{1,0:T(8,128)(2,1)S(1)}, u32[]{:S(2)}, u32[]{:S(2)}) collective-permute-start(bf16[512,512]{1,0:T(8,128)(2,1)S(1)} %get-tuple-element.70), channel_id=1, source_target_pairs={{0,1},{1,0},{2,3},{3,2},{4,5},{5,4},{6,7},{7,6},{8,9},{9,8},{10,11... | collective-permute-start | bytes 1572872 | tf_op jit(solution)/shard_map/finish/ppermute | solution.py:381
  43.6 17.4 %collective-permute-start.11 = (bf16[256,512]{1,0:T(8,128)(2,1)S(1)}, bf16[256,512]{1,0:T(8,128)(2,1)S(1)}, u32[]{:S(2)}, u32[]{:S(2)}) collective-permute-start(bf16[256,512]{1,0:T(8,128)(2,1)S(1)} %add_convert_fusion), channel_id=1, source_target_pairs={{0,2},{1,3},{2,0},{3,1},{4,6},{5,7},{6,4},{7,5},{8,10},{9,11},{10,... | collective-permute-start | bytes 786440 | tf_op jit(solution)/shard_map/reduce/ppermute | solution.py:381
  44.4 12.5 %collective-permute-start.12 = (bf16[2,64,256]{2,1,0:T(8,128)(2,1)S(1)}, bf16[2,64,256]{2,1,0:T(8,128)(2,1)S(1)}, u32[]{:S(2)}, u32[]{:S(2)}) collective-permute-start(bf16[2,64,256]{2,1,0:T(8,128)(2,1)S(1)} %get-tuple-element.80), channel_id=1, source_target_pairs={{0,8},{4,12},{8,0},{12,4},{16,24},{20,28},{24,16},{28,20},{1,9},{5... | collective-permute-start | bytes 196616 | tf_op jit(solution)/shard_map/exchange/ppermute | solution.py:381
  53.1 7.8 %collective-permute-start.13 = (bf16[2,64,256]{2,1,0:T(8,128)(2,1)S(1)}, bf16[2,64,256]{2,1,0:T(8,128)(2,1)S(1)}, u32[]{:S(2)}, u32[]{:S(2)}) collective-permute-start(bf16[2,64,256]{2,1,0:T(8,128)(2,1)S(1)} %get-tuple-element.81), channel_id=1, source_target_pairs={{0,16},{4,20},{8,24},{12,28},{16,0},{20,4},{24,8},{28,12},{1,17},{... | collective-permute-start | bytes 196616 | tf_op jit(solution)/shard_map/exchange/ppermute | solution.py:381
  53.2 7.8 %collective-permute-start.14 = (bf16[2,64,256]{2,1,0:T(8,128)(2,1)S(1)}, bf16[2,64,256]{2,1,0:T(8,128)(2,1)S(1)}, u32[]{:S(2)}, u32[]{:S(2)}) collective-permute-start(bf16[2,64,256]{2,1,0:T(8,128)(2,1)S(1)} %get-tuple-element.82), channel_id=1, source_target_pairs={{0,24},{4,28},{8,16},{12,20},{16,8},{20,12},{24,0},{28,4},{1,25},{... | collective-permute-start | bytes 196616 | tf_op jit(solution)/shard_map/exchange/ppermute | solution.py:381
where the time goes:
time: 62.8 us; the launch traced here: 62.6 us
  starting transfers between devices  24.6 us (39%)
  Pallas kernels  19.3 us (31%)
  waiting for transfers between devices  13.8 us (22%)
  other arithmetic  2.67 us (4%)
  between operations  2.19 us (3%)
    pallas_call x8, Pallas kernels, call(): pl.pallas_call(kernel, out_shape=out_shape, in_specs=in_specs, out_specs=...  19.3 us
    ppermute x15, starting transfers between devices, swap(): return lax.ppermute(x, axis, [(i, i ^ bit) for i in range(size)])  18.8 us
    ppermute x15, waiting for transfers between devices, swap(): return lax.ppermute(x, axis, [(i, i ^ bit) for i in range(size)])  11.6 us
    all_to_all x1, starting transfers between devices, exchange(): return lax.all_to_all(x, 'seq', split_axis=0, concat_axis=0, tiled=True)  5.81 us
    all_to_all x1, waiting for transfers between devices, exchange(): return lax.all_to_all(x, 'seq', split_axis=0, concat_axis=0, tiled=True)  2.26 us
  transfers between devices with their start and end apart: 16, of which 7 were waited for; matrix products, arithmetic and copies ran while one was open for 4% of the time, Pallas kernels for 29%

commit v1 on v0

--- a/solution.py
+++ b/solution.py
@@ -40,6 +40,18 @@
     for k, pair_ref in enumerate(pair_refs):
         pair_ref[0] = keep_ref[k]
         pair_ref[1] = got_ref[k]
+
+
+def place_kernel(p0, p1, p2, p3, out_hbm, sems):
+    me = lax.axis_index("seq")
+    stores = []
+    for k, pair_ref in enumerate((p0, p1, p2, p3)):
+        for j in range(2):
+            slot = out_hbm.at[me ^ (2 * k + j)]
+            stores.append(pltpu.make_async_copy(pair_ref.at[j], slot, sems.at[len(stores)]))
+            stores[-1].start()
+    for store in stores:
+        store.wait()
 
 
 def order_kernel(share, plan_ref, arrived_ref, out_ref):
@@ -309,19 +321,11 @@
     pass
 
 
-def finish_kernel(at, phased, plan_ref, tokens_ref, near_ref, got_ref, crossed_ref, *refs):
-    out_hbm, done, sems = refs[0 if not at else -3 - phased], refs[-2], refs[-1]
+def finish_kernel(at, plan_ref, tokens_ref, near_ref, got_ref, crossed_ref, *refs):
+    out_hbm, done, sems = refs[-3:]
     rows = crossed_ref.shape[0]
     half = rows // 2
     stores = []
-    if at and phased:
-        me = lax.axis_index("seq")
-        for k, pair_ref in enumerate(refs[:4]):
-            for j in range(2):
-                sem = sems.at[2 + len(stores)]
-                slot = refs[-3].at[me ^ (2 * k + j)]
-                stores.append(pltpu.make_async_copy(pair_ref.at[j], slot, sem))
-                stores[-1].start()
     for i in range(2):
         here = pl.ds(i * half, half)
         there = pl.ds(at + i * half, half)
@@ -351,6 +355,19 @@
         compiler_params=pltpu.CompilerParams(vmem_limit_bytes=int(mib * 1024 * 1024)),
         name=name,
     )(*args)
+
+
+def hand_on(x):
+    return pl.pallas_call(
+        hand_on_kernel,
+        out_shape=jax.ShapeDtypeStruct(x.shape, x.dtype),
+        in_specs=[pl.BlockSpec(memory_space=pl.ANY)],
+        out_specs=pl.BlockSpec(memory_space=pl.ANY),
+        input_output_aliases={0: 0},
+        cost_estimate=pl.CostEstimate(flops=1 << 34, bytes_accessed=1024, transcendentals=0),
+        compiler_params=pltpu.CompilerParams(vmem_limit_bytes=1 << 20),
+        name="hand_on",
+    )(x)
 
 
 def body(
@@ -500,26 +517,15 @@
                 far1, near1, before_rows, *old = sums
                 old.append(before_rows)
         with jax.named_scope("reduce"):
-            if c == 0 and phased:
-                far1, got = lax.optimization_barrier((far1, got))
             got1 = swap(far1, 1)
             if c and last:
-                before = pl.pallas_call(
-                    hand_on_kernel,
-                    out_shape=jax.ShapeDtypeStruct(before.shape, BF16),
-                    in_specs=[pl.BlockSpec(memory_space=pl.ANY)],
-                    out_specs=pl.BlockSpec(memory_space=pl.ANY),
-                    input_output_aliases={0: 0},
-                    cost_estimate=pl.CostEstimate(
-                        flops=1 << 34, bytes_accessed=1024, transcendentals=0
-                    ),
-                    compiler_params=pltpu.CompilerParams(vmem_limit_bytes=1 << 20),
-                    name="hand_on",
-                )(before)
+                before = hand_on(before)
                 before, got1 = lax.optimization_barrier((before, got1))
             pair = (near1.astype(F32) + got1.astype(F32)).astype(BF16)
             if not last:
                 query, pair = lax.optimization_barrier((query, pair))
+                if phased:
+                    old[0], got = lax.optimization_barrier((old[0], got))
             if last and phased:
                 pair, got = lax.optimization_barrier((pair, got))
             crossed = swap(pair, 2)
@@ -540,35 +546,36 @@
             for k in range(len(pairs) - 1, 0, -1):
                 pairs[k] = swap(pairs[k], 2 * k, "seq")
         else:
-            pairs = []
             new_cache = exchange(sent[0].reshape(groups, share, width))
 
     with jax.named_scope("finish"):
         got0 = swap(far0, 1)
-        ends = (plan, own, near0, got0)
-        out = jax.ShapeDtypeStruct((rows, cols), BF16)
-        scratch = [pltpu.VMEM((part, cols), BF16)]
-        mixed = call(
-            functools.partial(finish_kernel, 0, phased),
-            out,
-            [SMEM] + [VMEM] * 4,
-            (*ends, before),
-            flops=4 * part * cols,
-            scratch=scratch + [pltpu.SemaphoreType.DMA((2,))],
-            name="finish",
-            into={},
-        )
-        finished = call(
-            functools.partial(finish_kernel, part, phased),
-            [out, jax.ShapeDtypeStruct(old_cache.shape, BF16)] if phased else out,
-            [SMEM] + [VMEM] * (4 + len(pairs)) + [HBM],
-            (*ends, crossed, *pairs, mixed),
-            flops=4 * part * cols,
-            scratch=scratch + [pltpu.SemaphoreType.DMA((2 + groups * phased,))],
-            name="finish",
-            into={5 + len(pairs): 0},
-        )
-    return tuple(finished) if phased else (finished, new_cache)
+        mixed = None
+        for at, over in ((0, before), (part, crossed)):
+            mixed = call(
+                functools.partial(finish_kernel, at),
+                jax.ShapeDtypeStruct((rows, cols), BF16),
+                [SMEM] + [VMEM] * 4 + [HBM] * (at > 0),
+                (plan, own, near0, got0, over, *([mixed] if at else [])),
+                flops=4 * part * cols,
+                scratch=[pltpu.VMEM((part, cols), BF16), pltpu.SemaphoreType.DMA((2,))],
+                name="finish",
+                into={5: 0} if at else {},
+            )
+        if phased:
+            mixed, *pairs = lax.optimization_barrier((mixed, *pairs))
+            new_cache = call(
+                place_kernel,
+                jax.ShapeDtypeStruct(old_cache.shape, BF16),
+                [VMEM] * len(pairs),
+                pairs,
+                flops=0,
+                mib=8,
+                scratch=[pltpu.SemaphoreType.DMA((groups,))],
+                name="place",
+                into={},
+            )
+    return (mixed, new_cache)
 
 
 def solution(mesh):

time: 62.8 us -> 63.1 us (level)
  the two profiles are of different devices: /device:TPU:0 before, /device:TPU:2 now
where the time goes in v1:
time: 63.1 us; the launch traced here: 63.3 us
  Pallas kernels  21.4 us (34%)
  starting transfers between devices  19.9 us (32%)
  waiting for transfers between devices  17.1 us (27%)
  other arithmetic  2.67 us (4%)
  between operations  2.2 us (3%)
    pallas_call x9, Pallas kernels, call(): pl.pallas_call(kernel, out_shape=out_shape, in_specs=in_specs, out_specs=...  21.4 us
    ppermute x15, waiting for transfers between devices, swap(): return lax.ppermute(x, axis, [(i, i ^ bit) for i in range(size)])  15.1 us
    ppermute x15, starting transfers between devices, swap(): return lax.ppermute(x, axis, [(i, i ^ bit) for i in range(size)])  13.6 us
    all_to_all x1, starting transfers between devices, exchange(): return lax.all_to_all(x, 'seq', split_axis=0, concat_axis=0, tiled=True)  6.34 us
    all_to_all x1, waiting for transfers between devices, exchange(): return lax.all_to_all(x, 'seq', split_axis=0, concat_axis=0, tiled=True)  2 us
  transfers between devices with their start and end apart: 16, of which 11 were waited for; matrix products, arithmetic and copies ran while one was open for 4% of the time, Pallas kernels for 19%

profile of v1, /device:TPU:2, one launch (start us, length us, event | category | flops | bytes accessed | tf_op | source)
XLA Modules:
  0.0 63.3 jit_solution(13501752846854628920)
XLA Ops:
  0.6 1.6 %collective-permute-start = (bf16[512,512]{1,0:T(8,128)(2,1)}, bf16[512,512]{1,0:T(8,128)(2,1)S(1)}, u32[]{:S(2)}, u32[]{:S(2)}) collective-permute-start(bf16[512,512]{1,0:T(8,128)(2,1)} %param.10), channel_id=1, source_target_pairs={{0,2},{1,3},{2,0},{3,1},{4,6},{5,7},{6,4},{7,5},{8,10},{9,11},{10,... | collective-permute-start | bytes 1572872 | tf_op jit(solution)/shard_map/tokens_gather/ppermute | solution.py:398
  2.2 0.7 %broadcast_maximum_fusion.1 = f32[2048]{0:T(1024)S(1)} fusion(f32[2048]{0:T(1024)} %param.11), kind=kLoop, calls=%fused_computation.3 | loop fusion | flops 2048 | bytes 16384 | tf_op jit(solution)/shard_map/cache_gather/max | solution.py:410
  2.9 6.3 %all-to-all-start = ((bf16[8,64,256]{2,1,0:T(8,128)(2,1)}), bf16[8,64,256]{2,1,0:T(8,128)(2,1)S(1)}, u32[]{:S(2)}, u32[]{:S(2)}) async-start(bf16[8,64,256]{2,1,0:T(8,128)(2,1)} %param.19), calls=%async_computation | async-start | bytes 524288 | tf_op jit(solution)/shard_map/cache_gather/all_to_all | solution.py:401
  10.6 1.1 %broadcast_maximum_fusion.x0.tokens_ref = bf16[512,512]{1,0:T(8,128)(2,1)S(1)} fusion(bf16[512,512]{1,0:T(8,128)(2,1)} %param.10), kind=kLoop, calls=%fused_computation.2 | loop fusion | flops 262144 | bytes 1048576 | tf_op jit(solution)/shard_map/cache_gather/max | solution.py:413
  11.6 2.9 %collective-permute-done.x2 = bf16[512,512]{1,0:T(8,128)(2,1)S(1)} collective-permute-done((bf16[512,512]{1,0:T(8,128)(2,1)}, bf16[512,512]{1,0:T(8,128)(2,1)S(1)}, u32[]{:S(2)}, u32[]{:S(2)}) %collective-permute-start) | collective-permute-done | bytes 524320 | tf_op jit(solution)/shard_map/tokens_gather/ppermute | solution.py:398
  14.6 0.7 %pad_add_fusion.plan_ref = s32[18]{0:T(128)S(1)} fusion(s32[8]{0:T(128)} %bitcast.7, s32[8]{0:T(128)} %bitcast.8, s32[1]{0:T(128)S(6)} %copy.16, s32[1]{0:T(128)S(6)} %copy.17), kind=kLoop, calls=%fused_computation.4 | loop fusion | flops 54 | bytes 144 | tf_op jit(solution)/shard_map/cache_gather/concatenate | solution.py:417
  15.3 2.0 %all-to-all-done = bf16[8,64,256]{2,1,0:T(8,128)(2,1)S(1)} async-done(((bf16[8,64,256]{2,1,0:T(8,128)(2,1)}), bf16[8,64,256]{2,1,0:T(8,128)(2,1)S(1)}, u32[]{:S(2)}, u32[]{:S(2)}) %all-to-all-start) | async-done | bytes 262176 | tf_op jit(solution)/shard_map/cache_gather/all_to_all | solution.py:401
  17.9 0.6 collective-permute-start.4
  19.2 4.1 %project.1 = (bf16[2048,128]{1,0:T(8,128)(2,1)S(1)}, bf16[512,256]{1,0:T(8,128)(2,1)S(1)}, bf16[512,256]{1,0:T(8,128)(2,1)S(1)}, f32[2,8,128]{2,1,0:T(8,128)S(1)}) custom-call(bf16[512,512]{1,0:T(8,128)(2,1)S(1)} %broadcast_maximum_fusion.x0.tokens_ref, bf16[512,512]{1,0:T(8,128)(2,1)S(1)} %collective-permute-done.1.x1, ...), custom_call_target="tpu_custom_call" | custom-call | flops 1610612736 | bytes 6307840 | tf_op jit(solution)/shard_map/project/project/pallas_call | solution.py:347
  23.3 1.2 %extend.1 = (bf16[4,64,256]{2,1,0:T(8,128)(2,1)S(1)}, bf16[4,64,256]{2,1,0:T(8,128)(2,1)S(1)}) custom-call(s32[18]{0:T(128)S(1)} %pad_add_fusion.plan_ref, bf16[512,256]{1,0:T(8,128)(2,1)S(1)} %get-tuple-element.59.kv_ref, bf16[512,256]{1,0:T(8,128)(2,1)S(1)} %bitcast.5), custom_call_target="tpu_custom_call" | custom-call | flops 268435456 | bytes 786504 | tf_op jit(solution)/shard_map/extend/extend/pallas_call | solution.py:347
  24.5 0.7 %collective-permute-done.4.refs_3_ = bf16[384,256]{1,0:T(8,128)(2,1)S(1)} collective-permute-done((bf16[384,256]{1,0:T(8,128)(2,1)S(1)}, bf16[384,256]{1,0:T(8,128)(2,1)S(1)}, u32[]{:S(2)}, u32[]{:S(2)}) %collective-permute-start.4) | collective-permute-done | bytes 196640 | tf_op jit(solution)/shard_map/cache_gather/ppermute | solution.py:398
  25.3 1.4 %collective-permute-done.5.refs_4_ = bf16[384,256]{1,0:T(8,128)(2,1)S(1)} collective-permute-done((bf16[384,256]{1,0:T(8,128)(2,1)S(1)}, bf16[384,256]{1,0:T(8,128)(2,1)S(1)}, u32[]{:S(2)}, u32[]{:S(2)}) %collective-permute-start.5) | collective-permute-done | bytes 196640 | tf_op jit(solution)/shard_map/extend/ppermute | solution.py:398
  26.7 8.9 %attend.2 = (bf16[256,512]{1,0:T(8,128)(2,1)S(1)}, bf16[256,512]{1,0:T(8,128)(2,1)S(1)}, bf16[256,512]{1,0:T(8,128)(2,1)S(1)}, bf16[1536,256]{1,0:T(8,128)(2,1)S(1)}, f32[8,128]{1,0:T(8,128)S(1)}) custom-call(s32[18]{0:T(128)S(1)} %pad_add_fusion.plan_ref, bf16[2048,128]{1,0:T(8,128)(2,1)S(1)} %get-tuple-element.68.q_ref, ...), custom_call_target="tpu_custom_call" | custom-call | flops 1476395008 | bytes 5517384 | tf_op jit(solution)/shard_map/attend/attend/pallas_call | solution.py:347
  35.8 1.4 %collective-permute-done.6 = bf16[256,512]{1,0:T(8,128)(2,1)S(1)} collective-permute-done((bf16[256,512]{1,0:T(8,128)(2,1)S(1)}, bf16[256,512]{1,0:T(8,128)(2,1)S(1)}, u32[]{:S(2)}, u32[]{:S(2)}) %collective-permute-start.6) | collective-permute-done | bytes 262176 | tf_op jit(solution)/shard_map/reduce/ppermute | solution.py:398
  37.8 3.7 %collective-permute-done.7.got_ref = bf16[4,64,256]{2,1,0:T(8,128)(2,1)S(1)} collective-permute-done((bf16[4,64,256]{2,1,0:T(8,128)(2,1)S(1)}, bf16[4,64,256]{2,1,0:T(8,128)(2,1)S(1)}, u32[]{:S(2)}, u32[]{:S(2)}) %collective-permute-start.7) | collective-permute-done | bytes 131104 | tf_op jit(solution)/shard_map/extend/ppermute | solution.py:398
  41.6 3.1 %attend.3 = (bf16[512,512]{1,0:T(8,128)(2,1)S(1)}, bf16[256,512]{1,0:T(8,128)(2,1)S(1)}, bf16[512,512]{1,0:T(8,128)(2,1)S(1)}, bf16[256,512]{1,0:T(8,128)(2,1)S(1)}) custom-call(s32[18]{0:T(128)S(1)} %pad_add_fusion.plan_ref, bf16[2048,128]{1,0:T(8,128)(2,1)S(1)} %get-tuple-element.68.q_ref, bf16[512,256]{1,0:T(8,128)(2,1)S(1)} %get-tuple-element.59.kv_ref, ...), custom_call_target="tpu_custom_call" | custom-call | flops 1610612736 | bytes 6565960 | tf_op jit(solution)/shard_map/attend/attend/pallas_call | solution.py:347
  45.7 0.6 collective-permute-done.10
  46.9 3.0 %collective-permute-start.12 = (bf16[2,64,256]{2,1,0:T(8,128)(2,1)S(1)}, bf16[2,64,256]{2,1,0:T(8,128)(2,1)S(1)}, u32[]{:S(2)}, u32[]{:S(2)}) collective-permute-start(bf16[2,64,256]{2,1,0:T(8,128)(2,1)S(1)} %get-tuple-element.86), channel_id=1, source_target_pairs={{0,8},{4,12},{8,0},{12,4},{16,24},{20,28},{24,16},{28,20},{1,9},{5... | collective-permute-start | bytes 196616 | tf_op jit(solution)/shard_map/exchange/ppermute | solution.py:398
  49.9 6.3 %collective-permute-start.13 = (bf16[2,64,256]{2,1,0:T(8,128)(2,1)S(1)}, bf16[2,64,256]{2,1,0:T(8,128)(2,1)S(1)}, u32[]{:S(2)}, u32[]{:S(2)}) collective-permute-start(bf16[2,64,256]{2,1,0:T(8,128)(2,1)S(1)} %get-tuple-element.87), channel_id=1, source_target_pairs={{0,16},{4,20},{8,24},{12,28},{16,0},{20,4},{24,8},{28,12},{1,17},{... | collective-permute-start | bytes 196616 | tf_op jit(solution)/shard_map/exchange/ppermute | solution.py:398
  56.3 1.4 %finish.2.refs_0_ = bf16[512,512]{1,0:T(8,128)(2,1)} custom-call(s32[18]{0:T(128)S(1)} %pad_add_fusion.plan_ref, bf16[512,512]{1,0:T(8,128)(2,1)S(1)} %broadcast_maximum_fusion.x0.tokens_ref, bf16[512,512]{1,0:T(8,128)(2,1)S(1)} %get-tuple-element.74.near_ref, bf16[512,512]{1,0:T(8,128)(2,1)S(1)} %collective-permute-done.8.got_ref, ...), custom_call_target="tpu_custom_call" | custom-call | flops 524288 | bytes 2359368 | tf_op jit(solution)/shard_map/finish/finish/pallas_call | solution.py:347
  57.7 1.4 %finish.3 = bf16[512,512]{1,0:T(8,128)(2,1)} custom-call(s32[18]{0:T(128)S(1)} %pad_add_fusion.plan_ref, bf16[512,512]{1,0:T(8,128)(2,1)S(1)} %broadcast_maximum_fusion.x0.tokens_ref, bf16[512,512]{1,0:T(8,128)(2,1)S(1)} %get-tuple-element.74.near_ref, bf16[512,512]{1,0:T(8,128)(2,1)S(1)} %collective-permute-done.8.got_ref, ...), custom_call_target="tpu_custom_call", output_to_operand_aliasing={{}: (5, {})} | custom-call | flops 524288 | bytes 2883656 | tf_op jit(solution)/shard_map/finish/finish/pallas_call | solution.py:347
  59.1 1.8 %collective-permute-done.13.p2 = bf16[2,64,256]{2,1,0:T(8,128)(2,1)S(1)} collective-permute-done((bf16[2,64,256]{2,1,0:T(8,128)(2,1)S(1)}, bf16[2,64,256]{2,1,0:T(8,128)(2,1)S(1)}, u32[]{:S(2)}, u32[]{:S(2)}) %collective-permute-start.13) | collective-permute-done | bytes 65568 | tf_op jit(solution)/shard_map/exchange/ppermute | solution.py:398
  60.9 1.5 %collective-permute-done.14.p3 = bf16[2,64,256]{2,1,0:T(8,128)(2,1)S(1)} collective-permute-done((bf16[2,64,256]{2,1,0:T(8,128)(2,1)S(1)}, bf16[2,64,256]{2,1,0:T(8,128)(2,1)S(1)}, u32[]{:S(2)}, u32[]{:S(2)}) %collective-permute-start.14) | collective-permute-done | bytes 65568 | tf_op jit(solution)/shard_map/exchange/ppermute | solution.py:398
  62.3 0.8 %place.1 = bf16[8,64,256]{2,1,0:T(8,128)(2,1)} custom-call(bf16[2,64,256]{2,1,0:T(8,128)(2,1)S(1)} %get-tuple-element.90.p0, bf16[2,64,256]{2,1,0:T(8,128)(2,1)S(1)} %collective-permute-done.12.p1, bf16[2,64,256]{2,1,0:T(8,128)(2,1)S(1)} %collective-permute-done.13.p2, bf16[2,64,256]{2,1,0:T(8,128)(2,1)S(1)} %collective-permute-done.14.p3), custom_call_target="tpu_custom_call" | custom-call | bytes 524288 | tf_op jit(solution)/shard_map/finish/place/pallas_call | solution.py:347
  (23 shorter events, 3.8 us)
Async XLA Ops:
  0.6 13.9 %collective-permute-start = (bf16[512,512]{1,0:T(8,128)(2,1)}, bf16[512,512]{1,0:T(8,128)(2,1)S(1)}, u32[]{:S(2)}, u32[]{:S(2)}) collective-permute-start(bf16[512,512]{1,0:T(8,128)(2,1)} %param.10), channel_id=1, source_target_pairs={{0,2},{1,3},{2,0},{3,1},{4,6},{5,7},{6,4},{7,5},{8,10},{9,11},{10,... | collective-permute-start | bytes 1572872 | tf_op jit(solution)/shard_map/tokens_gather/ppermute | solution.py:398
  2.9 14.4 %all-to-all-start = ((bf16[8,64,256]{2,1,0:T(8,128)(2,1)}), bf16[8,64,256]{2,1,0:T(8,128)(2,1)S(1)}, u32[]{:S(2)}, u32[]{:S(2)}) async-start(bf16[8,64,256]{2,1,0:T(8,128)(2,1)} %param.19), calls=%async_computation | async-start | bytes 524288 | tf_op jit(solution)/shard_map/cache_gather/all_to_all | solution.py:401
  9.2 9.4 %collective-permute-start.1 = (bf16[512,512]{1,0:T(8,128)(2,1)}, bf16[512,512]{1,0:T(8,128)(2,1)S(1)}, u32[]{:S(2)}, u32[]{:S(2)}) collective-permute-start(bf16[512,512]{1,0:T(8,128)(2,1)} %param.10), channel_id=1, source_target_pairs={{0,1},{1,0},{2,3},{3,2},{4,5},{5,4},{6,7},{7,6},{8,9},{9,8},{10,11... | collective-permute-start | bytes 1572872 | tf_op jit(solution)/shard_map/tokens_gather/ppermute | solution.py:398
  17.3 1.9 %collective-permute-start.2 = (bf16[512,512]{1,0:T(8,128)(2,1)S(1)}, bf16[512,512]{1,0:T(8,128)(2,1)S(1)}, u32[]{:S(2)}, u32[]{:S(2)}) collective-permute-start(bf16[512,512]{1,0:T(8,128)(2,1)S(1)} %collective-permute-done.x2), channel_id=1, source_target_pairs={{0,1},{1,0},{2,3},{3,2},{4,5},{5,4},{6,7},{7,6},{8,9},{9,8},{10,11... | collective-permute-start | bytes 1572872 | tf_op jit(solution)/shard_map/project/ppermute | solution.py:398
  17.9 7.4 %collective-permute-start.4 = (bf16[384,256]{1,0:T(8,128)(2,1)S(1)}, bf16[384,256]{1,0:T(8,128)(2,1)S(1)}, u32[]{:S(2)}, u32[]{:S(2)}) collective-permute-start(bf16[384,256]{1,0:T(8,128)(2,1)S(1)} %order.1.refs_1_), channel_id=1, source_target_pairs={{0,2},{1,3},{2,0},{3,1},{4,6},{5,7},{6,4},{7,5},{8,10},{9,11},{10,... | collective-permute-start | bytes 589832 | tf_op jit(solution)/shard_map/cache_gather/ppermute | solution.py:398
  18.5 6.8 %collective-permute-start.3 = (bf16[384,256]{1,0:T(8,128)(2,1)S(1)}, bf16[384,256]{1,0:T(8,128)(2,1)S(1)}, u32[]{:S(2)}, u32[]{:S(2)}) collective-permute-start(bf16[384,256]{1,0:T(8,128)(2,1)S(1)} %order.1.refs_1_), channel_id=1, source_target_pairs={{0,1},{1,0},{2,3},{3,2},{4,5},{5,4},{6,7},{7,6},{8,9},{9,8},{10,11... | collective-permute-start | bytes 589832 | tf_op jit(solution)/shard_map/cache_gather/ppermute | solution.py:398
  25.3 1.4 %collective-permute-start.5 = (bf16[384,256]{1,0:T(8,128)(2,1)S(1)}, bf16[384,256]{1,0:T(8,128)(2,1)S(1)}, u32[]{:S(2)}, u32[]{:S(2)}) collective-permute-start(bf16[384,256]{1,0:T(8,128)(2,1)S(1)} %collective-permute-done.4.refs_3_), channel_id=1, source_target_pairs={{0,1},{1,0},{2,3},{3,2},{4,5},{5,4},{6,7},{7,6},{8,9},{9,8},{10,11... | collective-permute-start | bytes 589832 | tf_op jit(solution)/shard_map/extend/ppermute | solution.py:398
  35.6 1.6 %collective-permute-start.6 = (bf16[256,512]{1,0:T(8,128)(2,1)S(1)}, bf16[256,512]{1,0:T(8,128)(2,1)S(1)}, u32[]{:S(2)}, u32[]{:S(2)}) collective-permute-start(bf16[256,512]{1,0:T(8,128)(2,1)S(1)} %get-tuple-element.67), channel_id=1, source_target_pairs={{0,1},{1,0},{2,3},{3,2},{4,5},{5,4},{6,7},{7,6},{8,9},{9,8},{10,11... | collective-permute-start | bytes 786440 | tf_op jit(solution)/shard_map/reduce/ppermute | solution.py:398
  35.8 5.8 %collective-permute-start.7 = (bf16[4,64,256]{2,1,0:T(8,128)(2,1)S(1)}, bf16[4,64,256]{2,1,0:T(8,128)(2,1)S(1)}, u32[]{:S(2)}, u32[]{:S(2)}) collective-permute-start(bf16[4,64,256]{2,1,0:T(8,128)(2,1)S(1)} %get-tuple-element.70), channel_id=1, source_target_pairs={{0,4},{4,0},{8,12},{12,8},{16,20},{20,16},{24,28},{28,24},{1,5},{5... | collective-permute-start | bytes 393224 | tf_op jit(solution)/shard_map/extend/ppermute | solution.py:398
  37.2 8.4 %collective-permute-start.9 = (bf16[256,512]{1,0:T(8,128)(2,1)S(1)}, bf16[256,512]{1,0:T(8,128)(2,1)S(1)}, u32[]{:S(2)}, u32[]{:S(2)}) collective-permute-start(bf16[256,512]{1,0:T(8,128)(2,1)S(1)} %add_convert_fusion.1), channel_id=1, source_target_pairs={{0,2},{1,3},{2,0},{3,1},{4,6},{5,7},{6,4},{7,5},{8,10},{9,11},{10,... | collective-permute-start | bytes 786440 | tf_op jit(solution)/shard_map/reduce/ppermute | solution.py:398
  44.7 1.6 %collective-permute-start.10 = (bf16[256,512]{1,0:T(8,128)(2,1)S(1)}, bf16[256,512]{1,0:T(8,128)(2,1)S(1)}, u32[]{:S(2)}, u32[]{:S(2)}) collective-permute-start(bf16[256,512]{1,0:T(8,128)(2,1)S(1)} %get-tuple-element.78), channel_id=1, source_target_pairs={{0,1},{1,0},{2,3},{3,2},{4,5},{5,4},{6,7},{7,6},{8,9},{9,8},{10,11... | collective-permute-start | bytes 786440 | tf_op jit(solution)/shard_map/reduce/ppermute | solution.py:398
  44.8 11.5 %collective-permute-start.8 = (bf16[512,512]{1,0:T(8,128)(2,1)S(1)}, bf16[512,512]{1,0:T(8,128)(2,1)S(1)}, u32[]{:S(2)}, u32[]{:S(2)}) collective-permute-start(bf16[512,512]{1,0:T(8,128)(2,1)S(1)} %get-tuple-element.75), channel_id=1, source_target_pairs={{0,1},{1,0},{2,3},{3,2},{4,5},{5,4},{6,7},{7,6},{8,9},{9,8},{10,11... | collective-permute-start | bytes 1572872 | tf_op jit(solution)/shard_map/finish/ppermute | solution.py:398
  46.4 11.3 %collective-permute-start.11 = (bf16[256,512]{1,0:T(8,128)(2,1)S(1)}, bf16[256,512]{1,0:T(8,128)(2,1)S(1)}, u32[]{:S(2)}, u32[]{:S(2)}) collective-permute-start(bf16[256,512]{1,0:T(8,128)(2,1)S(1)} %add_convert_fusion), channel_id=1, source_target_pairs={{0,2},{1,3},{2,0},{3,1},{4,6},{5,7},{6,4},{7,5},{8,10},{9,11},{10,... | collective-permute-start | bytes 786440 | tf_op jit(solution)/shard_map/reduce/ppermute | solution.py:398
  46.9 12.1 %collective-permute-start.12 = (bf16[2,64,256]{2,1,0:T(8,128)(2,1)S(1)}, bf16[2,64,256]{2,1,0:T(8,128)(2,1)S(1)}, u32[]{:S(2)}, u32[]{:S(2)}) collective-permute-start(bf16[2,64,256]{2,1,0:T(8,128)(2,1)S(1)} %get-tuple-element.86), channel_id=1, source_target_pairs={{0,8},{4,12},{8,0},{12,4},{16,24},{20,28},{24,16},{28,20},{1,9},{5... | collective-permute-start | bytes 196616 | tf_op jit(solution)/shard_map/exchange/ppermute | solution.py:398
  49.9 10.9 %collective-permute-start.13 = (bf16[2,64,256]{2,1,0:T(8,128)(2,1)S(1)}, bf16[2,64,256]{2,1,0:T(8,128)(2,1)S(1)}, u32[]{:S(2)}, u32[]{:S(2)}) collective-permute-start(bf16[2,64,256]{2,1,0:T(8,128)(2,1)S(1)} %get-tuple-element.87), channel_id=1, source_target_pairs={{0,16},{4,20},{8,24},{12,28},{16,0},{20,4},{24,8},{28,12},{1,17},{... | collective-permute-start | bytes 196616 | tf_op jit(solution)/shard_map/exchange/ppermute | solution.py:398
  56.3 6.1 %collective-permute-start.14 = (bf16[2,64,256]{2,1,0:T(8,128)(2,1)S(1)}, bf16[2,64,256]{2,1,0:T(8,128)(2,1)S(1)}, u32[]{:S(2)}, u32[]{:S(2)}) collective-permute-start(bf16[2,64,256]{2,1,0:T(8,128)(2,1)S(1)} %get-tuple-element.88), channel_id=1, source_target_pairs={{0,24},{4,28},{8,16},{12,20},{16,8},{20,12},{24,0},{28,4},{1,25},{... | collective-permute-start | bytes 196616 | tf_op jit(solution)/shard_map/exchange/ppermute | solution.py:398

commit v2 on v1

--- a/solution.py
+++ b/solution.py
@@ -19,6 +19,7 @@
 PROJECT_MIB = 50.375
 LEAST = -3e38
 ATTEND_MIB = 49
+EARLY_MIB = 50
 SAFE = 60.0
 F32 = jnp.float32
 BF16 = jnp.bfloat16
@@ -164,13 +165,49 @@
     return jnp.max(squares.reshape(-1, 8, 128), axis=0)
 
 
+def lay_out(share, block_rows, held, owners, pieces, out_ref):
+    piece_rows, width = pieces[0].shape
+    hd = width // 2
+    group = KEY_TILE * lax.axis_size("tp")
+    tiles = (held + group - 1) // group
+    row = lax.broadcasted_iota(jnp.int32, (KEY_TILE, hd), 0)
+    place = row // share * block_rows + row % share
+
+    def lay(i, whole):
+        source = pl.ds(i * KEY_TILE, KEY_TILE)
+        for j, (owner, piece) in enumerate(zip(owners, pieces)):
+            at = pl.ds((i * len(pieces) + j) * KEY_TILE, KEY_TILE)
+            if whole:
+                out_ref[at, hd:] = piece[source, hd:]
+                out_ref[at, :hd] = jnp.ones((KEY_TILE, hd), BF16)
+                continue
+            used = place + owner * share + i * group < held
+            out_ref[at, hd:] = jnp.where(used, piece[source, hd:].astype(F32), 0.0).astype(BF16)
+            out_ref[at, :hd] = jnp.where(used, 1.0, 0.0).astype(BF16)
+
+    for i in range(piece_rows // KEY_TILE):
+        pl.when(i < tiles - 1)(functools.partial(lay, i, True))
+        pl.when(i == tiles - 1)(functools.partial(lay, i, False))
+
+
+def early_kernel(share, block_rows, plan_ref, *refs):
+    pieces, (out_ref, limit_ref) = refs[:-2], refs[-2:]
+    me = lax.axis_index("tp")
+    owners = [me ^ j for j in range(len(pieces))]
+    lay_out(share, block_rows, plan_ref[0], owners, pieces, out_ref)
+    limit_ref[...] = functools.reduce(
+        jnp.maximum, [longest(piece[:, : piece.shape[1] // 2]) for piece in pieces]
+    )
+
+
 def attend_kernel(share, block_rows, start_row, rows, plan_ref, q_ref, kv_ref, new_ref, *refs):
     limits_ref, pieces, wout_hbm = refs[0], refs[1:5], refs[5]
     total, high, context, wout, sem = refs[-5:]
+    most_ref, most_limit_ref = refs[6:8]
     if start_row:
-        old_ref, old_limit_ref, before_ref, far0_ref, far1_ref, near0_ref, near1_ref = refs[6:13]
+        rest_ref, rest_limit_ref, before_ref, far0_ref, far1_ref, near0_ref, near1_ref = refs[8:15]
     else:
-        far1_ref, near1_ref, context_out, old_ref, old_limit_ref = refs[6:11]
+        far1_ref, near1_ref, context_out, rest_ref, rest_limit_ref = refs[8:13]
     me = lax.axis_index("tp")
     held, span = plan_ref[0], plan_ref[1]
     piece_rows, width = pieces[0].shape
@@ -183,31 +220,13 @@
     most = piece_rows // KEY_TILE
     tiles = (held + group - 1) // group
     if not start_row:
-        row = lax.broadcasted_iota(jnp.int32, (KEY_TILE, hd), 0)
-        place = row // share * block_rows + row % share
-        limit = jnp.zeros((8, 128), F32)
-
-        def lay(i, whole):
-            source = pl.ds(i * KEY_TILE, KEY_TILE)
-            for j, piece in enumerate(pieces):
-                at = pl.ds(i * group + j * KEY_TILE, KEY_TILE)
-                if whole:
-                    old_ref[at, hd:] = piece[source, hd:]
-                    old_ref[at, :hd] = jnp.ones((KEY_TILE, hd), BF16)
-                    continue
-                used = place + (me ^ j) * share + i * group < held
-                old_ref[at, hd:] = jnp.where(used, piece[source, hd:].astype(F32), 0.0).astype(BF16)
-                old_ref[at, :hd] = jnp.where(used, 1.0, 0.0).astype(BF16)
-
-        for i in range(most):
-            pl.when(i < tiles - 1)(functools.partial(lay, i, True))
-            pl.when(i == tiles - 1)(functools.partial(lay, i, False))
-        for piece in pieces:
-            limit = jnp.maximum(limit, longest(piece[:, :hd]))
-        old_limit_ref[...] = limit
+        corner = len(pieces) - 1
+        lay_out(share, block_rows, held, [me ^ corner], pieces[corner:], rest_ref)
+        rest_limit_ref[...] = longest(pieces[corner][:, :hd])
 
     factor = hd ** (-0.5) * math.log2(math.e)
-    key_limit = jnp.max(jnp.maximum(old_limit_ref[...], limits_ref[0]))
+    old_limit = jnp.maximum(most_limit_ref[...], rest_limit_ref[...])
+    key_limit = jnp.max(jnp.maximum(old_limit, limits_ref[0]))
     small = key_limit * jnp.max(limits_ref[1]) * (1.05 / hd) < SAFE * SAFE
 
     tile_rows = ROW_TILE * heads
@@ -218,6 +237,14 @@
     def old_keys(i):
         source = pl.ds(i * KEY_TILE, KEY_TILE)
         return jnp.concatenate([piece[source, :hd] for piece in pieces], axis=0)
+
+    def old_values(i):
+        parts = []
+        for ref, count in ((most_ref, len(pieces) - 1), (rest_ref, 1)):
+            size = count * KEY_TILE
+            at = i * size if isinstance(i, int) else pl.multiple_of(i * size, KEY_TILE)
+            parts.append(ref[pl.ds(at, size), :])
+        return jnp.concatenate(parts, axis=0)
 
     def new_scores(t):
         known = start_row + t * ROW_TILE
@@ -253,7 +280,7 @@
             if at + 1 < len(steps):
                 ahead = score(*steps[at + 1])
             weights = jnp.exp2(scores * factor).astype(BF16)
-            values = new_values(t) if i == used else old_ref[pl.ds(i * group, group), :]
+            values = new_values(t) if i == used else old_values(i)
             part = dot(weights, values)
             both = part if i == 0 else both + part
             if i == used:
@@ -276,7 +303,7 @@
 
         def add(i, carry):
             weights = jnp.exp2((old_scores(i) - high[:, :1]) * factor).astype(BF16)
-            total[...] += dot(weights, old_ref[pl.ds(pl.multiple_of(i * group, group), group), :])
+            total[...] += dot(weights, old_values(i))
             return carry
 
         high[...] = jnp.zeros_like(high) + jnp.max(new_scores(t), axis=1, keepdims=True)
@@ -475,9 +502,23 @@
             keep, got = sent[0], swap(sent[1], 1, "seq")
         cached = (ordered, c_beside, c_across, swap(c_across, 1))
 
+    with jax.named_scope("early"):
+        early = call(
+            functools.partial(early_kernel, share, block_rows),
+            [
+                jax.ShapeDtypeStruct(((tp - 1) * piece_rows, width), BF16),
+                jax.ShapeDtypeStruct((8, 128), F32),
+            ],
+            [SMEM] + [VMEM] * (tp - 1),
+            (plan, *cached[:-1]),
+            flops=1 << 30,
+            mib=EARLY_MIB,
+            name="early",
+        )
+
     part = rows // CHUNKS
     tile_rows = ROW_TILE * (q_cols // hd)
-    old = []
+    old = list(early)
     mixed = None
     for c in range(CHUNKS):
         last = c == CHUNKS - 1
@@ -490,7 +531,7 @@
                     of_part,
                     of_part,
                     jax.ShapeDtypeStruct((part, q_cols), BF16),
-                    jax.ShapeDtypeStruct((most_held, width), BF16),
+                    jax.ShapeDtypeStruct((piece_rows, width), BF16),
                     jax.ShapeDtypeStruct((8, 128), F32),
                 ]
             seen = most_held + (c + 1) * part
@@ -514,9 +555,11 @@
             if last:
                 far0, far1, near0, near1 = sums
             else:
-                far1, near1, before_rows, *old = sums
-                old.append(before_rows)
+                far1, near1, before_rows, *rest = sums
+                old += [*rest, before_rows]
         with jax.named_scope("reduce"):
+            if last and phased:
+                far1, got = lax.optimization_barrier((far1, got))
             got1 = swap(far1, 1)
             if c and last:
                 before = hand_on(before)
@@ -524,8 +567,6 @@
             pair = (near1.astype(F32) + got1.astype(F32)).astype(BF16)
             if not last:
                 query, pair = lax.optimization_barrier((query, pair))
-                if phased:
-                    old[0], got = lax.optimization_barrier((old[0], got))
             if last and phased:
                 pair, got = lax.optimization_barrier((pair, got))
             crossed = swap(pair, 2)

time: 63.1 us -> 59.6 us (0.945)
  the two profiles are of different devices: /device:TPU:2 before, /device:TPU:0 now
where the time goes in v2:
time: 59.6 us; the launch traced here: 59.9 us
  starting transfers between devices  24.2 us (41%)
  Pallas kernels  18.3 us (31%)
  waiting for transfers between devices  12.5 us (21%)
  other arithmetic  2.67 us (4%)
  between operations  2.2 us (4%)
    ppermute x15, starting transfers between devices, swap(): return lax.ppermute(x, axis, [(i, i ^ bit) for i in range(size)])  18.4 us
    pallas_call x10, Pallas kernels, call(): pl.pallas_call(kernel, out_shape=out_shape, in_specs=in_specs, out_specs=...  18.3 us
    ppermute x15, waiting for transfers between devices, swap(): return lax.ppermute(x, axis, [(i, i ^ bit) for i in range(size)])  10.2 us
    all_to_all x1, starting transfers between devices, exchange(): return lax.all_to_all(x, 'seq', split_axis=0, concat_axis=0, tiled=True)  5.81 us
    all_to_all x1, waiting for transfers between devices, exchange(): return lax.all_to_all(x, 'seq', split_axis=0, concat_axis=0, tiled=True)  2.26 us
  transfers between devices with their start and end apart: 16, of which 9 were waited for; matrix products, arithmetic and copies ran while one was open for 4% of the time, Pallas kernels for 21%

profile of v2, /device:TPU:0, one launch (start us, length us, event | category | flops | bytes accessed | tf_op | source)
XLA Modules:
  0.0 59.9 jit_solution(3794148401430573431)
XLA Ops:
  0.6 3.0 %collective-permute-start = (bf16[512,512]{1,0:T(8,128)(2,1)}, bf16[512,512]{1,0:T(8,128)(2,1)S(1)}, u32[]{:S(2)}, u32[]{:S(2)}) collective-permute-start(bf16[512,512]{1,0:T(8,128)(2,1)} %param.10), channel_id=1, source_target_pairs={{0,2},{1,3},{2,0},{3,1},{4,6},{5,7},{6,4},{7,5},{8,10},{9,11},{10,... | collective-permute-start | bytes 1572872 | tf_op jit(solution)/shard_map/tokens_gather/ppermute | solution.py:425
  3.7 0.7 %broadcast_maximum_fusion.1 = f32[2048]{0:T(1024)S(1)} fusion(f32[2048]{0:T(1024)} %param.11), kind=kLoop, calls=%fused_computation.3 | loop fusion | flops 2048 | bytes 16384 | tf_op jit(solution)/shard_map/cache_gather/max | solution.py:437
  4.4 5.8 %all-to-all-start = ((bf16[8,64,256]{2,1,0:T(8,128)(2,1)}), bf16[8,64,256]{2,1,0:T(8,128)(2,1)S(1)}, u32[]{:S(2)}, u32[]{:S(2)}) async-start(bf16[8,64,256]{2,1,0:T(8,128)(2,1)} %param.19), calls=%async_computation | async-start | bytes 524288 | tf_op jit(solution)/shard_map/cache_gather/all_to_all | solution.py:428
  11.5 1.1 %broadcast_maximum_fusion.x0.tokens_ref = bf16[512,512]{1,0:T(8,128)(2,1)S(1)} fusion(bf16[512,512]{1,0:T(8,128)(2,1)} %param.10), kind=kLoop, calls=%fused_computation.2 | loop fusion | flops 262144 | bytes 1048576 | tf_op jit(solution)/shard_map/cache_gather/max | solution.py:440
  12.6 3.2 %collective-permute-done.x2 = bf16[512,512]{1,0:T(8,128)(2,1)S(1)} collective-permute-done((bf16[512,512]{1,0:T(8,128)(2,1)}, bf16[512,512]{1,0:T(8,128)(2,1)S(1)}, u32[]{:S(2)}, u32[]{:S(2)}) %collective-permute-start) | collective-permute-done | bytes 524320 | tf_op jit(solution)/shard_map/tokens_gather/ppermute | solution.py:425
  15.8 0.7 %pad_add_fusion.plan_ref = s32[18]{0:T(128)S(1)} fusion(s32[8]{0:T(128)} %bitcast.7, s32[8]{0:T(128)} %bitcast.8, s32[1]{0:T(128)S(6)} %copy.16, s32[1]{0:T(128)S(6)} %copy.17), kind=kLoop, calls=%fused_computation.4 | loop fusion | flops 54 | bytes 144 | tf_op jit(solution)/shard_map/cache_gather/concatenate | solution.py:444
  16.5 2.3 %all-to-all-done = bf16[8,64,256]{2,1,0:T(8,128)(2,1)S(1)} async-done(((bf16[8,64,256]{2,1,0:T(8,128)(2,1)}), bf16[8,64,256]{2,1,0:T(8,128)(2,1)S(1)}, u32[]{:S(2)}, u32[]{:S(2)}) %all-to-all-start) | async-done | bytes 262176 | tf_op jit(solution)/shard_map/cache_gather/all_to_all | solution.py:428
  20.7 4.1 %project.1 = (bf16[2048,128]{1,0:T(8,128)(2,1)S(1)}, bf16[512,256]{1,0:T(8,128)(2,1)S(1)}, bf16[512,256]{1,0:T(8,128)(2,1)S(1)}, f32[2,8,128]{2,1,0:T(8,128)S(1)}) custom-call(bf16[512,512]{1,0:T(8,128)(2,1)S(1)} %broadcast_maximum_fusion.x0.tokens_ref, bf16[512,512]{1,0:T(8,128)(2,1)S(1)} %collective-permute-done.1.x1, ...), custom_call_target="tpu_custom_call" | custom-call | flops 1610612736 | bytes 6307840 | tf_op jit(solution)/shard_map/project/project/pallas_call | solution.py:374
  24.8 1.2 %extend.1 = (bf16[4,64,256]{2,1,0:T(8,128)(2,1)S(1)}, bf16[4,64,256]{2,1,0:T(8,128)(2,1)S(1)}) custom-call(s32[18]{0:T(128)S(1)} %pad_add_fusion.plan_ref, bf16[512,256]{1,0:T(8,128)(2,1)S(1)} %get-tuple-element.61.kv_ref, bf16[512,256]{1,0:T(8,128)(2,1)S(1)} %bitcast.5), custom_call_target="tpu_custom_call" | custom-call | flops 268435456 | bytes 786504 | tf_op jit(solution)/shard_map/extend/extend/pallas_call | solution.py:374
  26.0 0.7 %collective-permute-done.4.refs_2_.refs_3_ = bf16[384,256]{1,0:T(8,128)(2,1)S(1)} collective-permute-done((bf16[384,256]{1,0:T(8,128)(2,1)S(1)}, bf16[384,256]{1,0:T(8,128)(2,1)S(1)}, u32[]{:S(2)}, u32[]{:S(2)}) %collective-permute-start.4) | collective-permute-done | bytes 196640 | tf_op jit(solution)/shard_map/cache_gather/ppermute | solution.py:425
  26.8 0.9 %early.1 = (bf16[1152,256]{1,0:T(8,128)(2,1)S(1)}, f32[8,128]{1,0:T(8,128)S(1)}) custom-call(s32[18]{0:T(128)S(1)} %pad_add_fusion.plan_ref, bf16[384,256]{1,0:T(8,128)(2,1)S(1)} %order.1.refs_0_.refs_1_, bf16[384,256]{1,0:T(8,128)(2,1)S(1)} %collective-permute-done.3.refs_1_.refs_2_, bf16[384,256]{1,0:T(8,128)(2,1)S(1)} %collective-permute-done.4.refs_2_.refs_3_), custom_call_target="tpu_custom_call" | custom-call | flops 1073741824 | bytes 1183816 | tf_op jit(solution)/shard_map/early/early/pallas_call | solution.py:374
  27.6 0.6 collective-permute-done.5.refs_4_
  28.2 5.0 %attend.2 = (bf16[256,512]{1,0:T(8,128)(2,1)S(1)}, bf16[256,512]{1,0:T(8,128)(2,1)S(1)}, bf16[256,512]{1,0:T(8,128)(2,1)S(1)}, bf16[384,256]{1,0:T(8,128)(2,1)S(1)}, f32[8,128]{1,0:T(8,128)S(1)}) custom-call(s32[18]{0:T(128)S(1)} %pad_add_fusion.plan_ref, bf16[2048,128]{1,0:T(8,128)(2,1)S(1)} %get-tuple-element.72.q_ref, ...), custom_call_target="tpu_custom_call" | custom-call | flops 1476395008 | bytes 5521480 | tf_op jit(solution)/shard_map/attend/attend/pallas_call | solution.py:374
  33.4 1.4 %collective-permute-done.6 = bf16[256,512]{1,0:T(8,128)(2,1)S(1)} collective-permute-done((bf16[256,512]{1,0:T(8,128)(2,1)S(1)}, bf16[256,512]{1,0:T(8,128)(2,1)S(1)}, u32[]{:S(2)}, u32[]{:S(2)}) %collective-permute-start.6) | collective-permute-done | bytes 262176 | tf_op jit(solution)/shard_map/reduce/ppermute | solution.py:425
  35.4 5.2 %collective-permute-start.9 = (bf16[4,64,256]{2,1,0:T(8,128)(2,1)S(1)}, bf16[4,64,256]{2,1,0:T(8,128)(2,1)S(1)}, u32[]{:S(2)}, u32[]{:S(2)}) collective-permute-start(bf16[4,64,256]{2,1,0:T(8,128)(2,1)S(1)} %get-tuple-element.81), channel_id=1, source_target_pairs={{0,4},{4,0},{8,12},{12,8},{16,20},{20,16},{24,28},{28,24},{1,5},{5... | collective-permute-start | bytes 393224 | tf_op jit(solution)/shard_map/extend/ppermute | solution.py:425
  40.6 3.1 %attend.3 = (bf16[512,512]{1,0:T(8,128)(2,1)S(1)}, bf16[256,512]{1,0:T(8,128)(2,1)S(1)}, bf16[512,512]{1,0:T(8,128)(2,1)S(1)}, bf16[256,512]{1,0:T(8,128)(2,1)S(1)}) custom-call(s32[18]{0:T(128)S(1)} %pad_add_fusion.plan_ref, bf16[2048,128]{1,0:T(8,128)(2,1)S(1)} %get-tuple-element.72.q_ref, bf16[512,256]{1,0:T(8,128)(2,1)S(1)} %get-tuple-element.61.kv_ref, ...), custom_call_target="tpu_custom_call" | custom-call | flops 1610612736 | bytes 6570056 | tf_op jit(solution)/shard_map/attend/attend/pallas_call | solution.py:374
  44.6 1.0 %collective-permute-done.10 = bf16[256,512]{1,0:T(8,128)(2,1)S(1)} collective-permute-done((bf16[256,512]{1,0:T(8,128)(2,1)S(1)}, bf16[256,512]{1,0:T(8,128)(2,1)S(1)}, u32[]{:S(2)}, u32[]{:S(2)}) %collective-permute-start.10) | collective-permute-done | bytes 262176 | tf_op jit(solution)/shard_map/reduce/ppermute | solution.py:425
  45.7 1.6 %collective-permute-start.11 = (bf16[256,512]{1,0:T(8,128)(2,1)S(1)}, bf16[256,512]{1,0:T(8,128)(2,1)S(1)}, u32[]{:S(2)}, u32[]{:S(2)}) collective-permute-start(bf16[256,512]{1,0:T(8,128)(2,1)S(1)} %add_convert_fusion), channel_id=1, source_target_pairs={{0,2},{1,3},{2,0},{3,1},{4,6},{5,7},{6,4},{7,5},{8,10},{9,11},{10,... | collective-permute-start | bytes 786440 | tf_op jit(solution)/shard_map/reduce/ppermute | solution.py:425
  47.3 4.1 %collective-permute-start.12 = (bf16[2,64,256]{2,1,0:T(8,128)(2,1)S(1)}, bf16[2,64,256]{2,1,0:T(8,128)(2,1)S(1)}, u32[]{:S(2)}, u32[]{:S(2)}) collective-permute-start(bf16[2,64,256]{2,1,0:T(8,128)(2,1)S(1)} %get-tuple-element.90), channel_id=1, source_target_pairs={{0,8},{4,12},{8,0},{12,4},{16,24},{20,28},{24,16},{28,20},{1,9},{5... | collective-permute-start | bytes 196616 | tf_op jit(solution)/shard_map/exchange/ppermute | solution.py:425
  51.4 2.4 %collective-permute-start.14 = (bf16[2,64,256]{2,1,0:T(8,128)(2,1)S(1)}, bf16[2,64,256]{2,1,0:T(8,128)(2,1)S(1)}, u32[]{:S(2)}, u32[]{:S(2)}) collective-permute-start(bf16[2,64,256]{2,1,0:T(8,128)(2,1)S(1)} %get-tuple-element.92), channel_id=1, source_target_pairs={{0,24},{4,28},{8,16},{12,20},{16,8},{20,12},{24,0},{28,4},{1,25},{... | collective-permute-start | bytes 196616 | tf_op jit(solution)/shard_map/exchange/ppermute | solution.py:425
  53.9 1.4 %finish.2.refs_0_ = bf16[512,512]{1,0:T(8,128)(2,1)} custom-call(s32[18]{0:T(128)S(1)} %pad_add_fusion.plan_ref, bf16[512,512]{1,0:T(8,128)(2,1)S(1)} %broadcast_maximum_fusion.x0.tokens_ref, bf16[512,512]{1,0:T(8,128)(2,1)S(1)} %get-tuple-element.76.near_ref, bf16[512,512]{1,0:T(8,128)(2,1)S(1)} %collective-permute-done.7.got_ref, ...), custom_call_target="tpu_custom_call" | custom-call | flops 524288 | bytes 2359368 | tf_op jit(solution)/shard_map/finish/finish/pallas_call | solution.py:374
  55.2 1.4 %finish.3 = bf16[512,512]{1,0:T(8,128)(2,1)} custom-call(s32[18]{0:T(128)S(1)} %pad_add_fusion.plan_ref, bf16[512,512]{1,0:T(8,128)(2,1)S(1)} %broadcast_maximum_fusion.x0.tokens_ref, bf16[512,512]{1,0:T(8,128)(2,1)S(1)} %get-tuple-element.76.near_ref, bf16[512,512]{1,0:T(8,128)(2,1)S(1)} %collective-permute-done.7.got_ref, ...), custom_call_target="tpu_custom_call", output_to_operand_aliasing={{}: (5, {})} | custom-call | flops 524288 | bytes 2883656 | tf_op jit(solution)/shard_map/finish/finish/pallas_call | solution.py:374
  56.6 2.3 %collective-permute-done.13.p2 = bf16[2,64,256]{2,1,0:T(8,128)(2,1)S(1)} collective-permute-done((bf16[2,64,256]{2,1,0:T(8,128)(2,1)S(1)}, bf16[2,64,256]{2,1,0:T(8,128)(2,1)S(1)}, u32[]{:S(2)}, u32[]{:S(2)}) %collective-permute-start.13) | collective-permute-done | bytes 65568 | tf_op jit(solution)/shard_map/exchange/ppermute | solution.py:425
  58.9 0.8 %place.1 = bf16[8,64,256]{2,1,0:T(8,128)(2,1)} custom-call(bf16[2,64,256]{2,1,0:T(8,128)(2,1)S(1)} %get-tuple-element.94.p0, bf16[2,64,256]{2,1,0:T(8,128)(2,1)S(1)} %collective-permute-done.12.p1, bf16[2,64,256]{2,1,0:T(8,128)(2,1)S(1)} %collective-permute-done.13.p2, bf16[2,64,256]{2,1,0:T(8,128)(2,1)S(1)} %collective-permute-done.14.p3), custom_call_target="tpu_custom_call" | custom-call | bytes 524288 | tf_op jit(solution)/shard_map/finish/place/pallas_call | solution.py:374
  (24 shorter events, 3.7 us)
Async XLA Ops:
  0.6 15.2 %collective-permute-start = (bf16[512,512]{1,0:T(8,128)(2,1)}, bf16[512,512]{1,0:T(8,128)(2,1)S(1)}, u32[]{:S(2)}, u32[]{:S(2)}) collective-permute-start(bf16[512,512]{1,0:T(8,128)(2,1)} %param.10), channel_id=1, source_target_pairs={{0,2},{1,3},{2,0},{3,1},{4,6},{5,7},{6,4},{7,5},{8,10},{9,11},{10,... | collective-permute-start | bytes 1572872 | tf_op jit(solution)/shard_map/tokens_gather/ppermute | solution.py:425
  4.4 14.4 %all-to-all-start = ((bf16[8,64,256]{2,1,0:T(8,128)(2,1)}), bf16[8,64,256]{2,1,0:T(8,128)(2,1)S(1)}, u32[]{:S(2)}, u32[]{:S(2)}) async-start(bf16[8,64,256]{2,1,0:T(8,128)(2,1)} %param.19), calls=%async_computation | async-start | bytes 524288 | tf_op jit(solution)/shard_map/cache_gather/all_to_all | solution.py:428
  10.2 10.0 %collective-permute-start.1 = (bf16[512,512]{1,0:T(8,128)(2,1)}, bf16[512,512]{1,0:T(8,128)(2,1)S(1)}, u32[]{:S(2)}, u32[]{:S(2)}) collective-permute-start(bf16[512,512]{1,0:T(8,128)(2,1)} %param.10), channel_id=1, source_target_pairs={{0,1},{1,0},{2,3},{3,2},{4,5},{5,4},{6,7},{7,6},{8,9},{9,8},{10,11... | collective-permute-start | bytes 1572872 | tf_op jit(solution)/shard_map/tokens_gather/ppermute | solution.py:425
  18.8 1.9 %collective-permute-start.2 = (bf16[512,512]{1,0:T(8,128)(2,1)S(1)}, bf16[512,512]{1,0:T(8,128)(2,1)S(1)}, u32[]{:S(2)}, u32[]{:S(2)}) collective-permute-start(bf16[512,512]{1,0:T(8,128)(2,1)S(1)} %collective-permute-done.x2), channel_id=1, source_target_pairs={{0,1},{1,0},{2,3},{3,2},{4,5},{5,4},{6,7},{7,6},{8,9},{9,8},{10,11... | collective-permute-start | bytes 1572872 | tf_op jit(solution)/shard_map/project/ppermute | solution.py:425
  19.4 7.4 %collective-permute-start.4 = (bf16[384,256]{1,0:T(8,128)(2,1)S(1)}, bf16[384,256]{1,0:T(8,128)(2,1)S(1)}, u32[]{:S(2)}, u32[]{:S(2)}) collective-permute-start(bf16[384,256]{1,0:T(8,128)(2,1)S(1)} %order.1.refs_0_.refs_1_), channel_id=1, source_target_pairs={{0,2},{1,3},{2,0},{3,1},{4,6},{5,7},{6,4},{7,5},{8,10},{9,11},{10,... | collective-permute-start | bytes 589832 | tf_op jit(solution)/shard_map/cache_gather/ppermute | solution.py:425
  19.9 6.8 %collective-permute-start.3 = (bf16[384,256]{1,0:T(8,128)(2,1)S(1)}, bf16[384,256]{1,0:T(8,128)(2,1)S(1)}, u32[]{:S(2)}, u32[]{:S(2)}) collective-permute-start(bf16[384,256]{1,0:T(8,128)(2,1)S(1)} %order.1.refs_0_.refs_1_), channel_id=1, source_target_pairs={{0,1},{1,0},{2,3},{3,2},{4,5},{5,4},{6,7},{7,6},{8,9},{9,8},{10,11... | collective-permute-start | bytes 589832 | tf_op jit(solution)/shard_map/cache_gather/ppermute | solution.py:425
  26.8 1.4 %collective-permute-start.5 = (bf16[384,256]{1,0:T(8,128)(2,1)S(1)}, bf16[384,256]{1,0:T(8,128)(2,1)S(1)}, u32[]{:S(2)}, u32[]{:S(2)}) collective-permute-start(bf16[384,256]{1,0:T(8,128)(2,1)S(1)} %collective-permute-done.4.refs_2_.refs_3_), channel_id=1, source_target_pairs={{0,1},{1,0},{2,3},{3,2},{4,5},{5,4},{6,7},{7,6},{8,9},{9,8},{10,11... | collective-permute-start | bytes 589832 | tf_op jit(solution)/shard_map/extend/ppermute | solution.py:425
  33.2 1.6 %collective-permute-start.6 = (bf16[256,512]{1,0:T(8,128)(2,1)S(1)}, bf16[256,512]{1,0:T(8,128)(2,1)S(1)}, u32[]{:S(2)}, u32[]{:S(2)}) collective-permute-start(bf16[256,512]{1,0:T(8,128)(2,1)S(1)} %get-tuple-element.71), channel_id=1, source_target_pairs={{0,1},{1,0},{2,3},{3,2},{4,5},{5,4},{6,7},{7,6},{8,9},{9,8},{10,11... | collective-permute-start | bytes 786440 | tf_op jit(solution)/shard_map/reduce/ppermute | solution.py:425
  34.8 9.8 %collective-permute-start.8 = (bf16[256,512]{1,0:T(8,128)(2,1)S(1)}, bf16[256,512]{1,0:T(8,128)(2,1)S(1)}, u32[]{:S(2)}, u32[]{:S(2)}) collective-permute-start(bf16[256,512]{1,0:T(8,128)(2,1)S(1)} %add_convert_fusion.1), channel_id=1, source_target_pairs={{0,2},{1,3},{2,0},{3,1},{4,6},{5,7},{6,4},{7,5},{8,10},{9,11},{10,... | collective-permute-start | bytes 786440 | tf_op jit(solution)/shard_map/reduce/ppermute | solution.py:425
  35.4 8.7 %collective-permute-start.9 = (bf16[4,64,256]{2,1,0:T(8,128)(2,1)S(1)}, bf16[4,64,256]{2,1,0:T(8,128)(2,1)S(1)}, u32[]{:S(2)}, u32[]{:S(2)}) collective-permute-start(bf16[4,64,256]{2,1,0:T(8,128)(2,1)S(1)} %get-tuple-element.81), channel_id=1, source_target_pairs={{0,4},{4,0},{8,12},{12,8},{16,20},{20,16},{24,28},{28,24},{1,5},{5... | collective-permute-start | bytes 393224 | tf_op jit(solution)/shard_map/extend/ppermute | solution.py:425
  44.1 1.5 %collective-permute-start.10 = (bf16[256,512]{1,0:T(8,128)(2,1)S(1)}, bf16[256,512]{1,0:T(8,128)(2,1)S(1)}, u32[]{:S(2)}, u32[]{:S(2)}) collective-permute-start(bf16[256,512]{1,0:T(8,128)(2,1)S(1)} %get-tuple-element.82), channel_id=1, source_target_pairs={{0,1},{1,0},{2,3},{3,2},{4,5},{5,4},{6,7},{7,6},{8,9},{9,8},{10,11... | collective-permute-start | bytes 786440 | tf_op jit(solution)/shard_map/reduce/ppermute | solution.py:425
  44.1 9.7 %collective-permute-start.7 = (bf16[512,512]{1,0:T(8,128)(2,1)S(1)}, bf16[512,512]{1,0:T(8,128)(2,1)S(1)}, u32[]{:S(2)}, u32[]{:S(2)}) collective-permute-start(bf16[512,512]{1,0:T(8,128)(2,1)S(1)} %get-tuple-element.77), channel_id=1, source_target_pairs={{0,1},{1,0},{2,3},{3,2},{4,5},{5,4},{6,7},{7,6},{8,9},{9,8},{10,11... | collective-permute-start | bytes 1572872 | tf_op jit(solution)/shard_map/finish/ppermute | solution.py:425
  45.7 9.5 %collective-permute-start.11 = (bf16[256,512]{1,0:T(8,128)(2,1)S(1)}, bf16[256,512]{1,0:T(8,128)(2,1)S(1)}, u32[]{:S(2)}, u32[]{:S(2)}) collective-permute-start(bf16[256,512]{1,0:T(8,128)(2,1)S(1)} %add_convert_fusion), channel_id=1, source_target_pairs={{0,2},{1,3},{2,0},{3,1},{4,6},{5,7},{6,4},{7,5},{8,10},{9,11},{10,... | collective-permute-start | bytes 786440 | tf_op jit(solution)/shard_map/reduce/ppermute | solution.py:425
  47.3 9.3 %collective-permute-start.12 = (bf16[2,64,256]{2,1,0:T(8,128)(2,1)S(1)}, bf16[2,64,256]{2,1,0:T(8,128)(2,1)S(1)}, u32[]{:S(2)}, u32[]{:S(2)}) collective-permute-start(bf16[2,64,256]{2,1,0:T(8,128)(2,1)S(1)} %get-tuple-element.90), channel_id=1, source_target_pairs={{0,8},{4,12},{8,0},{12,4},{16,24},{20,28},{24,16},{28,20},{1,9},{5... | collective-permute-start | bytes 196616 | tf_op jit(solution)/shard_map/exchange/ppermute | solution.py:425
  51.4 7.5 %collective-permute-start.13 = (bf16[2,64,256]{2,1,0:T(8,128)(2,1)S(1)}, bf16[2,64,256]{2,1,0:T(8,128)(2,1)S(1)}, u32[]{:S(2)}, u32[]{:S(2)}) collective-permute-start(bf16[2,64,256]{2,1,0:T(8,128)(2,1)S(1)} %get-tuple-element.91), channel_id=1, source_target_pairs={{0,16},{4,20},{8,24},{12,28},{16,0},{20,4},{24,8},{28,12},{1,17},{... | collective-permute-start | bytes 196616 | tf_op jit(solution)/shard_map/exchange/ppermute | solution.py:425
  51.4 7.5 %collective-permute-start.14 = (bf16[2,64,256]{2,1,0:T(8,128)(2,1)S(1)}, bf16[2,64,256]{2,1,0:T(8,128)(2,1)S(1)}, u32[]{:S(2)}, u32[]{:S(2)}) collective-permute-start(bf16[2,64,256]{2,1,0:T(8,128)(2,1)S(1)} %get-tuple-element.92), channel_id=1, source_target_pairs={{0,24},{4,28},{8,16},{12,20},{16,8},{20,12},{24,0},{28,4},{1,25},{... | collective-permute-start | bytes 196616 | tf_op jit(solution)/shard_map/exchange/ppermute | solution.py:425

commit v3 on v2

--- a/solution.py
+++ b/solution.py
@@ -43,7 +43,7 @@
         pair_ref[1] = got_ref[k]
 
 
-def place_kernel(p0, p1, p2, p3, out_hbm, sems):
+def place_kernel(p3, p2, p1, p0, out_hbm, sems):
     me = lax.axis_index("seq")
     stores = []
     for k, pair_ref in enumerate((p0, p1, p2, p3)):
@@ -584,7 +584,7 @@
                 mib=8,
                 name="pair",
             ))
-            for k in range(len(pairs) - 1, 0, -1):
+            for k in range(len(pairs) - 1, 1, -1):
                 pairs[k] = swap(pairs[k], 2 * k, "seq")
         else:
             new_cache = exchange(sent[0].reshape(groups, share, width))
@@ -603,13 +603,16 @@
                 name="finish",
                 into={5: 0} if at else {},
             )
+            if phased and not at:
+                mixed, pairs[1] = lax.optimization_barrier((mixed, pairs[1]))
+                pairs[1] = swap(pairs[1], 2, "seq")
         if phased:
             mixed, *pairs = lax.optimization_barrier((mixed, *pairs))
             new_cache = call(
                 place_kernel,
                 jax.ShapeDtypeStruct(old_cache.shape, BF16),
                 [VMEM] * len(pairs),
-                pairs,
+                pairs[::-1],
                 flops=0,
                 mib=8,
                 scratch=[pltpu.SemaphoreType.DMA((groups,))],

time: 59.6 us -> 60.4 us (1.013)
  Pallas kernels: 18.3 us -> 24.5 us
  starting transfers between devices: 24.2 us -> 19.5 us
  waiting for transfers between devices: 12.5 us -> 11.5 us
    pallas_call x10, Pallas kernels: 18.3 us -> 24.5 us  [call(): pl.pallas_call(kernel, out_shape=out_shape, in_specs=in_specs, out_specs=...]
    ppermute x15, starting transfers between devices: 18.4 us -> 13.7 us  [swap(): return lax.ppermute(x, axis, [(i, i ^ bit) for i in range(size)])]
    ppermute x15, waiting for transfers between devices: 10.2 us -> 9.29 us  [swap(): return lax.ppermute(x, axis, [(i, i ^ bit) for i in range(size)])]
  transfers between devices with their start and end apart: 16 -> 16, of which waited for: 9 -> 8; matrix products, arithmetic and copies ran while one was open for 4% -> 4% of each run, Pallas kernels for 21% -> 28%
where the time goes in v3:
time: 60.4 us; the launch traced here: 60.5 us
  Pallas kernels  24.5 us (41%)
  starting transfers between devices  19.5 us (32%)
  waiting for transfers between devices  11.5 us (19%)
  other arithmetic  2.67 us (4%)
  between operations  2.23 us (4%)
    pallas_call x10, Pallas kernels, call(): pl.pallas_call(kernel, out_shape=out_shape, in_specs=in_specs, out_specs=...  24.5 us
    ppermute x15, starting transfers between devices, swap(): return lax.ppermute(x, axis, [(i, i ^ bit) for i in range(size)])  13.7 us
    ppermute x15, waiting for transfers between devices, swap(): return lax.ppermute(x, axis, [(i, i ^ bit) for i in range(size)])  9.29 us
    all_to_all x1, starting transfers between devices, exchange(): return lax.all_to_all(x, 'seq', split_axis=0, concat_axis=0, tiled=True)  5.81 us
    all_to_all x1, waiting for transfers between devices, exchange(): return lax.all_to_all(x, 'seq', split_axis=0, concat_axis=0, tiled=True)  2.26 us
  transfers between devices with their start and end apart: 16, of which 8 were waited for; matrix products, arithmetic and copies ran while one was open for 4% of the time, Pallas kernels for 28%

profile of v3, /device:TPU:0, one launch (start us, length us, event | category | flops | bytes accessed | tf_op | source)
XLA Modules:
  0.0 60.5 jit_solution(15966275457512358667)
XLA Ops:
  0.6 3.0 %collective-permute-start = (bf16[512,512]{1,0:T(8,128)(2,1)}, bf16[512,512]{1,0:T(8,128)(2,1)S(1)}, u32[]{:S(2)}, u32[]{:S(2)}) collective-permute-start(bf16[512,512]{1,0:T(8,128)(2,1)} %param.10), channel_id=1, source_target_pairs={{0,2},{1,3},{2,0},{3,1},{4,6},{5,7},{6,4},{7,5},{8,10},{9,11},{10,... | collective-permute-start | bytes 1572872 | tf_op jit(solution)/shard_map/tokens_gather/ppermute | solution.py:425
  3.7 0.7 %broadcast_maximum_fusion.1 = f32[2048]{0:T(1024)S(1)} fusion(f32[2048]{0:T(1024)} %param.11), kind=kLoop, calls=%fused_computation.3 | loop fusion | flops 2048 | bytes 16384 | tf_op jit(solution)/shard_map/cache_gather/max | solution.py:437
  4.4 5.8 %all-to-all-start = ((bf16[8,64,256]{2,1,0:T(8,128)(2,1)}), bf16[8,64,256]{2,1,0:T(8,128)(2,1)S(1)}, u32[]{:S(2)}, u32[]{:S(2)}) async-start(bf16[8,64,256]{2,1,0:T(8,128)(2,1)} %param.19), calls=%async_computation | async-start | bytes 524288 | tf_op jit(solution)/shard_map/cache_gather/all_to_all | solution.py:428
  11.5 1.1 %broadcast_maximum_fusion.x0.tokens_ref = bf16[512,512]{1,0:T(8,128)(2,1)S(1)} fusion(bf16[512,512]{1,0:T(8,128)(2,1)} %param.10), kind=kLoop, calls=%fused_computation.2 | loop fusion | flops 262144 | bytes 1048576 | tf_op jit(solution)/shard_map/cache_gather/max | solution.py:440
  12.6 3.2 %collective-permute-done.x2 = bf16[512,512]{1,0:T(8,128)(2,1)S(1)} collective-permute-done((bf16[512,512]{1,0:T(8,128)(2,1)}, bf16[512,512]{1,0:T(8,128)(2,1)S(1)}, u32[]{:S(2)}, u32[]{:S(2)}) %collective-permute-start) | collective-permute-done | bytes 524320 | tf_op jit(solution)/shard_map/tokens_gather/ppermute | solution.py:425
  15.8 0.7 %pad_add_fusion.plan_ref = s32[18]{0:T(128)S(1)} fusion(s32[8]{0:T(128)} %bitcast.7, s32[8]{0:T(128)} %bitcast.8, s32[1]{0:T(128)S(6)} %copy.16, s32[1]{0:T(128)S(6)} %copy.17), kind=kLoop, calls=%fused_computation.4 | loop fusion | flops 54 | bytes 144 | tf_op jit(solution)/shard_map/cache_gather/concatenate | solution.py:444
  16.5 2.3 %all-to-all-done = bf16[8,64,256]{2,1,0:T(8,128)(2,1)S(1)} async-done(((bf16[8,64,256]{2,1,0:T(8,128)(2,1)}), bf16[8,64,256]{2,1,0:T(8,128)(2,1)S(1)}, u32[]{:S(2)}, u32[]{:S(2)}) %all-to-all-start) | async-done | bytes 262176 | tf_op jit(solution)/shard_map/cache_gather/all_to_all | solution.py:428
  19.4 0.6 collective-permute-start.4
  20.7 4.1 %project.1 = (bf16[2048,128]{1,0:T(8,128)(2,1)S(1)}, bf16[512,256]{1,0:T(8,128)(2,1)S(1)}, bf16[512,256]{1,0:T(8,128)(2,1)S(1)}, f32[2,8,128]{2,1,0:T(8,128)S(1)}) custom-call(bf16[512,512]{1,0:T(8,128)(2,1)S(1)} %broadcast_maximum_fusion.x0.tokens_ref, bf16[512,512]{1,0:T(8,128)(2,1)S(1)} %collective-permute-done.1.x1, ...), custom_call_target="tpu_custom_call" | custom-call | flops 1610612736 | bytes 6307840 | tf_op jit(solution)/shard_map/project/project/pallas_call | solution.py:374
  24.8 1.2 %extend.1 = (bf16[4,64,256]{2,1,0:T(8,128)(2,1)S(1)}, bf16[4,64,256]{2,1,0:T(8,128)(2,1)S(1)}) custom-call(s32[18]{0:T(128)S(1)} %pad_add_fusion.plan_ref, bf16[512,256]{1,0:T(8,128)(2,1)S(1)} %get-tuple-element.63.kv_ref, bf16[512,256]{1,0:T(8,128)(2,1)S(1)} %bitcast.5), custom_call_target="tpu_custom_call" | custom-call | flops 268435456 | bytes 786504 | tf_op jit(solution)/shard_map/extend/extend/pallas_call | solution.py:374
  26.0 0.7 %collective-permute-done.4.refs_2_.refs_3_ = bf16[384,256]{1,0:T(8,128)(2,1)S(1)} collective-permute-done((bf16[384,256]{1,0:T(8,128)(2,1)S(1)}, bf16[384,256]{1,0:T(8,128)(2,1)S(1)}, u32[]{:S(2)}, u32[]{:S(2)}) %collective-permute-start.4) | collective-permute-done | bytes 196640 | tf_op jit(solution)/shard_map/cache_gather/ppermute | solution.py:425
  26.8 0.9 %early.1 = (bf16[1152,256]{1,0:T(8,128)(2,1)S(1)}, f32[8,128]{1,0:T(8,128)S(1)}) custom-call(s32[18]{0:T(128)S(1)} %pad_add_fusion.plan_ref, bf16[384,256]{1,0:T(8,128)(2,1)S(1)} %order.1.refs_0_.refs_1_, bf16[384,256]{1,0:T(8,128)(2,1)S(1)} %collective-permute-done.3.refs_1_.refs_2_, bf16[384,256]{1,0:T(8,128)(2,1)S(1)} %collective-permute-done.4.refs_2_.refs_3_), custom_call_target="tpu_custom_call" | custom-call | flops 1073741824 | bytes 1183816 | tf_op jit(solution)/shard_map/early/early/pallas_call | solution.py:374
  28.2 6.8 %attend.2 = (bf16[256,512]{1,0:T(8,128)(2,1)S(1)}, bf16[256,512]{1,0:T(8,128)(2,1)S(1)}, bf16[256,512]{1,0:T(8,128)(2,1)S(1)}, bf16[384,256]{1,0:T(8,128)(2,1)S(1)}, f32[8,128]{1,0:T(8,128)S(1)}) custom-call(s32[18]{0:T(128)S(1)} %pad_add_fusion.plan_ref, bf16[2048,128]{1,0:T(8,128)(2,1)S(1)} %get-tuple-element.74.q_ref, ...), custom_call_target="tpu_custom_call" | custom-call | flops 1476395008 | bytes 5521480 | tf_op jit(solution)/shard_map/attend/attend/pallas_call | solution.py:374
  35.3 1.4 %collective-permute-done.6 = bf16[256,512]{1,0:T(8,128)(2,1)S(1)} collective-permute-done((bf16[256,512]{1,0:T(8,128)(2,1)S(1)}, bf16[256,512]{1,0:T(8,128)(2,1)S(1)}, u32[]{:S(2)}, u32[]{:S(2)}) %collective-permute-start.6) | collective-permute-done | bytes 262176 | tf_op jit(solution)/shard_map/reduce/ppermute | solution.py:425
  36.7 0.6 collective-permute-start.8
  37.3 3.3 %collective-permute-start.9 = (bf16[4,64,256]{2,1,0:T(8,128)(2,1)S(1)}, bf16[4,64,256]{2,1,0:T(8,128)(2,1)S(1)}, u32[]{:S(2)}, u32[]{:S(2)}) collective-permute-start(bf16[4,64,256]{2,1,0:T(8,128)(2,1)S(1)} %get-tuple-element.83), channel_id=1, source_target_pairs={{0,4},{4,0},{8,12},{12,8},{16,20},{20,16},{24,28},{28,24},{1,5},{5... | collective-permute-start | bytes 393224 | tf_op jit(solution)/shard_map/extend/ppermute | solution.py:425
  40.6 7.4 %attend.3 = (bf16[512,512]{1,0:T(8,128)(2,1)S(1)}, bf16[256,512]{1,0:T(8,128)(2,1)S(1)}, bf16[512,512]{1,0:T(8,128)(2,1)S(1)}, bf16[256,512]{1,0:T(8,128)(2,1)S(1)}) custom-call(s32[18]{0:T(128)S(1)} %pad_add_fusion.plan_ref, bf16[2048,128]{1,0:T(8,128)(2,1)S(1)} %get-tuple-element.74.q_ref, bf16[512,256]{1,0:T(8,128)(2,1)S(1)} %get-tuple-element.63.kv_ref, ...), custom_call_target="tpu_custom_call" | custom-call | flops 1610612736 | bytes 6570056 | tf_op jit(solution)/shard_map/attend/attend/pallas_call | solution.py:374
  48.6 1.0 %collective-permute-done.10 = bf16[256,512]{1,0:T(8,128)(2,1)S(1)} collective-permute-done((bf16[256,512]{1,0:T(8,128)(2,1)S(1)}, bf16[256,512]{1,0:T(8,128)(2,1)S(1)}, u32[]{:S(2)}, u32[]{:S(2)}) %collective-permute-start.10) | collective-permute-done | bytes 262176 | tf_op jit(solution)/shard_map/reduce/ppermute | solution.py:425
  49.7 1.6 %collective-permute-start.11 = (bf16[256,512]{1,0:T(8,128)(2,1)S(1)}, bf16[256,512]{1,0:T(8,128)(2,1)S(1)}, u32[]{:S(2)}, u32[]{:S(2)}) collective-permute-start(bf16[256,512]{1,0:T(8,128)(2,1)S(1)} %add_convert_fusion), channel_id=1, source_target_pairs={{0,2},{1,3},{2,0},{3,1},{4,6},{5,7},{6,4},{7,5},{8,10},{9,11},{10,... | collective-permute-start | bytes 786440 | tf_op jit(solution)/shard_map/reduce/ppermute | solution.py:425
  51.5 1.4 %finish.2.refs_0_ = bf16[512,512]{1,0:T(8,128)(2,1)} custom-call(s32[18]{0:T(128)S(1)} %pad_add_fusion.plan_ref, bf16[512,512]{1,0:T(8,128)(2,1)S(1)} %broadcast_maximum_fusion.x0.tokens_ref, bf16[512,512]{1,0:T(8,128)(2,1)S(1)} %get-tuple-element.78.near_ref, bf16[512,512]{1,0:T(8,128)(2,1)S(1)} %collective-permute-done.7.got_ref, ...), custom_call_target="tpu_custom_call" | custom-call | flops 524288 | bytes 2359368 | tf_op jit(solution)/shard_map/finish/finish/pallas_call | solution.py:374
  52.9 3.4 %collective-permute-start.12 = (bf16[2,64,256]{2,1,0:T(8,128)(2,1)S(1)}, bf16[2,64,256]{2,1,0:T(8,128)(2,1)S(1)}, u32[]{:S(2)}, u32[]{:S(2)}) collective-permute-start(bf16[2,64,256]{2,1,0:T(8,128)(2,1)S(1)} %get-tuple-element.94), channel_id=1, source_target_pairs={{0,8},{4,12},{8,0},{12,4},{16,24},{20,28},{24,16},{28,20},{1,9},{5... | collective-permute-start | bytes 196616 | tf_op jit(solution)/shard_map/finish/ppermute | solution.py:425
  56.3 1.8 %collective-permute-done.11.crossed_ref = bf16[256,512]{1,0:T(8,128)(2,1)S(1)} collective-permute-done((bf16[256,512]{1,0:T(8,128)(2,1)S(1)}, bf16[256,512]{1,0:T(8,128)(2,1)S(1)}, u32[]{:S(2)}, u32[]{:S(2)}) %collective-permute-start.11) | collective-permute-done | bytes 262176 | tf_op jit(solution)/shard_map/reduce/ppermute | solution.py:425
  58.1 1.4 %finish.3 = bf16[512,512]{1,0:T(8,128)(2,1)} custom-call(s32[18]{0:T(128)S(1)} %pad_add_fusion.plan_ref, bf16[512,512]{1,0:T(8,128)(2,1)S(1)} %broadcast_maximum_fusion.x0.tokens_ref, bf16[512,512]{1,0:T(8,128)(2,1)S(1)} %get-tuple-element.78.near_ref, bf16[512,512]{1,0:T(8,128)(2,1)S(1)} %collective-permute-done.7.got_ref, ...), custom_call_target="tpu_custom_call", output_to_operand_aliasing={{}: (5, {})} | custom-call | flops 524288 | bytes 2883656 | tf_op jit(solution)/shard_map/finish/finish/pallas_call | solution.py:374
  59.5 0.8 %place.1 = bf16[8,64,256]{2,1,0:T(8,128)(2,1)} custom-call(bf16[2,64,256]{2,1,0:T(8,128)(2,1)S(1)} %collective-permute-done.14.p3, bf16[2,64,256]{2,1,0:T(8,128)(2,1)S(1)} %collective-permute-done.13.p2, bf16[2,64,256]{2,1,0:T(8,128)(2,1)S(1)} %collective-permute-done.12.p1, bf16[2,64,256]{2,1,0:T(8,128)(2,1)S(1)} %get-tuple-element.101.p0), custom_call_target="tpu_custom_call" | custom-call | bytes 524288 | tf_op jit(solution)/shard_map/finish/place/pallas_call | solution.py:374
  (24 shorter events, 3.0 us)
Async XLA Ops:
  0.6 15.2 %collective-permute-start = (bf16[512,512]{1,0:T(8,128)(2,1)}, bf16[512,512]{1,0:T(8,128)(2,1)S(1)}, u32[]{:S(2)}, u32[]{:S(2)}) collective-permute-start(bf16[512,512]{1,0:T(8,128)(2,1)} %param.10), channel_id=1, source_target_pairs={{0,2},{1,3},{2,0},{3,1},{4,6},{5,7},{6,4},{7,5},{8,10},{9,11},{10,... | collective-permute-start | bytes 1572872 | tf_op jit(solution)/shard_map/tokens_gather/ppermute | solution.py:425
  4.4 14.4 %all-to-all-start = ((bf16[8,64,256]{2,1,0:T(8,128)(2,1)}), bf16[8,64,256]{2,1,0:T(8,128)(2,1)S(1)}, u32[]{:S(2)}, u32[]{:S(2)}) async-start(bf16[8,64,256]{2,1,0:T(8,128)(2,1)} %param.19), calls=%async_computation | async-start | bytes 524288 | tf_op jit(solution)/shard_map/cache_gather/all_to_all | solution.py:428
  10.2 10.0 %collective-permute-start.1 = (bf16[512,512]{1,0:T(8,128)(2,1)}, bf16[512,512]{1,0:T(8,128)(2,1)S(1)}, u32[]{:S(2)}, u32[]{:S(2)}) collective-permute-start(bf16[512,512]{1,0:T(8,128)(2,1)} %param.10), channel_id=1, source_target_pairs={{0,1},{1,0},{2,3},{3,2},{4,5},{5,4},{6,7},{7,6},{8,9},{9,8},{10,11... | collective-permute-start | bytes 1572872 | tf_op jit(solution)/shard_map/tokens_gather/ppermute | solution.py:425
  18.8 1.9 %collective-permute-start.2 = (bf16[512,512]{1,0:T(8,128)(2,1)S(1)}, bf16[512,512]{1,0:T(8,128)(2,1)S(1)}, u32[]{:S(2)}, u32[]{:S(2)}) collective-permute-start(bf16[512,512]{1,0:T(8,128)(2,1)S(1)} %collective-permute-done.x2), channel_id=1, source_target_pairs={{0,1},{1,0},{2,3},{3,2},{4,5},{5,4},{6,7},{7,6},{8,9},{9,8},{10,11... | collective-permute-start | bytes 1572872 | tf_op jit(solution)/shard_map/project/ppermute | solution.py:425
  19.4 7.4 %collective-permute-start.4 = (bf16[384,256]{1,0:T(8,128)(2,1)S(1)}, bf16[384,256]{1,0:T(8,128)(2,1)S(1)}, u32[]{:S(2)}, u32[]{:S(2)}) collective-permute-start(bf16[384,256]{1,0:T(8,128)(2,1)S(1)} %order.1.refs_0_.refs_1_), channel_id=1, source_target_pairs={{0,2},{1,3},{2,0},{3,1},{4,6},{5,7},{6,4},{7,5},{8,10},{9,11},{10,... | collective-permute-start | bytes 589832 | tf_op jit(solution)/shard_map/cache_gather/ppermute | solution.py:425
  19.9 6.8 %collective-permute-start.3 = (bf16[384,256]{1,0:T(8,128)(2,1)S(1)}, bf16[384,256]{1,0:T(8,128)(2,1)S(1)}, u32[]{:S(2)}, u32[]{:S(2)}) collective-permute-start(bf16[384,256]{1,0:T(8,128)(2,1)S(1)} %order.1.refs_0_.refs_1_), channel_id=1, source_target_pairs={{0,1},{1,0},{2,3},{3,2},{4,5},{5,4},{6,7},{7,6},{8,9},{9,8},{10,11... | collective-permute-start | bytes 589832 | tf_op jit(solution)/shard_map/cache_gather/ppermute | solution.py:425
  26.8 1.4 %collective-permute-start.5 = (bf16[384,256]{1,0:T(8,128)(2,1)S(1)}, bf16[384,256]{1,0:T(8,128)(2,1)S(1)}, u32[]{:S(2)}, u32[]{:S(2)}) collective-permute-start(bf16[384,256]{1,0:T(8,128)(2,1)S(1)} %collective-permute-done.4.refs_2_.refs_3_), channel_id=1, source_target_pairs={{0,1},{1,0},{2,3},{3,2},{4,5},{5,4},{6,7},{7,6},{8,9},{9,8},{10,11... | collective-permute-start | bytes 589832 | tf_op jit(solution)/shard_map/extend/ppermute | solution.py:425
  35.0 1.6 %collective-permute-start.6 = (bf16[256,512]{1,0:T(8,128)(2,1)S(1)}, bf16[256,512]{1,0:T(8,128)(2,1)S(1)}, u32[]{:S(2)}, u32[]{:S(2)}) collective-permute-start(bf16[256,512]{1,0:T(8,128)(2,1)S(1)} %get-tuple-element.73), channel_id=1, source_target_pairs={{0,1},{1,0},{2,3},{3,2},{4,5},{5,4},{6,7},{7,6},{8,9},{9,8},{10,11... | collective-permute-start | bytes 786440 | tf_op jit(solution)/shard_map/reduce/ppermute | solution.py:425
  36.7 11.9 %collective-permute-start.8 = (bf16[256,512]{1,0:T(8,128)(2,1)S(1)}, bf16[256,512]{1,0:T(8,128)(2,1)S(1)}, u32[]{:S(2)}, u32[]{:S(2)}) collective-permute-start(bf16[256,512]{1,0:T(8,128)(2,1)S(1)} %add_convert_fusion.1), channel_id=1, source_target_pairs={{0,2},{1,3},{2,0},{3,1},{4,6},{5,7},{6,4},{7,5},{8,10},{9,11},{10,... | collective-permute-start | bytes 786440 | tf_op jit(solution)/shard_map/reduce/ppermute | solution.py:425
  37.3 10.7 %collective-permute-start.9 = (bf16[4,64,256]{2,1,0:T(8,128)(2,1)S(1)}, bf16[4,64,256]{2,1,0:T(8,128)(2,1)S(1)}, u32[]{:S(2)}, u32[]{:S(2)}) collective-permute-start(bf16[4,64,256]{2,1,0:T(8,128)(2,1)S(1)} %get-tuple-element.83), channel_id=1, source_target_pairs={{0,4},{4,0},{8,12},{12,8},{16,20},{20,16},{24,28},{28,24},{1,5},{5... | collective-permute-start | bytes 393224 | tf_op jit(solution)/shard_map/extend/ppermute | solution.py:425
  48.0 1.6 %collective-permute-start.10 = (bf16[256,512]{1,0:T(8,128)(2,1)S(1)}, bf16[256,512]{1,0:T(8,128)(2,1)S(1)}, u32[]{:S(2)}, u32[]{:S(2)}) collective-permute-start(bf16[256,512]{1,0:T(8,128)(2,1)S(1)} %get-tuple-element.84), channel_id=1, source_target_pairs={{0,1},{1,0},{2,3},{3,2},{4,5},{5,4},{6,7},{7,6},{8,9},{9,8},{10,11... | collective-permute-start | bytes 786440 | tf_op jit(solution)/shard_map/reduce/ppermute | solution.py:425
  48.1 3.4 %collective-permute-start.7 = (bf16[512,512]{1,0:T(8,128)(2,1)S(1)}, bf16[512,512]{1,0:T(8,128)(2,1)S(1)}, u32[]{:S(2)}, u32[]{:S(2)}) collective-permute-start(bf16[512,512]{1,0:T(8,128)(2,1)S(1)} %get-tuple-element.79), channel_id=1, source_target_pairs={{0,1},{1,0},{2,3},{3,2},{4,5},{5,4},{6,7},{7,6},{8,9},{9,8},{10,11... | collective-permute-start | bytes 1572872 | tf_op jit(solution)/shard_map/finish/ppermute | solution.py:425
  49.7 8.4 %collective-permute-start.11 = (bf16[256,512]{1,0:T(8,128)(2,1)S(1)}, bf16[256,512]{1,0:T(8,128)(2,1)S(1)}, u32[]{:S(2)}, u32[]{:S(2)}) collective-permute-start(bf16[256,512]{1,0:T(8,128)(2,1)S(1)} %add_convert_fusion), channel_id=1, source_target_pairs={{0,2},{1,3},{2,0},{3,1},{4,6},{5,7},{6,4},{7,5},{8,10},{9,11},{10,... | collective-permute-start | bytes 786440 | tf_op jit(solution)/shard_map/reduce/ppermute | solution.py:425
  51.3 8.2 %collective-permute-start.13 = (bf16[2,64,256]{2,1,0:T(8,128)(2,1)S(1)}, bf16[2,64,256]{2,1,0:T(8,128)(2,1)S(1)}, u32[]{:S(2)}, u32[]{:S(2)}) collective-permute-start(bf16[2,64,256]{2,1,0:T(8,128)(2,1)S(1)} %get-tuple-element.95), channel_id=1, source_target_pairs={{0,16},{4,20},{8,24},{12,28},{16,0},{20,4},{24,8},{28,12},{1,17},{... | collective-permute-start | bytes 196616 | tf_op jit(solution)/shard_map/exchange/ppermute | solution.py:425
  51.4 8.1 %collective-permute-start.14 = (bf16[2,64,256]{2,1,0:T(8,128)(2,1)S(1)}, bf16[2,64,256]{2,1,0:T(8,128)(2,1)S(1)}, u32[]{:S(2)}, u32[]{:S(2)}) collective-permute-start(bf16[2,64,256]{2,1,0:T(8,128)(2,1)S(1)} %get-tuple-element.96), channel_id=1, source_target_pairs={{0,24},{4,28},{8,16},{12,20},{16,8},{20,12},{24,0},{28,4},{1,25},{... | collective-permute-start | bytes 196616 | tf_op jit(solution)/shard_map/exchange/ppermute | solution.py:425
  52.9 6.6 %collective-permute-start.12 = (bf16[2,64,256]{2,1,0:T(8,128)(2,1)S(1)}, bf16[2,64,256]{2,1,0:T(8,128)(2,1)S(1)}, u32[]{:S(2)}, u32[]{:S(2)}) collective-permute-start(bf16[2,64,256]{2,1,0:T(8,128)(2,1)S(1)} %get-tuple-element.94), channel_id=1, source_target_pairs={{0,8},{4,12},{8,0},{12,4},{16,24},{20,28},{24,16},{28,20},{1,9},{5... | collective-permute-start | bytes 196616 | tf_op jit(solution)/shard_map/finish/ppermute | solution.py:425

commit v4 on v2

--- a/solution.py
+++ b/solution.py
@@ -584,13 +584,16 @@
                 mib=8,
                 name="pair",
             ))
-            for k in range(len(pairs) - 1, 0, -1):
+            for k in range(len(pairs) - 1, 1, -1):
                 pairs[k] = swap(pairs[k], 2 * k, "seq")
         else:
             new_cache = exchange(sent[0].reshape(groups, share, width))
 
     with jax.named_scope("finish"):
         got0 = swap(far0, 1)
+        if phased:
+            got0, pairs[1] = lax.optimization_barrier((got0, pairs[1]))
+            pairs[1] = swap(pairs[1], 2, "seq")
         mixed = None
         for at, over in ((0, before), (part, crossed)):
             mixed = call(

time: 59.6 us -> 60.5 us (1.015); the launches traced: 59.9 us -> 59.3 us
  starting transfers between devices: 24.2 us -> 17.6 us
  Pallas kernels: 18.3 us -> 22.1 us
  waiting for transfers between devices: 12.5 us -> 14.7 us
    ppermute x15, starting transfers between devices: 18.4 us -> 11.8 us  [swap(): return lax.ppermute(x, axis, [(i, i ^ bit) for i in range(size)])]
    pallas_call x10, Pallas kernels: 18.3 us -> 22.1 us  [call(): pl.pallas_call(kernel, out_shape=out_shape, in_specs=in_specs, out_specs=...]
    ppermute x15, waiting for transfers between devices: 10.2 us -> 12.5 us  [swap(): return lax.ppermute(x, axis, [(i, i ^ bit) for i in range(size)])]
  transfers between devices with their start and end apart: 16 -> 16, of which waited for: 9 -> 10; matrix products, arithmetic and copies ran while one was open for 4% -> 4% of each run, Pallas kernels for 21% -> 21%
where the time goes in v4:
time: 60.5 us; the launch traced here: 59.3 us
  Pallas kernels  22.1 us (37%)
  starting transfers between devices  17.6 us (29%)
  waiting for transfers between devices  14.7 us (24%)
  other arithmetic  2.67 us (4%)
  between operations  2.2 us (4%)
    pallas_call x10, Pallas kernels, call(): pl.pallas_call(kernel, out_shape=out_shape, in_specs=in_specs, out_specs=...  22.1 us
    ppermute x15, waiting for transfers between devices, swap(): return lax.ppermute(x, axis, [(i, i ^ bit) for i in range(size)])  12.5 us
    ppermute x15, starting transfers between devices, swap(): return lax.ppermute(x, axis, [(i, i ^ bit) for i in range(size)])  11.8 us
    all_to_all x1, starting transfers between devices, exchange(): return lax.all_to_all(x, 'seq', split_axis=0, concat_axis=0, tiled=True)  5.81 us
    all_to_all x1, waiting for transfers between devices, exchange(): return lax.all_to_all(x, 'seq', split_axis=0, concat_axis=0, tiled=True)  2.26 us
  transfers between devices with their start and end apart: 16, of which 10 were waited for; matrix products, arithmetic and copies ran while one was open for 4% of the time, Pallas kernels for 21%

profile of v4, /device:TPU:0, one launch (start us, length us, event | category | flops | bytes accessed | tf_op | source)
XLA Modules:
  0.0 59.3 jit_solution(8657059294848222876)
XLA Ops:
  0.6 3.0 %collective-permute-start = (bf16[512,512]{1,0:T(8,128)(2,1)}, bf16[512,512]{1,0:T(8,128)(2,1)S(1)}, u32[]{:S(2)}, u32[]{:S(2)}) collective-permute-start(bf16[512,512]{1,0:T(8,128)(2,1)} %param.10), channel_id=1, source_target_pairs={{0,2},{1,3},{2,0},{3,1},{4,6},{5,7},{6,4},{7,5},{8,10},{9,11},{10,... | collective-permute-start | bytes 1572872 | tf_op jit(solution)/shard_map/tokens_gather/ppermute | solution.py:425
  3.7 0.7 %broadcast_maximum_fusion.1 = f32[2048]{0:T(1024)S(1)} fusion(f32[2048]{0:T(1024)} %param.11), kind=kLoop, calls=%fused_computation.3 | loop fusion | flops 2048 | bytes 16384 | tf_op jit(solution)/shard_map/cache_gather/max | solution.py:437
  4.4 5.8 %all-to-all-start = ((bf16[8,64,256]{2,1,0:T(8,128)(2,1)}), bf16[8,64,256]{2,1,0:T(8,128)(2,1)S(1)}, u32[]{:S(2)}, u32[]{:S(2)}) async-start(bf16[8,64,256]{2,1,0:T(8,128)(2,1)} %param.19), calls=%async_computation | async-start | bytes 524288 | tf_op jit(solution)/shard_map/cache_gather/all_to_all | solution.py:428
  11.5 1.1 %broadcast_maximum_fusion.x0.tokens_ref = bf16[512,512]{1,0:T(8,128)(2,1)S(1)} fusion(bf16[512,512]{1,0:T(8,128)(2,1)} %param.10), kind=kLoop, calls=%fused_computation.2 | loop fusion | flops 262144 | bytes 1048576 | tf_op jit(solution)/shard_map/cache_gather/max | solution.py:440
  12.6 3.2 %collective-permute-done.x2 = bf16[512,512]{1,0:T(8,128)(2,1)S(1)} collective-permute-done((bf16[512,512]{1,0:T(8,128)(2,1)}, bf16[512,512]{1,0:T(8,128)(2,1)S(1)}, u32[]{:S(2)}, u32[]{:S(2)}) %collective-permute-start) | collective-permute-done | bytes 524320 | tf_op jit(solution)/shard_map/tokens_gather/ppermute | solution.py:425
  15.8 0.7 %pad_add_fusion.plan_ref = s32[18]{0:T(128)S(1)} fusion(s32[8]{0:T(128)} %bitcast.7, s32[8]{0:T(128)} %bitcast.8, s32[1]{0:T(128)S(6)} %copy.16, s32[1]{0:T(128)S(6)} %copy.17), kind=kLoop, calls=%fused_computation.4 | loop fusion | flops 54 | bytes 144 | tf_op jit(solution)/shard_map/cache_gather/concatenate | solution.py:444
  16.5 2.3 %all-to-all-done = bf16[8,64,256]{2,1,0:T(8,128)(2,1)S(1)} async-done(((bf16[8,64,256]{2,1,0:T(8,128)(2,1)}), bf16[8,64,256]{2,1,0:T(8,128)(2,1)S(1)}, u32[]{:S(2)}, u32[]{:S(2)}) %all-to-all-start) | async-done | bytes 262176 | tf_op jit(solution)/shard_map/cache_gather/all_to_all | solution.py:428
  20.7 4.1 %project.1 = (bf16[2048,128]{1,0:T(8,128)(2,1)S(1)}, bf16[512,256]{1,0:T(8,128)(2,1)S(1)}, bf16[512,256]{1,0:T(8,128)(2,1)S(1)}, f32[2,8,128]{2,1,0:T(8,128)S(1)}) custom-call(bf16[512,512]{1,0:T(8,128)(2,1)S(1)} %broadcast_maximum_fusion.x0.tokens_ref, bf16[512,512]{1,0:T(8,128)(2,1)S(1)} %collective-permute-done.1.x1, ...), custom_call_target="tpu_custom_call" | custom-call | flops 1610612736 | bytes 6307840 | tf_op jit(solution)/shard_map/project/project/pallas_call | solution.py:374
  24.8 1.2 %extend.1 = (bf16[4,64,256]{2,1,0:T(8,128)(2,1)S(1)}, bf16[4,64,256]{2,1,0:T(8,128)(2,1)S(1)}) custom-call(s32[18]{0:T(128)S(1)} %pad_add_fusion.plan_ref, bf16[512,256]{1,0:T(8,128)(2,1)S(1)} %get-tuple-element.63.kv_ref, bf16[512,256]{1,0:T(8,128)(2,1)S(1)} %bitcast.5), custom_call_target="tpu_custom_call" | custom-call | flops 268435456 | bytes 786504 | tf_op jit(solution)/shard_map/extend/extend/pallas_call | solution.py:374
  26.0 0.7 %collective-permute-done.4.refs_2_.refs_3_ = bf16[384,256]{1,0:T(8,128)(2,1)S(1)} collective-permute-done((bf16[384,256]{1,0:T(8,128)(2,1)S(1)}, bf16[384,256]{1,0:T(8,128)(2,1)S(1)}, u32[]{:S(2)}, u32[]{:S(2)}) %collective-permute-start.4) | collective-permute-done | bytes 196640 | tf_op jit(solution)/shard_map/cache_gather/ppermute | solution.py:425
  26.8 0.9 %early.1 = (bf16[1152,256]{1,0:T(8,128)(2,1)S(1)}, f32[8,128]{1,0:T(8,128)S(1)}) custom-call(s32[18]{0:T(128)S(1)} %pad_add_fusion.plan_ref, bf16[384,256]{1,0:T(8,128)(2,1)S(1)} %order.1.refs_0_.refs_1_, bf16[384,256]{1,0:T(8,128)(2,1)S(1)} %collective-permute-done.3.refs_1_.refs_2_, bf16[384,256]{1,0:T(8,128)(2,1)S(1)} %collective-permute-done.4.refs_2_.refs_3_), custom_call_target="tpu_custom_call" | custom-call | flops 1073741824 | bytes 1183816 | tf_op jit(solution)/shard_map/early/early/pallas_call | solution.py:374
  28.2 8.7 %attend.2 = (bf16[256,512]{1,0:T(8,128)(2,1)S(1)}, bf16[256,512]{1,0:T(8,128)(2,1)S(1)}, bf16[256,512]{1,0:T(8,128)(2,1)S(1)}, bf16[384,256]{1,0:T(8,128)(2,1)S(1)}, f32[8,128]{1,0:T(8,128)S(1)}) custom-call(s32[18]{0:T(128)S(1)} %pad_add_fusion.plan_ref, bf16[2048,128]{1,0:T(8,128)(2,1)S(1)} %get-tuple-element.74.q_ref, ...), custom_call_target="tpu_custom_call" | custom-call | flops 1476395008 | bytes 5521480 | tf_op jit(solution)/shard_map/attend/attend/pallas_call | solution.py:374
  37.1 1.4 %collective-permute-done.6 = bf16[256,512]{1,0:T(8,128)(2,1)S(1)} collective-permute-done((bf16[256,512]{1,0:T(8,128)(2,1)S(1)}, bf16[256,512]{1,0:T(8,128)(2,1)S(1)}, u32[]{:S(2)}, u32[]{:S(2)}) %collective-permute-start.6) | collective-permute-done | bytes 262176 | tf_op jit(solution)/shard_map/reduce/ppermute | solution.py:425
  38.6 0.6 collective-permute-start.8
  39.2 3.1 %attend.3 = (bf16[512,512]{1,0:T(8,128)(2,1)S(1)}, bf16[256,512]{1,0:T(8,128)(2,1)S(1)}, bf16[512,512]{1,0:T(8,128)(2,1)S(1)}, bf16[256,512]{1,0:T(8,128)(2,1)S(1)}) custom-call(s32[18]{0:T(128)S(1)} %pad_add_fusion.plan_ref, bf16[2048,128]{1,0:T(8,128)(2,1)S(1)} %get-tuple-element.74.q_ref, bf16[512,256]{1,0:T(8,128)(2,1)S(1)} %get-tuple-element.63.kv_ref, ...), custom_call_target="tpu_custom_call" | custom-call | flops 1610612736 | bytes 6570056 | tf_op jit(solution)/shard_map/attend/attend/pallas_call | solution.py:374
  42.3 2.1 %collective-permute-done.9.got_ref = bf16[4,64,256]{2,1,0:T(8,128)(2,1)S(1)} collective-permute-done((bf16[4,64,256]{2,1,0:T(8,128)(2,1)S(1)}, bf16[4,64,256]{2,1,0:T(8,128)(2,1)S(1)}, u32[]{:S(2)}, u32[]{:S(2)}) %collective-permute-start.9) | collective-permute-done | bytes 131104 | tf_op jit(solution)/shard_map/extend/ppermute | solution.py:425
  45.0 2.1 %collective-permute-done.8.in_ref = bf16[256,512]{1,0:T(8,128)(2,1)S(1)} collective-permute-done((bf16[256,512]{1,0:T(8,128)(2,1)S(1)}, bf16[256,512]{1,0:T(8,128)(2,1)S(1)}, u32[]{:S(2)}, u32[]{:S(2)}) %collective-permute-start.8) | collective-permute-done | bytes 262176 | tf_op jit(solution)/shard_map/reduce/ppermute | solution.py:425
  47.7 2.4 %collective-permute-start.13 = (bf16[2,64,256]{2,1,0:T(8,128)(2,1)S(1)}, bf16[2,64,256]{2,1,0:T(8,128)(2,1)S(1)}, u32[]{:S(2)}, u32[]{:S(2)}) collective-permute-start(bf16[2,64,256]{2,1,0:T(8,128)(2,1)S(1)} %get-tuple-element.95), channel_id=1, source_target_pairs={{0,16},{4,20},{8,24},{12,28},{16,0},{20,4},{24,8},{28,12},{1,17},{... | collective-permute-start | bytes 196616 | tf_op jit(solution)/shard_map/exchange/ppermute | solution.py:425
  50.1 3.7 %collective-permute-start.14 = (bf16[2,64,256]{2,1,0:T(8,128)(2,1)S(1)}, bf16[2,64,256]{2,1,0:T(8,128)(2,1)S(1)}, u32[]{:S(2)}, u32[]{:S(2)}) collective-permute-start(bf16[2,64,256]{2,1,0:T(8,128)(2,1)S(1)} %get-tuple-element.96), channel_id=1, source_target_pairs={{0,24},{4,28},{8,16},{12,20},{16,8},{20,12},{24,0},{28,4},{1,25},{... | collective-permute-start | bytes 196616 | tf_op jit(solution)/shard_map/exchange/ppermute | solution.py:425
  53.8 1.4 %finish.2.refs_0_ = bf16[512,512]{1,0:T(8,128)(2,1)} custom-call(s32[18]{0:T(128)S(1)} %pad_add_fusion.plan_ref, bf16[512,512]{1,0:T(8,128)(2,1)S(1)} %broadcast_maximum_fusion.x0.tokens_ref, bf16[512,512]{1,0:T(8,128)(2,1)S(1)} %get-tuple-element.78.near_ref, bf16[512,512]{1,0:T(8,128)(2,1)S(1)} %collective-permute-done.7.got_ref, ...), custom_call_target="tpu_custom_call" | custom-call | flops 524288 | bytes 2359368 | tf_op jit(solution)/shard_map/finish/finish/pallas_call | solution.py:374
  55.2 1.4 %finish.3 = bf16[512,512]{1,0:T(8,128)(2,1)} custom-call(s32[18]{0:T(128)S(1)} %pad_add_fusion.plan_ref, bf16[512,512]{1,0:T(8,128)(2,1)S(1)} %broadcast_maximum_fusion.x0.tokens_ref, bf16[512,512]{1,0:T(8,128)(2,1)S(1)} %get-tuple-element.78.near_ref, bf16[512,512]{1,0:T(8,128)(2,1)S(1)} %collective-permute-done.7.got_ref, ...), custom_call_target="tpu_custom_call", output_to_operand_aliasing={{}: (5, {})} | custom-call | flops 524288 | bytes 2883656 | tf_op jit(solution)/shard_map/finish/finish/pallas_call | solution.py:374
  56.6 1.2 %collective-permute-done.14.p3 = bf16[2,64,256]{2,1,0:T(8,128)(2,1)S(1)} collective-permute-done((bf16[2,64,256]{2,1,0:T(8,128)(2,1)S(1)}, bf16[2,64,256]{2,1,0:T(8,128)(2,1)S(1)}, u32[]{:S(2)}, u32[]{:S(2)}) %collective-permute-start.14) | collective-permute-done | bytes 65568 | tf_op jit(solution)/shard_map/exchange/ppermute | solution.py:425
  57.7 0.7 %collective-permute-done.12.p1 = bf16[2,64,256]{2,1,0:T(8,128)(2,1)S(1)} collective-permute-done((bf16[2,64,256]{2,1,0:T(8,128)(2,1)S(1)}, bf16[2,64,256]{2,1,0:T(8,128)(2,1)S(1)}, u32[]{:S(2)}, u32[]{:S(2)}) %collective-permute-start.12) | collective-permute-done | bytes 65568 | tf_op jit(solution)/shard_map/finish/ppermute | solution.py:425
  58.4 0.8 %place.1 = bf16[8,64,256]{2,1,0:T(8,128)(2,1)} custom-call(bf16[2,64,256]{2,1,0:T(8,128)(2,1)S(1)} %get-tuple-element.98.p0, bf16[2,64,256]{2,1,0:T(8,128)(2,1)S(1)} %collective-permute-done.12.p1, bf16[2,64,256]{2,1,0:T(8,128)(2,1)S(1)} %collective-permute-done.13.p2, bf16[2,64,256]{2,1,0:T(8,128)(2,1)S(1)} %collective-permute-done.14.p3), custom_call_target="tpu_custom_call" | custom-call | bytes 524288 | tf_op jit(solution)/shard_map/finish/place/pallas_call | solution.py:374
  (24 shorter events, 3.9 us)
Async XLA Ops:
  0.6 15.2 %collective-permute-start = (bf16[512,512]{1,0:T(8,128)(2,1)}, bf16[512,512]{1,0:T(8,128)(2,1)S(1)}, u32[]{:S(2)}, u32[]{:S(2)}) collective-permute-start(bf16[512,512]{1,0:T(8,128)(2,1)} %param.10), channel_id=1, source_target_pairs={{0,2},{1,3},{2,0},{3,1},{4,6},{5,7},{6,4},{7,5},{8,10},{9,11},{10,... | collective-permute-start | bytes 1572872 | tf_op jit(solution)/shard_map/tokens_gather/ppermute | solution.py:425
  4.4 14.4 %all-to-all-start = ((bf16[8,64,256]{2,1,0:T(8,128)(2,1)}), bf16[8,64,256]{2,1,0:T(8,128)(2,1)S(1)}, u32[]{:S(2)}, u32[]{:S(2)}) async-start(bf16[8,64,256]{2,1,0:T(8,128)(2,1)} %param.19), calls=%async_computation | async-start | bytes 524288 | tf_op jit(solution)/shard_map/cache_gather/all_to_all | solution.py:428
  10.2 10.0 %collective-permute-start.1 = (bf16[512,512]{1,0:T(8,128)(2,1)}, bf16[512,512]{1,0:T(8,128)(2,1)S(1)}, u32[]{:S(2)}, u32[]{:S(2)}) collective-permute-start(bf16[512,512]{1,0:T(8,128)(2,1)} %param.10), channel_id=1, source_target_pairs={{0,1},{1,0},{2,3},{3,2},{4,5},{5,4},{6,7},{7,6},{8,9},{9,8},{10,11... | collective-permute-start | bytes 1572872 | tf_op jit(solution)/shard_map/tokens_gather/ppermute | solution.py:425
  18.8 1.9 %collective-permute-start.2 = (bf16[512,512]{1,0:T(8,128)(2,1)S(1)}, bf16[512,512]{1,0:T(8,128)(2,1)S(1)}, u32[]{:S(2)}, u32[]{:S(2)}) collective-permute-start(bf16[512,512]{1,0:T(8,128)(2,1)S(1)} %collective-permute-done.x2), channel_id=1, source_target_pairs={{0,1},{1,0},{2,3},{3,2},{4,5},{5,4},{6,7},{7,6},{8,9},{9,8},{10,11... | collective-permute-start | bytes 1572872 | tf_op jit(solution)/shard_map/project/ppermute | solution.py:425
  19.4 7.4 %collective-permute-start.4 = (bf16[384,256]{1,0:T(8,128)(2,1)S(1)}, bf16[384,256]{1,0:T(8,128)(2,1)S(1)}, u32[]{:S(2)}, u32[]{:S(2)}) collective-permute-start(bf16[384,256]{1,0:T(8,128)(2,1)S(1)} %order.1.refs_0_.refs_1_), channel_id=1, source_target_pairs={{0,2},{1,3},{2,0},{3,1},{4,6},{5,7},{6,4},{7,5},{8,10},{9,11},{10,... | collective-permute-start | bytes 589832 | tf_op jit(solution)/shard_map/cache_gather/ppermute | solution.py:425
  19.9 6.8 %collective-permute-start.3 = (bf16[384,256]{1,0:T(8,128)(2,1)S(1)}, bf16[384,256]{1,0:T(8,128)(2,1)S(1)}, u32[]{:S(2)}, u32[]{:S(2)}) collective-permute-start(bf16[384,256]{1,0:T(8,128)(2,1)S(1)} %order.1.refs_0_.refs_1_), channel_id=1, source_target_pairs={{0,1},{1,0},{2,3},{3,2},{4,5},{5,4},{6,7},{7,6},{8,9},{9,8},{10,11... | collective-permute-start | bytes 589832 | tf_op jit(solution)/shard_map/cache_gather/ppermute | solution.py:425
  26.8 1.4 %collective-permute-start.5 = (bf16[384,256]{1,0:T(8,128)(2,1)S(1)}, bf16[384,256]{1,0:T(8,128)(2,1)S(1)}, u32[]{:S(2)}, u32[]{:S(2)}) collective-permute-start(bf16[384,256]{1,0:T(8,128)(2,1)S(1)} %collective-permute-done.4.refs_2_.refs_3_), channel_id=1, source_target_pairs={{0,1},{1,0},{2,3},{3,2},{4,5},{5,4},{6,7},{7,6},{8,9},{9,8},{10,11... | collective-permute-start | bytes 589832 | tf_op jit(solution)/shard_map/extend/ppermute | solution.py:425
  36.9 1.6 %collective-permute-start.6 = (bf16[256,512]{1,0:T(8,128)(2,1)S(1)}, bf16[256,512]{1,0:T(8,128)(2,1)S(1)}, u32[]{:S(2)}, u32[]{:S(2)}) collective-permute-start(bf16[256,512]{1,0:T(8,128)(2,1)S(1)} %get-tuple-element.73), channel_id=1, source_target_pairs={{0,1},{1,0},{2,3},{3,2},{4,5},{5,4},{6,7},{7,6},{8,9},{9,8},{10,11... | collective-permute-start | bytes 786440 | tf_op jit(solution)/shard_map/reduce/ppermute | solution.py:425
  38.6 8.4 %collective-permute-start.8 = (bf16[256,512]{1,0:T(8,128)(2,1)S(1)}, bf16[256,512]{1,0:T(8,128)(2,1)S(1)}, u32[]{:S(2)}, u32[]{:S(2)}) collective-permute-start(bf16[256,512]{1,0:T(8,128)(2,1)S(1)} %add_convert_fusion.1), channel_id=1, source_target_pairs={{0,2},{1,3},{2,0},{3,1},{4,6},{5,7},{6,4},{7,5},{8,10},{9,11},{10,... | collective-permute-start | bytes 786440 | tf_op jit(solution)/shard_map/reduce/ppermute | solution.py:425
  39.2 5.3 %collective-permute-start.9 = (bf16[4,64,256]{2,1,0:T(8,128)(2,1)S(1)}, bf16[4,64,256]{2,1,0:T(8,128)(2,1)S(1)}, u32[]{:S(2)}, u32[]{:S(2)}) collective-permute-start(bf16[4,64,256]{2,1,0:T(8,128)(2,1)S(1)} %get-tuple-element.84), channel_id=1, source_target_pairs={{0,4},{4,0},{8,12},{12,8},{16,20},{20,16},{24,28},{28,24},{1,5},{5... | collective-permute-start | bytes 393224 | tf_op jit(solution)/shard_map/extend/ppermute | solution.py:425
  44.4 2.6 %collective-permute-start.10 = (bf16[256,512]{1,0:T(8,128)(2,1)S(1)}, bf16[256,512]{1,0:T(8,128)(2,1)S(1)}, u32[]{:S(2)}, u32[]{:S(2)}) collective-permute-start(bf16[256,512]{1,0:T(8,128)(2,1)S(1)} %get-tuple-element.85), channel_id=1, source_target_pairs={{0,1},{1,0},{2,3},{3,2},{4,5},{5,4},{6,7},{7,6},{8,9},{9,8},{10,11... | collective-permute-start | bytes 786440 | tf_op jit(solution)/shard_map/reduce/ppermute | solution.py:425
  44.4 9.3 %collective-permute-start.7 = (bf16[512,512]{1,0:T(8,128)(2,1)S(1)}, bf16[512,512]{1,0:T(8,128)(2,1)S(1)}, u32[]{:S(2)}, u32[]{:S(2)}) collective-permute-start(bf16[512,512]{1,0:T(8,128)(2,1)S(1)} %get-tuple-element.79), channel_id=1, source_target_pairs={{0,1},{1,0},{2,3},{3,2},{4,5},{5,4},{6,7},{7,6},{8,9},{9,8},{10,11... | collective-permute-start | bytes 1572872 | tf_op jit(solution)/shard_map/finish/ppermute | solution.py:425
  47.1 8.1 %collective-permute-start.11 = (bf16[256,512]{1,0:T(8,128)(2,1)S(1)}, bf16[256,512]{1,0:T(8,128)(2,1)S(1)}, u32[]{:S(2)}, u32[]{:S(2)}) collective-permute-start(bf16[256,512]{1,0:T(8,128)(2,1)S(1)} %add_convert_fusion), channel_id=1, source_target_pairs={{0,2},{1,3},{2,0},{3,1},{4,6},{5,7},{6,4},{7,5},{8,10},{9,11},{10,... | collective-permute-start | bytes 786440 | tf_op jit(solution)/shard_map/reduce/ppermute | solution.py:425
  47.7 8.9 %collective-permute-start.13 = (bf16[2,64,256]{2,1,0:T(8,128)(2,1)S(1)}, bf16[2,64,256]{2,1,0:T(8,128)(2,1)S(1)}, u32[]{:S(2)}, u32[]{:S(2)}) collective-permute-start(bf16[2,64,256]{2,1,0:T(8,128)(2,1)S(1)} %get-tuple-element.95), channel_id=1, source_target_pairs={{0,16},{4,20},{8,24},{12,28},{16,0},{20,4},{24,8},{28,12},{1,17},{... | collective-permute-start | bytes 196616 | tf_op jit(solution)/shard_map/exchange/ppermute | solution.py:425
  50.1 7.6 %collective-permute-start.14 = (bf16[2,64,256]{2,1,0:T(8,128)(2,1)S(1)}, bf16[2,64,256]{2,1,0:T(8,128)(2,1)S(1)}, u32[]{:S(2)}, u32[]{:S(2)}) collective-permute-start(bf16[2,64,256]{2,1,0:T(8,128)(2,1)S(1)} %get-tuple-element.96), channel_id=1, source_target_pairs={{0,24},{4,28},{8,16},{12,20},{16,8},{20,12},{24,0},{28,4},{1,25},{... | collective-permute-start | bytes 196616 | tf_op jit(solution)/shard_map/exchange/ppermute | solution.py:425
  53.8 4.6 %collective-permute-start.12 = (bf16[2,64,256]{2,1,0:T(8,128)(2,1)S(1)}, bf16[2,64,256]{2,1,0:T(8,128)(2,1)S(1)}, u32[]{:S(2)}, u32[]{:S(2)}) collective-permute-start(bf16[2,64,256]{2,1,0:T(8,128)(2,1)S(1)} %get-tuple-element.94), channel_id=1, source_target_pairs={{0,8},{4,12},{8,0},{12,4},{16,24},{20,28},{24,16},{28,20},{1,9},{5... | collective-permute-start | bytes 196616 | tf_op jit(solution)/shard_map/finish/ppermute | solution.py:425

commit v5 on v4

--- a/solution.py
+++ b/solution.py
@@ -268,11 +268,13 @@
             ]
 
     def fast(used, begin):
-        row_tiles = range(begin // ROW_TILE, min(begin + PART_ROWS, rows) // ROW_TILE)
-        steps = [(t, i) for t in row_tiles for i in range(used + 1)]
+        first = begin // ROW_TILE
+        tiles_of = range(first, min(begin + PART_ROWS, rows) // ROW_TILE)
+        at_all = pl.ds((start_row + begin) * heads, len(tiles_of) * tile_rows)
+        steps = [(None, i) for i in range(used)] + [(t, used) for t in tiles_of]
 
         def score(t, i):
-            return new_scores(t) if i == used else dot_t(queries(t), old_keys(i))
+            return new_scores(t) if i == used else dot_t(q_ref[at_all, :], old_keys(i))
 
         ahead, both = score(*steps[0]), None
         for at, (t, i) in enumerate(steps):
@@ -280,11 +282,12 @@
             if at + 1 < len(steps):
                 ahead = score(*steps[at + 1])
             weights = jnp.exp2(scores * factor).astype(BF16)
-            values = new_values(t) if i == used else old_values(i)
-            part = dot(weights, values)
-            both = part if i == 0 else both + part
-            if i == used:
-                put(t, both)
+            if i < used:
+                part = dot(weights, old_values(i))
+                both = part if i == 0 else both + part
+            else:
+                here = (t - first) * tile_rows
+                put(t, both[here : here + tile_rows] + dot(weights, new_values(t)))
 
     def exact(t):
         column = lax.broadcasted_iota(jnp.int32, (tile_rows, group), 1)

time: 60.5 us -> 61 us (level); the launches traced: 59.3 us -> 60.9 us
  Pallas kernels: 22.1 us -> 28.3 us
  waiting for transfers between devices: 14.7 us -> 11.6 us
  starting transfers between devices: 17.6 us -> 16.1 us
    pallas_call x10, Pallas kernels: 22.1 us -> 28.3 us  [call(): pl.pallas_call(kernel, out_shape=out_shape, in_specs=in_specs, out_specs=...]
    ppermute x15, waiting for transfers between devices: 12.5 us -> 9.33 us  [swap(): return lax.ppermute(x, axis, [(i, i ^ bit) for i in range(size)])]
    ppermute x15, starting transfers between devices: 11.8 us -> 10.3 us  [swap(): return lax.ppermute(x, axis, [(i, i ^ bit) for i in range(size)])]
  transfers between devices with their start and end apart: 16 -> 16, of which waited for: 10 -> 8; matrix products, arithmetic and copies ran while one was open for 4% -> 4% of each run, Pallas kernels for 21% -> 31%
where the time goes in v5:
time: 61 us; the launch traced here: 60.9 us
  Pallas kernels  28.3 us (46%)
  starting transfers between devices  16.1 us (26%)
  waiting for transfers between devices  11.6 us (19%)
  other arithmetic  2.67 us (4%)
  between operations  2.24 us (4%)
    pallas_call x10, Pallas kernels, call(): pl.pallas_call(kernel, out_shape=out_shape, in_specs=in_specs, out_specs=...  28.3 us
    ppermute x15, starting transfers between devices, swap(): return lax.ppermute(x, axis, [(i, i ^ bit) for i in range(size)])  10.3 us
    ppermute x15, waiting for transfers between devices, swap(): return lax.ppermute(x, axis, [(i, i ^ bit) for i in range(size)])  9.33 us
    all_to_all x1, starting transfers between devices, exchange(): return lax.all_to_all(x, 'seq', split_axis=0, concat_axis=0, tiled=True)  5.81 us
    all_to_all x1, waiting for transfers between devices, exchange(): return lax.all_to_all(x, 'seq', split_axis=0, concat_axis=0, tiled=True)  2.26 us
  transfers between devices with their start and end apart: 16, of which 8 were waited for; matrix products, arithmetic and copies ran while one was open for 4% of the time, Pallas kernels for 31%

profile of v5, /device:TPU:0, one launch (start us, length us, event | category | flops | bytes accessed | tf_op | source)
XLA Modules:
  0.0 60.9 jit_solution(12353748025500867383)
XLA Ops:
  0.6 3.0 %collective-permute-start = (bf16[512,512]{1,0:T(8,128)(2,1)}, bf16[512,512]{1,0:T(8,128)(2,1)S(1)}, u32[]{:S(2)}, u32[]{:S(2)}) collective-permute-start(bf16[512,512]{1,0:T(8,128)(2,1)} %param.10), channel_id=1, source_target_pairs={{0,2},{1,3},{2,0},{3,1},{4,6},{5,7},{6,4},{7,5},{8,10},{9,11},{10,... | collective-permute-start | bytes 1572872 | tf_op jit(solution)/shard_map/tokens_gather/ppermute | solution.py:428
  3.7 0.7 %broadcast_maximum_fusion.1 = f32[2048]{0:T(1024)S(1)} fusion(f32[2048]{0:T(1024)} %param.11), kind=kLoop, calls=%fused_computation.3 | loop fusion | flops 2048 | bytes 16384 | tf_op jit(solution)/shard_map/cache_gather/max | solution.py:440
  4.4 5.8 %all-to-all-start = ((bf16[8,64,256]{2,1,0:T(8,128)(2,1)}), bf16[8,64,256]{2,1,0:T(8,128)(2,1)S(1)}, u32[]{:S(2)}, u32[]{:S(2)}) async-start(bf16[8,64,256]{2,1,0:T(8,128)(2,1)} %param.19), calls=%async_computation | async-start | bytes 524288 | tf_op jit(solution)/shard_map/cache_gather/all_to_all | solution.py:431
  11.5 1.1 %broadcast_maximum_fusion.x0.tokens_ref = bf16[512,512]{1,0:T(8,128)(2,1)S(1)} fusion(bf16[512,512]{1,0:T(8,128)(2,1)} %param.10), kind=kLoop, calls=%fused_computation.2 | loop fusion | flops 262144 | bytes 1048576 | tf_op jit(solution)/shard_map/cache_gather/max | solution.py:443
  12.6 3.2 %collective-permute-done.x2 = bf16[512,512]{1,0:T(8,128)(2,1)S(1)} collective-permute-done((bf16[512,512]{1,0:T(8,128)(2,1)}, bf16[512,512]{1,0:T(8,128)(2,1)S(1)}, u32[]{:S(2)}, u32[]{:S(2)}) %collective-permute-start) | collective-permute-done | bytes 524320 | tf_op jit(solution)/shard_map/tokens_gather/ppermute | solution.py:428
  15.8 0.7 %pad_add_fusion.plan_ref = s32[18]{0:T(128)S(1)} fusion(s32[8]{0:T(128)} %bitcast.7, s32[8]{0:T(128)} %bitcast.8, s32[1]{0:T(128)S(6)} %copy.16, s32[1]{0:T(128)S(6)} %copy.17), kind=kLoop, calls=%fused_computation.4 | loop fusion | flops 54 | bytes 144 | tf_op jit(solution)/shard_map/cache_gather/concatenate | solution.py:447
  16.5 2.3 %all-to-all-done = bf16[8,64,256]{2,1,0:T(8,128)(2,1)S(1)} async-done(((bf16[8,64,256]{2,1,0:T(8,128)(2,1)}), bf16[8,64,256]{2,1,0:T(8,128)(2,1)S(1)}, u32[]{:S(2)}, u32[]{:S(2)}) %all-to-all-start) | async-done | bytes 262176 | tf_op jit(solution)/shard_map/cache_gather/all_to_all | solution.py:431
  18.8 0.6 order.1.refs_0_.refs_1_
  19.4 0.6 collective-permute-start.4
  20.7 4.1 %project.1 = (bf16[2048,128]{1,0:T(8,128)(2,1)S(1)}, bf16[512,256]{1,0:T(8,128)(2,1)S(1)}, bf16[512,256]{1,0:T(8,128)(2,1)S(1)}, f32[2,8,128]{2,1,0:T(8,128)S(1)}) custom-call(bf16[512,512]{1,0:T(8,128)(2,1)S(1)} %broadcast_maximum_fusion.x0.tokens_ref, bf16[512,512]{1,0:T(8,128)(2,1)S(1)} %collective-permute-done.1.x1, ...), custom_call_target="tpu_custom_call" | custom-call | flops 1610612736 | bytes 6307840 | tf_op jit(solution)/shard_map/project/project/pallas_call | solution.py:377
  24.8 1.2 %extend.1 = (bf16[4,64,256]{2,1,0:T(8,128)(2,1)S(1)}, bf16[4,64,256]{2,1,0:T(8,128)(2,1)S(1)}) custom-call(s32[18]{0:T(128)S(1)} %pad_add_fusion.plan_ref, bf16[512,256]{1,0:T(8,128)(2,1)S(1)} %get-tuple-element.63.kv_ref, bf16[512,256]{1,0:T(8,128)(2,1)S(1)} %bitcast.5), custom_call_target="tpu_custom_call" | custom-call | flops 268435456 | bytes 786504 | tf_op jit(solution)/shard_map/extend/extend/pallas_call | solution.py:377
  26.0 0.7 %collective-permute-done.4.refs_2_.refs_3_ = bf16[384,256]{1,0:T(8,128)(2,1)S(1)} collective-permute-done((bf16[384,256]{1,0:T(8,128)(2,1)S(1)}, bf16[384,256]{1,0:T(8,128)(2,1)S(1)}, u32[]{:S(2)}, u32[]{:S(2)}) %collective-permute-start.4) | collective-permute-done | bytes 196640 | tf_op jit(solution)/shard_map/cache_gather/ppermute | solution.py:428
  26.8 0.9 %early.1 = (bf16[1152,256]{1,0:T(8,128)(2,1)S(1)}, f32[8,128]{1,0:T(8,128)S(1)}) custom-call(s32[18]{0:T(128)S(1)} %pad_add_fusion.plan_ref, bf16[384,256]{1,0:T(8,128)(2,1)S(1)} %order.1.refs_0_.refs_1_, bf16[384,256]{1,0:T(8,128)(2,1)S(1)} %collective-permute-done.3.refs_1_.refs_2_, bf16[384,256]{1,0:T(8,128)(2,1)S(1)} %collective-permute-done.4.refs_2_.refs_3_), custom_call_target="tpu_custom_call" | custom-call | flops 1073741824 | bytes 1183816 | tf_op jit(solution)/shard_map/early/early/pallas_call | solution.py:377
  28.2 8.7 %attend.2 = (bf16[256,512]{1,0:T(8,128)(2,1)S(1)}, bf16[256,512]{1,0:T(8,128)(2,1)S(1)}, bf16[256,512]{1,0:T(8,128)(2,1)S(1)}, bf16[384,256]{1,0:T(8,128)(2,1)S(1)}, f32[8,128]{1,0:T(8,128)S(1)}) custom-call(s32[18]{0:T(128)S(1)} %pad_add_fusion.plan_ref, bf16[2048,128]{1,0:T(8,128)(2,1)S(1)} %get-tuple-element.74.q_ref, ...), custom_call_target="tpu_custom_call" | custom-call | flops 1476395008 | bytes 5521480 | tf_op jit(solution)/shard_map/attend/attend/pallas_call | solution.py:377
  37.1 1.4 %collective-permute-done.6 = bf16[256,512]{1,0:T(8,128)(2,1)S(1)} collective-permute-done((bf16[256,512]{1,0:T(8,128)(2,1)S(1)}, bf16[256,512]{1,0:T(8,128)(2,1)S(1)}, u32[]{:S(2)}, u32[]{:S(2)}) %collective-permute-start.6) | collective-permute-done | bytes 262176 | tf_op jit(solution)/shard_map/reduce/ppermute | solution.py:428
  38.6 0.6 collective-permute-start.8
  39.2 9.3 %attend.3 = (bf16[512,512]{1,0:T(8,128)(2,1)S(1)}, bf16[256,512]{1,0:T(8,128)(2,1)S(1)}, bf16[512,512]{1,0:T(8,128)(2,1)S(1)}, bf16[256,512]{1,0:T(8,128)(2,1)S(1)}) custom-call(s32[18]{0:T(128)S(1)} %pad_add_fusion.plan_ref, bf16[2048,128]{1,0:T(8,128)(2,1)S(1)} %get-tuple-element.74.q_ref, bf16[512,256]{1,0:T(8,128)(2,1)S(1)} %get-tuple-element.63.kv_ref, ...), custom_call_target="tpu_custom_call" | custom-call | flops 1610612736 | bytes 6570056 | tf_op jit(solution)/shard_map/attend/attend/pallas_call | solution.py:377
  49.0 1.0 %collective-permute-done.10 = bf16[256,512]{1,0:T(8,128)(2,1)S(1)} collective-permute-done((bf16[256,512]{1,0:T(8,128)(2,1)S(1)}, bf16[256,512]{1,0:T(8,128)(2,1)S(1)}, u32[]{:S(2)}, u32[]{:S(2)}) %collective-permute-start.10) | collective-permute-done | bytes 262176 | tf_op jit(solution)/shard_map/reduce/ppermute | solution.py:428
  50.1 1.6 %collective-permute-start.11 = (bf16[256,512]{1,0:T(8,128)(2,1)S(1)}, bf16[256,512]{1,0:T(8,128)(2,1)S(1)}, u32[]{:S(2)}, u32[]{:S(2)}) collective-permute-start(bf16[256,512]{1,0:T(8,128)(2,1)S(1)} %add_convert_fusion), channel_id=1, source_target_pairs={{0,2},{1,3},{2,0},{3,1},{4,6},{5,7},{6,4},{7,5},{8,10},{9,11},{10,... | collective-permute-start | bytes 786440 | tf_op jit(solution)/shard_map/reduce/ppermute | solution.py:428
  51.9 3.4 %collective-permute-start.12 = (bf16[2,64,256]{2,1,0:T(8,128)(2,1)S(1)}, bf16[2,64,256]{2,1,0:T(8,128)(2,1)S(1)}, u32[]{:S(2)}, u32[]{:S(2)}) collective-permute-start(bf16[2,64,256]{2,1,0:T(8,128)(2,1)S(1)} %get-tuple-element.94), channel_id=1, source_target_pairs={{0,8},{4,12},{8,0},{12,4},{16,24},{20,28},{24,16},{28,20},{1,9},{5... | collective-permute-start | bytes 196616 | tf_op jit(solution)/shard_map/finish/ppermute | solution.py:428
  55.3 1.4 %finish.2.refs_0_ = bf16[512,512]{1,0:T(8,128)(2,1)} custom-call(s32[18]{0:T(128)S(1)} %pad_add_fusion.plan_ref, bf16[512,512]{1,0:T(8,128)(2,1)S(1)} %broadcast_maximum_fusion.x0.tokens_ref, bf16[512,512]{1,0:T(8,128)(2,1)S(1)} %get-tuple-element.78.near_ref, bf16[512,512]{1,0:T(8,128)(2,1)S(1)} %collective-permute-done.7.got_ref, ...), custom_call_target="tpu_custom_call" | custom-call | flops 524288 | bytes 2359368 | tf_op jit(solution)/shard_map/finish/finish/pallas_call | solution.py:377
  56.7 1.9 %collective-permute-done.11.crossed_ref = bf16[256,512]{1,0:T(8,128)(2,1)S(1)} collective-permute-done((bf16[256,512]{1,0:T(8,128)(2,1)S(1)}, bf16[256,512]{1,0:T(8,128)(2,1)S(1)}, u32[]{:S(2)}, u32[]{:S(2)}) %collective-permute-start.11) | collective-permute-done | bytes 262176 | tf_op jit(solution)/shard_map/reduce/ppermute | solution.py:428
  58.5 1.4 %finish.3 = bf16[512,512]{1,0:T(8,128)(2,1)} custom-call(s32[18]{0:T(128)S(1)} %pad_add_fusion.plan_ref, bf16[512,512]{1,0:T(8,128)(2,1)S(1)} %broadcast_maximum_fusion.x0.tokens_ref, bf16[512,512]{1,0:T(8,128)(2,1)S(1)} %get-tuple-element.78.near_ref, bf16[512,512]{1,0:T(8,128)(2,1)S(1)} %collective-permute-done.7.got_ref, ...), custom_call_target="tpu_custom_call", output_to_operand_aliasing={{}: (5, {})} | custom-call | flops 524288 | bytes 2883656 | tf_op jit(solution)/shard_map/finish/finish/pallas_call | solution.py:377
  60.0 0.8 %place.1 = bf16[8,64,256]{2,1,0:T(8,128)(2,1)} custom-call(bf16[2,64,256]{2,1,0:T(8,128)(2,1)S(1)} %get-tuple-element.98.p0, bf16[2,64,256]{2,1,0:T(8,128)(2,1)S(1)} %collective-permute-done.12.p1, bf16[2,64,256]{2,1,0:T(8,128)(2,1)S(1)} %collective-permute-done.13.p2, bf16[2,64,256]{2,1,0:T(8,128)(2,1)S(1)} %collective-permute-done.14.p3), custom_call_target="tpu_custom_call" | custom-call | bytes 524288 | tf_op jit(solution)/shard_map/finish/place/pallas_call | solution.py:377
  (24 shorter events, 2.4 us)
Async XLA Ops:
  0.6 15.2 %collective-permute-start = (bf16[512,512]{1,0:T(8,128)(2,1)}, bf16[512,512]{1,0:T(8,128)(2,1)S(1)}, u32[]{:S(2)}, u32[]{:S(2)}) collective-permute-start(bf16[512,512]{1,0:T(8,128)(2,1)} %param.10), channel_id=1, source_target_pairs={{0,2},{1,3},{2,0},{3,1},{4,6},{5,7},{6,4},{7,5},{8,10},{9,11},{10,... | collective-permute-start | bytes 1572872 | tf_op jit(solution)/shard_map/tokens_gather/ppermute | solution.py:428
  4.4 14.4 %all-to-all-start = ((bf16[8,64,256]{2,1,0:T(8,128)(2,1)}), bf16[8,64,256]{2,1,0:T(8,128)(2,1)S(1)}, u32[]{:S(2)}, u32[]{:S(2)}) async-start(bf16[8,64,256]{2,1,0:T(8,128)(2,1)} %param.19), calls=%async_computation | async-start | bytes 524288 | tf_op jit(solution)/shard_map/cache_gather/all_to_all | solution.py:431
  10.2 10.0 %collective-permute-start.1 = (bf16[512,512]{1,0:T(8,128)(2,1)}, bf16[512,512]{1,0:T(8,128)(2,1)S(1)}, u32[]{:S(2)}, u32[]{:S(2)}) collective-permute-start(bf16[512,512]{1,0:T(8,128)(2,1)} %param.10), channel_id=1, source_target_pairs={{0,1},{1,0},{2,3},{3,2},{4,5},{5,4},{6,7},{7,6},{8,9},{9,8},{10,11... | collective-permute-start | bytes 1572872 | tf_op jit(solution)/shard_map/tokens_gather/ppermute | solution.py:428
  18.8 1.9 %collective-permute-start.2 = (bf16[512,512]{1,0:T(8,128)(2,1)S(1)}, bf16[512,512]{1,0:T(8,128)(2,1)S(1)}, u32[]{:S(2)}, u32[]{:S(2)}) collective-permute-start(bf16[512,512]{1,0:T(8,128)(2,1)S(1)} %collective-permute-done.x2), channel_id=1, source_target_pairs={{0,1},{1,0},{2,3},{3,2},{4,5},{5,4},{6,7},{7,6},{8,9},{9,8},{10,11... | collective-permute-start | bytes 1572872 | tf_op jit(solution)/shard_map/project/ppermute | solution.py:428
  19.4 7.4 %collective-permute-start.4 = (bf16[384,256]{1,0:T(8,128)(2,1)S(1)}, bf16[384,256]{1,0:T(8,128)(2,1)S(1)}, u32[]{:S(2)}, u32[]{:S(2)}) collective-permute-start(bf16[384,256]{1,0:T(8,128)(2,1)S(1)} %order.1.refs_0_.refs_1_), channel_id=1, source_target_pairs={{0,2},{1,3},{2,0},{3,1},{4,6},{5,7},{6,4},{7,5},{8,10},{9,11},{10,... | collective-permute-start | bytes 589832 | tf_op jit(solution)/shard_map/cache_gather/ppermute | solution.py:428
  19.9 6.8 %collective-permute-start.3 = (bf16[384,256]{1,0:T(8,128)(2,1)S(1)}, bf16[384,256]{1,0:T(8,128)(2,1)S(1)}, u32[]{:S(2)}, u32[]{:S(2)}) collective-permute-start(bf16[384,256]{1,0:T(8,128)(2,1)S(1)} %order.1.refs_0_.refs_1_), channel_id=1, source_target_pairs={{0,1},{1,0},{2,3},{3,2},{4,5},{5,4},{6,7},{7,6},{8,9},{9,8},{10,11... | collective-permute-start | bytes 589832 | tf_op jit(solution)/shard_map/cache_gather/ppermute | solution.py:428
  26.8 1.4 %collective-permute-start.5 = (bf16[384,256]{1,0:T(8,128)(2,1)S(1)}, bf16[384,256]{1,0:T(8,128)(2,1)S(1)}, u32[]{:S(2)}, u32[]{:S(2)}) collective-permute-start(bf16[384,256]{1,0:T(8,128)(2,1)S(1)} %collective-permute-done.4.refs_2_.refs_3_), channel_id=1, source_target_pairs={{0,1},{1,0},{2,3},{3,2},{4,5},{5,4},{6,7},{7,6},{8,9},{9,8},{10,11... | collective-permute-start | bytes 589832 | tf_op jit(solution)/shard_map/extend/ppermute | solution.py:428
  36.9 1.6 %collective-permute-start.6 = (bf16[256,512]{1,0:T(8,128)(2,1)S(1)}, bf16[256,512]{1,0:T(8,128)(2,1)S(1)}, u32[]{:S(2)}, u32[]{:S(2)}) collective-permute-start(bf16[256,512]{1,0:T(8,128)(2,1)S(1)} %get-tuple-element.73), channel_id=1, source_target_pairs={{0,1},{1,0},{2,3},{3,2},{4,5},{5,4},{6,7},{7,6},{8,9},{9,8},{10,11... | collective-permute-start | bytes 786440 | tf_op jit(solution)/shard_map/reduce/ppermute | solution.py:428
  38.6 10.5 %collective-permute-start.8 = (bf16[256,512]{1,0:T(8,128)(2,1)S(1)}, bf16[256,512]{1,0:T(8,128)(2,1)S(1)}, u32[]{:S(2)}, u32[]{:S(2)}) collective-permute-start(bf16[256,512]{1,0:T(8,128)(2,1)S(1)} %add_convert_fusion.1), channel_id=1, source_target_pairs={{0,2},{1,3},{2,0},{3,1},{4,6},{5,7},{6,4},{7,5},{8,10},{9,11},{10,... | collective-permute-start | bytes 786440 | tf_op jit(solution)/shard_map/reduce/ppermute | solution.py:428
  39.2 9.3 %collective-permute-start.9 = (bf16[4,64,256]{2,1,0:T(8,128)(2,1)S(1)}, bf16[4,64,256]{2,1,0:T(8,128)(2,1)S(1)}, u32[]{:S(2)}, u32[]{:S(2)}) collective-permute-start(bf16[4,64,256]{2,1,0:T(8,128)(2,1)S(1)} %get-tuple-element.84), channel_id=1, source_target_pairs={{0,4},{4,0},{8,12},{12,8},{16,20},{20,16},{24,28},{28,24},{1,5},{5... | collective-permute-start | bytes 393224 | tf_op jit(solution)/shard_map/extend/ppermute | solution.py:428
  48.5 1.6 %collective-permute-start.10 = (bf16[256,512]{1,0:T(8,128)(2,1)S(1)}, bf16[256,512]{1,0:T(8,128)(2,1)S(1)}, u32[]{:S(2)}, u32[]{:S(2)}) collective-permute-start(bf16[256,512]{1,0:T(8,128)(2,1)S(1)} %get-tuple-element.85), channel_id=1, source_target_pairs={{0,1},{1,0},{2,3},{3,2},{4,5},{5,4},{6,7},{7,6},{8,9},{9,8},{10,11... | collective-permute-start | bytes 786440 | tf_op jit(solution)/shard_map/reduce/ppermute | solution.py:428
  48.5 3.4 %collective-permute-start.7 = (bf16[512,512]{1,0:T(8,128)(2,1)S(1)}, bf16[512,512]{1,0:T(8,128)(2,1)S(1)}, u32[]{:S(2)}, u32[]{:S(2)}) collective-permute-start(bf16[512,512]{1,0:T(8,128)(2,1)S(1)} %get-tuple-element.79), channel_id=1, source_target_pairs={{0,1},{1,0},{2,3},{3,2},{4,5},{5,4},{6,7},{7,6},{8,9},{9,8},{10,11... | collective-permute-start | bytes 1572872 | tf_op jit(solution)/shard_map/finish/ppermute | solution.py:428
  50.1 8.4 %collective-permute-start.11 = (bf16[256,512]{1,0:T(8,128)(2,1)S(1)}, bf16[256,512]{1,0:T(8,128)(2,1)S(1)}, u32[]{:S(2)}, u32[]{:S(2)}) collective-permute-start(bf16[256,512]{1,0:T(8,128)(2,1)S(1)} %add_convert_fusion), channel_id=1, source_target_pairs={{0,2},{1,3},{2,0},{3,1},{4,6},{5,7},{6,4},{7,5},{8,10},{9,11},{10,... | collective-permute-start | bytes 786440 | tf_op jit(solution)/shard_map/reduce/ppermute | solution.py:428
  51.7 8.2 %collective-permute-start.13 = (bf16[2,64,256]{2,1,0:T(8,128)(2,1)S(1)}, bf16[2,64,256]{2,1,0:T(8,128)(2,1)S(1)}, u32[]{:S(2)}, u32[]{:S(2)}) collective-permute-start(bf16[2,64,256]{2,1,0:T(8,128)(2,1)S(1)} %get-tuple-element.95), channel_id=1, source_target_pairs={{0,16},{4,20},{8,24},{12,28},{16,0},{20,4},{24,8},{28,12},{1,17},{... | collective-permute-start | bytes 196616 | tf_op jit(solution)/shard_map/exchange/ppermute | solution.py:428
  51.8 8.1 %collective-permute-start.14 = (bf16[2,64,256]{2,1,0:T(8,128)(2,1)S(1)}, bf16[2,64,256]{2,1,0:T(8,128)(2,1)S(1)}, u32[]{:S(2)}, u32[]{:S(2)}) collective-permute-start(bf16[2,64,256]{2,1,0:T(8,128)(2,1)S(1)} %get-tuple-element.96), channel_id=1, source_target_pairs={{0,24},{4,28},{8,16},{12,20},{16,8},{20,12},{24,0},{28,4},{1,25},{... | collective-permute-start | bytes 196616 | tf_op jit(solution)/shard_map/exchange/ppermute | solution.py:428
  51.9 8.1 %collective-permute-start.12 = (bf16[2,64,256]{2,1,0:T(8,128)(2,1)S(1)}, bf16[2,64,256]{2,1,0:T(8,128)(2,1)S(1)}, u32[]{:S(2)}, u32[]{:S(2)}) collective-permute-start(bf16[2,64,256]{2,1,0:T(8,128)(2,1)S(1)} %get-tuple-element.94), channel_id=1, source_target_pairs={{0,8},{4,12},{8,0},{12,4},{16,24},{20,28},{24,16},{28,20},{1,9},{5... | collective-permute-start | bytes 196616 | tf_op jit(solution)/shard_map/finish/ppermute | solution.py:428

commit v6 on v4

--- a/solution.py
+++ b/solution.py
@@ -231,8 +231,9 @@
 
     tile_rows = ROW_TILE * heads
 
-    def queries(t):
-        return q_ref[pl.ds(start_row * heads + t * tile_rows, tile_rows), :]
+    def queries(t, first=0, count=heads):
+        at = start_row * heads + t * tile_rows + first * ROW_TILE
+        return q_ref[pl.ds(at, count * ROW_TILE), :]
 
     def old_keys(i):
         source = pl.ds(i * KEY_TILE, KEY_TILE)
@@ -246,36 +247,39 @@
             parts.append(ref[pl.ds(at, size), :])
         return jnp.concatenate(parts, axis=0)
 
-    def new_scores(t):
+    def new_scores(t, first=0, count=heads):
         known = start_row + t * ROW_TILE
-        scores = dot_t(queries(t), kv_ref[pl.ds(0, known + ROW_TILE), :hd])
-        to = lax.broadcasted_iota(jnp.int32, (tile_rows, ROW_TILE), 0) % ROW_TILE
-        by = lax.broadcasted_iota(jnp.int32, (tile_rows, ROW_TILE), 1)
+        scores = dot_t(queries(t, first, count), kv_ref[pl.ds(0, known + ROW_TILE), :hd])
+        to = lax.broadcasted_iota(jnp.int32, (count * ROW_TILE, ROW_TILE), 0) % ROW_TILE
+        by = lax.broadcasted_iota(jnp.int32, (count * ROW_TILE, ROW_TILE), 1)
         last = jnp.where(by <= to, scores[:, known:], MASKED)
         return jnp.concatenate([scores[:, :known], last], axis=1) if known else last
 
     def new_values(t):
         return new_ref[pl.ds(0, start_row + (t + 1) * ROW_TILE), :]
 
-    def put(t, both):
+    def put(t, both, first=0, count=heads):
         sums = both[:, :hd]
         inverse = pl.reciprocal(sums, approx=True)
         inverse = inverse * (2.0 - sums * inverse)
         out = (both[:, hd:] * inverse).astype(BF16)
-        for h in range(heads):
-            context[pl.ds(t * ROW_TILE, ROW_TILE), h * hd : (h + 1) * hd] = out[
-                h * ROW_TILE : (h + 1) * ROW_TILE
-            ]
+        for h in range(count):
+            to = slice((first + h) * hd, (first + h + 1) * hd)
+            context[pl.ds(t * ROW_TILE, ROW_TILE), to] = out[h * ROW_TILE : (h + 1) * ROW_TILE]
 
     def fast(used, begin):
         row_tiles = range(begin // ROW_TILE, min(begin + PART_ROWS, rows) // ROW_TILE)
-        steps = [(t, i) for t in row_tiles for i in range(used + 1)]
-
-        def score(t, i):
-            return new_scores(t) if i == used else dot_t(queries(t), old_keys(i))
+        count = max(heads // 2, 1)
+        groups = range(0, heads, count)
+        steps = [(t, g, i) for t in row_tiles for g in groups for i in range(used + 1)]
+
+        def score(t, g, i):
+            if i == used:
+                return new_scores(t, g, count)
+            return dot_t(queries(t, g, count), old_keys(i))
 
         ahead, both = score(*steps[0]), None
-        for at, (t, i) in enumerate(steps):
+        for at, (t, g, i) in enumerate(steps):
             scores = ahead
             if at + 1 < len(steps):
                 ahead = score(*steps[at + 1])
@@ -284,7 +288,7 @@
             part = dot(weights, values)
             both = part if i == 0 else both + part
             if i == used:
-                put(t, both)
+                put(t, both, g, count)
 
     def exact(t):
         column = lax.broadcasted_iota(jnp.int32, (tile_rows, group), 1)

time: 60.5 us -> 61.4 us (1.015); the launches traced: 59.3 us -> 60.9 us
  Pallas kernels: 22.1 us -> 28.3 us
  waiting for transfers between devices: 14.7 us -> 11.6 us
  starting transfers between devices: 17.6 us -> 16.1 us
    pallas_call x10, Pallas kernels: 22.1 us -> 28.3 us  [call(): pl.pallas_call(kernel, out_shape=out_shape, in_specs=in_specs, out_specs=...]
    ppermute x15, waiting for transfers between devices: 12.5 us -> 9.33 us  [swap(): return lax.ppermute(x, axis, [(i, i ^ bit) for i in range(size)])]
    ppermute x15, starting transfers between devices: 11.8 us -> 10.3 us  [swap(): return lax.ppermute(x, axis, [(i, i ^ bit) for i in range(size)])]
  transfers between devices with their start and end apart: 16 -> 16, of which waited for: 10 -> 8; matrix products, arithmetic and copies ran while one was open for 4% -> 4% of each run, Pallas kernels for 21% -> 31%
where the time goes in v6:
time: 61.4 us; the launch traced here: 60.9 us
  Pallas kernels  28.3 us (46%)
  starting transfers between devices  16.1 us (26%)
  waiting for transfers between devices  11.6 us (19%)
  other arithmetic  2.67 us (4%)
  between operations  2.23 us (4%)
    pallas_call x10, Pallas kernels, call(): pl.pallas_call(kernel, out_shape=out_shape, in_specs=in_specs, out_specs=...  28.3 us
    ppermute x15, starting transfers between devices, swap(): return lax.ppermute(x, axis, [(i, i ^ bit) for i in range(size)])  10.3 us
    ppermute x15, waiting for transfers between devices, swap(): return lax.ppermute(x, axis, [(i, i ^ bit) for i in range(size)])  9.33 us
    all_to_all x1, starting transfers between devices, exchange(): return lax.all_to_all(x, 'seq', split_axis=0, concat_axis=0, tiled=True)  5.81 us
    all_to_all x1, waiting for transfers between devices, exchange(): return lax.all_to_all(x, 'seq', split_axis=0, concat_axis=0, tiled=True)  2.26 us
  transfers between devices with their start and end apart: 16, of which 8 were waited for; matrix products, arithmetic and copies ran while one was open for 4% of the time, Pallas kernels for 31%

profile of v6, /device:TPU:0, one launch (start us, length us, event | category | flops | bytes accessed | tf_op | source)
XLA Modules:
  0.0 60.9 jit_solution(16297816282775759329)
XLA Ops:
  0.6 3.0 %collective-permute-start = (bf16[512,512]{1,0:T(8,128)(2,1)}, bf16[512,512]{1,0:T(8,128)(2,1)S(1)}, u32[]{:S(2)}, u32[]{:S(2)}) collective-permute-start(bf16[512,512]{1,0:T(8,128)(2,1)} %param.10), channel_id=1, source_target_pairs={{0,2},{1,3},{2,0},{3,1},{4,6},{5,7},{6,4},{7,5},{8,10},{9,11},{10,... | collective-permute-start | bytes 1572872 | tf_op jit(solution)/shard_map/tokens_gather/ppermute | solution.py:429
  3.7 0.7 %broadcast_maximum_fusion.1 = f32[2048]{0:T(1024)S(1)} fusion(f32[2048]{0:T(1024)} %param.11), kind=kLoop, calls=%fused_computation.3 | loop fusion | flops 2048 | bytes 16384 | tf_op jit(solution)/shard_map/cache_gather/max | solution.py:441
  4.4 5.8 %all-to-all-start = ((bf16[8,64,256]{2,1,0:T(8,128)(2,1)}), bf16[8,64,256]{2,1,0:T(8,128)(2,1)S(1)}, u32[]{:S(2)}, u32[]{:S(2)}) async-start(bf16[8,64,256]{2,1,0:T(8,128)(2,1)} %param.19), calls=%async_computation | async-start | bytes 524288 | tf_op jit(solution)/shard_map/cache_gather/all_to_all | solution.py:432
  11.5 1.1 %broadcast_maximum_fusion.x0.tokens_ref = bf16[512,512]{1,0:T(8,128)(2,1)S(1)} fusion(bf16[512,512]{1,0:T(8,128)(2,1)} %param.10), kind=kLoop, calls=%fused_computation.2 | loop fusion | flops 262144 | bytes 1048576 | tf_op jit(solution)/shard_map/cache_gather/max | solution.py:444
  12.6 3.2 %collective-permute-done.x2 = bf16[512,512]{1,0:T(8,128)(2,1)S(1)} collective-permute-done((bf16[512,512]{1,0:T(8,128)(2,1)}, bf16[512,512]{1,0:T(8,128)(2,1)S(1)}, u32[]{:S(2)}, u32[]{:S(2)}) %collective-permute-start) | collective-permute-done | bytes 524320 | tf_op jit(solution)/shard_map/tokens_gather/ppermute | solution.py:429
  15.8 0.7 %pad_add_fusion.plan_ref = s32[18]{0:T(128)S(1)} fusion(s32[8]{0:T(128)} %bitcast.7, s32[8]{0:T(128)} %bitcast.8, s32[1]{0:T(128)S(6)} %copy.16, s32[1]{0:T(128)S(6)} %copy.17), kind=kLoop, calls=%fused_computation.4 | loop fusion | flops 54 | bytes 144 | tf_op jit(solution)/shard_map/cache_gather/concatenate | solution.py:448
  16.5 2.3 %all-to-all-done = bf16[8,64,256]{2,1,0:T(8,128)(2,1)S(1)} async-done(((bf16[8,64,256]{2,1,0:T(8,128)(2,1)}), bf16[8,64,256]{2,1,0:T(8,128)(2,1)S(1)}, u32[]{:S(2)}, u32[]{:S(2)}) %all-to-all-start) | async-done | bytes 262176 | tf_op jit(solution)/shard_map/cache_gather/all_to_all | solution.py:432
  19.4 0.6 collective-permute-start.4
  20.7 4.1 %project.1 = (bf16[2048,128]{1,0:T(8,128)(2,1)S(1)}, bf16[512,256]{1,0:T(8,128)(2,1)S(1)}, bf16[512,256]{1,0:T(8,128)(2,1)S(1)}, f32[2,8,128]{2,1,0:T(8,128)S(1)}) custom-call(bf16[512,512]{1,0:T(8,128)(2,1)S(1)} %broadcast_maximum_fusion.x0.tokens_ref, bf16[512,512]{1,0:T(8,128)(2,1)S(1)} %collective-permute-done.1.x1, ...), custom_call_target="tpu_custom_call" | custom-call | flops 1610612736 | bytes 6307840 | tf_op jit(solution)/shard_map/project/project/pallas_call | solution.py:378
  24.8 1.2 %extend.1 = (bf16[4,64,256]{2,1,0:T(8,128)(2,1)S(1)}, bf16[4,64,256]{2,1,0:T(8,128)(2,1)S(1)}) custom-call(s32[18]{0:T(128)S(1)} %pad_add_fusion.plan_ref, bf16[512,256]{1,0:T(8,128)(2,1)S(1)} %get-tuple-element.63.kv_ref, bf16[512,256]{1,0:T(8,128)(2,1)S(1)} %bitcast.5), custom_call_target="tpu_custom_call" | custom-call | flops 268435456 | bytes 786504 | tf_op jit(solution)/shard_map/extend/extend/pallas_call | solution.py:378
  26.0 0.7 %collective-permute-done.4.refs_2_.refs_3_ = bf16[384,256]{1,0:T(8,128)(2,1)S(1)} collective-permute-done((bf16[384,256]{1,0:T(8,128)(2,1)S(1)}, bf16[384,256]{1,0:T(8,128)(2,1)S(1)}, u32[]{:S(2)}, u32[]{:S(2)}) %collective-permute-start.4) | collective-permute-done | bytes 196640 | tf_op jit(solution)/shard_map/cache_gather/ppermute | solution.py:429
  26.8 0.9 %early.1 = (bf16[1152,256]{1,0:T(8,128)(2,1)S(1)}, f32[8,128]{1,0:T(8,128)S(1)}) custom-call(s32[18]{0:T(128)S(1)} %pad_add_fusion.plan_ref, bf16[384,256]{1,0:T(8,128)(2,1)S(1)} %order.1.refs_0_.refs_1_, bf16[384,256]{1,0:T(8,128)(2,1)S(1)} %collective-permute-done.3.refs_1_.refs_2_, bf16[384,256]{1,0:T(8,128)(2,1)S(1)} %collective-permute-done.4.refs_2_.refs_3_), custom_call_target="tpu_custom_call" | custom-call | flops 1073741824 | bytes 1183816 | tf_op jit(solution)/shard_map/early/early/pallas_call | solution.py:378
  28.2 8.7 %attend.2 = (bf16[256,512]{1,0:T(8,128)(2,1)S(1)}, bf16[256,512]{1,0:T(8,128)(2,1)S(1)}, bf16[256,512]{1,0:T(8,128)(2,1)S(1)}, bf16[384,256]{1,0:T(8,128)(2,1)S(1)}, f32[8,128]{1,0:T(8,128)S(1)}) custom-call(s32[18]{0:T(128)S(1)} %pad_add_fusion.plan_ref, bf16[2048,128]{1,0:T(8,128)(2,1)S(1)} %get-tuple-element.74.q_ref, ...), custom_call_target="tpu_custom_call" | custom-call | flops 1476395008 | bytes 5521480 | tf_op jit(solution)/shard_map/attend/attend/pallas_call | solution.py:378
  37.1 1.4 %collective-permute-done.6 = bf16[256,512]{1,0:T(8,128)(2,1)S(1)} collective-permute-done((bf16[256,512]{1,0:T(8,128)(2,1)S(1)}, bf16[256,512]{1,0:T(8,128)(2,1)S(1)}, u32[]{:S(2)}, u32[]{:S(2)}) %collective-permute-start.6) | collective-permute-done | bytes 262176 | tf_op jit(solution)/shard_map/reduce/ppermute | solution.py:429
  38.6 0.6 collective-permute-start.8
  39.2 9.3 %attend.3 = (bf16[512,512]{1,0:T(8,128)(2,1)S(1)}, bf16[256,512]{1,0:T(8,128)(2,1)S(1)}, bf16[512,512]{1,0:T(8,128)(2,1)S(1)}, bf16[256,512]{1,0:T(8,128)(2,1)S(1)}) custom-call(s32[18]{0:T(128)S(1)} %pad_add_fusion.plan_ref, bf16[2048,128]{1,0:T(8,128)(2,1)S(1)} %get-tuple-element.74.q_ref, bf16[512,256]{1,0:T(8,128)(2,1)S(1)} %get-tuple-element.63.kv_ref, ...), custom_call_target="tpu_custom_call" | custom-call | flops 1610612736 | bytes 6570056 | tf_op jit(solution)/shard_map/attend/attend/pallas_call | solution.py:378
  49.0 1.0 %collective-permute-done.10 = bf16[256,512]{1,0:T(8,128)(2,1)S(1)} collective-permute-done((bf16[256,512]{1,0:T(8,128)(2,1)S(1)}, bf16[256,512]{1,0:T(8,128)(2,1)S(1)}, u32[]{:S(2)}, u32[]{:S(2)}) %collective-permute-start.10) | collective-permute-done | bytes 262176 | tf_op jit(solution)/shard_map/reduce/ppermute | solution.py:429
  50.1 1.6 %collective-permute-start.11 = (bf16[256,512]{1,0:T(8,128)(2,1)S(1)}, bf16[256,512]{1,0:T(8,128)(2,1)S(1)}, u32[]{:S(2)}, u32[]{:S(2)}) collective-permute-start(bf16[256,512]{1,0:T(8,128)(2,1)S(1)} %add_convert_fusion), channel_id=1, source_target_pairs={{0,2},{1,3},{2,0},{3,1},{4,6},{5,7},{6,4},{7,5},{8,10},{9,11},{10,... | collective-permute-start | bytes 786440 | tf_op jit(solution)/shard_map/reduce/ppermute | solution.py:429
  51.8 1.6 %collective-permute-start.14 = (bf16[2,64,256]{2,1,0:T(8,128)(2,1)S(1)}, bf16[2,64,256]{2,1,0:T(8,128)(2,1)S(1)}, u32[]{:S(2)}, u32[]{:S(2)}) collective-permute-start(bf16[2,64,256]{2,1,0:T(8,128)(2,1)S(1)} %get-tuple-element.96), channel_id=1, source_target_pairs={{0,24},{4,28},{8,16},{12,20},{16,8},{20,12},{24,0},{28,4},{1,25},{... | collective-permute-start | bytes 196616 | tf_op jit(solution)/shard_map/exchange/ppermute | solution.py:429
  53.5 1.8 %collective-permute-start.12 = (bf16[2,64,256]{2,1,0:T(8,128)(2,1)S(1)}, bf16[2,64,256]{2,1,0:T(8,128)(2,1)S(1)}, u32[]{:S(2)}, u32[]{:S(2)}) collective-permute-start(bf16[2,64,256]{2,1,0:T(8,128)(2,1)S(1)} %get-tuple-element.94), channel_id=1, source_target_pairs={{0,8},{4,12},{8,0},{12,4},{16,24},{20,28},{24,16},{28,20},{1,9},{5... | collective-permute-start | bytes 196616 | tf_op jit(solution)/shard_map/finish/ppermute | solution.py:429
  55.3 1.4 %finish.2.refs_0_ = bf16[512,512]{1,0:T(8,128)(2,1)} custom-call(s32[18]{0:T(128)S(1)} %pad_add_fusion.plan_ref, bf16[512,512]{1,0:T(8,128)(2,1)S(1)} %broadcast_maximum_fusion.x0.tokens_ref, bf16[512,512]{1,0:T(8,128)(2,1)S(1)} %get-tuple-element.78.near_ref, bf16[512,512]{1,0:T(8,128)(2,1)S(1)} %collective-permute-done.7.got_ref, ...), custom_call_target="tpu_custom_call" | custom-call | flops 524288 | bytes 2359368 | tf_op jit(solution)/shard_map/finish/finish/pallas_call | solution.py:378
  56.7 1.9 %collective-permute-done.11.crossed_ref = bf16[256,512]{1,0:T(8,128)(2,1)S(1)} collective-permute-done((bf16[256,512]{1,0:T(8,128)(2,1)S(1)}, bf16[256,512]{1,0:T(8,128)(2,1)S(1)}, u32[]{:S(2)}, u32[]{:S(2)}) %collective-permute-start.11) | collective-permute-done | bytes 262176 | tf_op jit(solution)/shard_map/reduce/ppermute | solution.py:429
  58.5 1.4 %finish.3 = bf16[512,512]{1,0:T(8,128)(2,1)} custom-call(s32[18]{0:T(128)S(1)} %pad_add_fusion.plan_ref, bf16[512,512]{1,0:T(8,128)(2,1)S(1)} %broadcast_maximum_fusion.x0.tokens_ref, bf16[512,512]{1,0:T(8,128)(2,1)S(1)} %get-tuple-element.78.near_ref, bf16[512,512]{1,0:T(8,128)(2,1)S(1)} %collective-permute-done.7.got_ref, ...), custom_call_target="tpu_custom_call", output_to_operand_aliasing={{}: (5, {})} | custom-call | flops 524288 | bytes 2883656 | tf_op jit(solution)/shard_map/finish/finish/pallas_call | solution.py:378
  60.0 0.8 %place.1 = bf16[8,64,256]{2,1,0:T(8,128)(2,1)} custom-call(bf16[2,64,256]{2,1,0:T(8,128)(2,1)S(1)} %get-tuple-element.98.p0, bf16[2,64,256]{2,1,0:T(8,128)(2,1)S(1)} %collective-permute-done.12.p1, bf16[2,64,256]{2,1,0:T(8,128)(2,1)S(1)} %collective-permute-done.13.p2, bf16[2,64,256]{2,1,0:T(8,128)(2,1)S(1)} %collective-permute-done.14.p3), custom_call_target="tpu_custom_call" | custom-call | bytes 524288 | tf_op jit(solution)/shard_map/finish/place/pallas_call | solution.py:378
  (24 shorter events, 2.9 us)
Async XLA Ops:
  0.6 15.2 %collective-permute-start = (bf16[512,512]{1,0:T(8,128)(2,1)}, bf16[512,512]{1,0:T(8,128)(2,1)S(1)}, u32[]{:S(2)}, u32[]{:S(2)}) collective-permute-start(bf16[512,512]{1,0:T(8,128)(2,1)} %param.10), channel_id=1, source_target_pairs={{0,2},{1,3},{2,0},{3,1},{4,6},{5,7},{6,4},{7,5},{8,10},{9,11},{10,... | collective-permute-start | bytes 1572872 | tf_op jit(solution)/shard_map/tokens_gather/ppermute | solution.py:429
  4.4 14.4 %all-to-all-start = ((bf16[8,64,256]{2,1,0:T(8,128)(2,1)}), bf16[8,64,256]{2,1,0:T(8,128)(2,1)S(1)}, u32[]{:S(2)}, u32[]{:S(2)}) async-start(bf16[8,64,256]{2,1,0:T(8,128)(2,1)} %param.19), calls=%async_computation | async-start | bytes 524288 | tf_op jit(solution)/shard_map/cache_gather/all_to_all | solution.py:432
  10.2 10.0 %collective-permute-start.1 = (bf16[512,512]{1,0:T(8,128)(2,1)}, bf16[512,512]{1,0:T(8,128)(2,1)S(1)}, u32[]{:S(2)}, u32[]{:S(2)}) collective-permute-start(bf16[512,512]{1,0:T(8,128)(2,1)} %param.10), channel_id=1, source_target_pairs={{0,1},{1,0},{2,3},{3,2},{4,5},{5,4},{6,7},{7,6},{8,9},{9,8},{10,11... | collective-permute-start | bytes 1572872 | tf_op jit(solution)/shard_map/tokens_gather/ppermute | solution.py:429
  18.8 1.9 %collective-permute-start.2 = (bf16[512,512]{1,0:T(8,128)(2,1)S(1)}, bf16[512,512]{1,0:T(8,128)(2,1)S(1)}, u32[]{:S(2)}, u32[]{:S(2)}) collective-permute-start(bf16[512,512]{1,0:T(8,128)(2,1)S(1)} %collective-permute-done.x2), channel_id=1, source_target_pairs={{0,1},{1,0},{2,3},{3,2},{4,5},{5,4},{6,7},{7,6},{8,9},{9,8},{10,11... | collective-permute-start | bytes 1572872 | tf_op jit(solution)/shard_map/project/ppermute | solution.py:429
  19.4 7.4 %collective-permute-start.4 = (bf16[384,256]{1,0:T(8,128)(2,1)S(1)}, bf16[384,256]{1,0:T(8,128)(2,1)S(1)}, u32[]{:S(2)}, u32[]{:S(2)}) collective-permute-start(bf16[384,256]{1,0:T(8,128)(2,1)S(1)} %order.1.refs_0_.refs_1_), channel_id=1, source_target_pairs={{0,2},{1,3},{2,0},{3,1},{4,6},{5,7},{6,4},{7,5},{8,10},{9,11},{10,... | collective-permute-start | bytes 589832 | tf_op jit(solution)/shard_map/cache_gather/ppermute | solution.py:429
  19.9 6.8 %collective-permute-start.3 = (bf16[384,256]{1,0:T(8,128)(2,1)S(1)}, bf16[384,256]{1,0:T(8,128)(2,1)S(1)}, u32[]{:S(2)}, u32[]{:S(2)}) collective-permute-start(bf16[384,256]{1,0:T(8,128)(2,1)S(1)} %order.1.refs_0_.refs_1_), channel_id=1, source_target_pairs={{0,1},{1,0},{2,3},{3,2},{4,5},{5,4},{6,7},{7,6},{8,9},{9,8},{10,11... | collective-permute-start | bytes 589832 | tf_op jit(solution)/shard_map/cache_gather/ppermute | solution.py:429
  26.8 1.4 %collective-permute-start.5 = (bf16[384,256]{1,0:T(8,128)(2,1)S(1)}, bf16[384,256]{1,0:T(8,128)(2,1)S(1)}, u32[]{:S(2)}, u32[]{:S(2)}) collective-permute-start(bf16[384,256]{1,0:T(8,128)(2,1)S(1)} %collective-permute-done.4.refs_2_.refs_3_), channel_id=1, source_target_pairs={{0,1},{1,0},{2,3},{3,2},{4,5},{5,4},{6,7},{7,6},{8,9},{9,8},{10,11... | collective-permute-start | bytes 589832 | tf_op jit(solution)/shard_map/extend/ppermute | solution.py:429
  36.9 1.6 %collective-permute-start.6 = (bf16[256,512]{1,0:T(8,128)(2,1)S(1)}, bf16[256,512]{1,0:T(8,128)(2,1)S(1)}, u32[]{:S(2)}, u32[]{:S(2)}) collective-permute-start(bf16[256,512]{1,0:T(8,128)(2,1)S(1)} %get-tuple-element.73), channel_id=1, source_target_pairs={{0,1},{1,0},{2,3},{3,2},{4,5},{5,4},{6,7},{7,6},{8,9},{9,8},{10,11... | collective-permute-start | bytes 786440 | tf_op jit(solution)/shard_map/reduce/ppermute | solution.py:429
  38.6 10.5 %collective-permute-start.8 = (bf16[256,512]{1,0:T(8,128)(2,1)S(1)}, bf16[256,512]{1,0:T(8,128)(2,1)S(1)}, u32[]{:S(2)}, u32[]{:S(2)}) collective-permute-start(bf16[256,512]{1,0:T(8,128)(2,1)S(1)} %add_convert_fusion.1), channel_id=1, source_target_pairs={{0,2},{1,3},{2,0},{3,1},{4,6},{5,7},{6,4},{7,5},{8,10},{9,11},{10,... | collective-permute-start | bytes 786440 | tf_op jit(solution)/shard_map/reduce/ppermute | solution.py:429
  39.2 9.3 %collective-permute-start.9 = (bf16[4,64,256]{2,1,0:T(8,128)(2,1)S(1)}, bf16[4,64,256]{2,1,0:T(8,128)(2,1)S(1)}, u32[]{:S(2)}, u32[]{:S(2)}) collective-permute-start(bf16[4,64,256]{2,1,0:T(8,128)(2,1)S(1)} %get-tuple-element.84), channel_id=1, source_target_pairs={{0,4},{4,0},{8,12},{12,8},{16,20},{20,16},{24,28},{28,24},{1,5},{5... | collective-permute-start | bytes 393224 | tf_op jit(solution)/shard_map/extend/ppermute | solution.py:429
  48.5 1.6 %collective-permute-start.10 = (bf16[256,512]{1,0:T(8,128)(2,1)S(1)}, bf16[256,512]{1,0:T(8,128)(2,1)S(1)}, u32[]{:S(2)}, u32[]{:S(2)}) collective-permute-start(bf16[256,512]{1,0:T(8,128)(2,1)S(1)} %get-tuple-element.85), channel_id=1, source_target_pairs={{0,1},{1,0},{2,3},{3,2},{4,5},{5,4},{6,7},{7,6},{8,9},{9,8},{10,11... | collective-permute-start | bytes 786440 | tf_op jit(solution)/shard_map/reduce/ppermute | solution.py:429
  48.5 4.9 %collective-permute-start.7 = (bf16[512,512]{1,0:T(8,128)(2,1)S(1)}, bf16[512,512]{1,0:T(8,128)(2,1)S(1)}, u32[]{:S(2)}, u32[]{:S(2)}) collective-permute-start(bf16[512,512]{1,0:T(8,128)(2,1)S(1)} %get-tuple-element.79), channel_id=1, source_target_pairs={{0,1},{1,0},{2,3},{3,2},{4,5},{5,4},{6,7},{7,6},{8,9},{9,8},{10,11... | collective-permute-start | bytes 1572872 | tf_op jit(solution)/shard_map/finish/ppermute | solution.py:429
  50.1 8.4 %collective-permute-start.11 = (bf16[256,512]{1,0:T(8,128)(2,1)S(1)}, bf16[256,512]{1,0:T(8,128)(2,1)S(1)}, u32[]{:S(2)}, u32[]{:S(2)}) collective-permute-start(bf16[256,512]{1,0:T(8,128)(2,1)S(1)} %add_convert_fusion), channel_id=1, source_target_pairs={{0,2},{1,3},{2,0},{3,1},{4,6},{5,7},{6,4},{7,5},{8,10},{9,11},{10,... | collective-permute-start | bytes 786440 | tf_op jit(solution)/shard_map/reduce/ppermute | solution.py:429
  51.7 8.2 %collective-permute-start.13 = (bf16[2,64,256]{2,1,0:T(8,128)(2,1)S(1)}, bf16[2,64,256]{2,1,0:T(8,128)(2,1)S(1)}, u32[]{:S(2)}, u32[]{:S(2)}) collective-permute-start(bf16[2,64,256]{2,1,0:T(8,128)(2,1)S(1)} %get-tuple-element.95), channel_id=1, source_target_pairs={{0,16},{4,20},{8,24},{12,28},{16,0},{20,4},{24,8},{28,12},{1,17},{... | collective-permute-start | bytes 196616 | tf_op jit(solution)/shard_map/exchange/ppermute | solution.py:429
  51.8 8.1 %collective-permute-start.14 = (bf16[2,64,256]{2,1,0:T(8,128)(2,1)S(1)}, bf16[2,64,256]{2,1,0:T(8,128)(2,1)S(1)}, u32[]{:S(2)}, u32[]{:S(2)}) collective-permute-start(bf16[2,64,256]{2,1,0:T(8,128)(2,1)S(1)} %get-tuple-element.96), channel_id=1, source_target_pairs={{0,24},{4,28},{8,16},{12,20},{16,8},{20,12},{24,0},{28,4},{1,25},{... | collective-permute-start | bytes 196616 | tf_op jit(solution)/shard_map/exchange/ppermute | solution.py:429
  53.5 6.5 %collective-permute-start.12 = (bf16[2,64,256]{2,1,0:T(8,128)(2,1)S(1)}, bf16[2,64,256]{2,1,0:T(8,128)(2,1)S(1)}, u32[]{:S(2)}, u32[]{:S(2)}) collective-permute-start(bf16[2,64,256]{2,1,0:T(8,128)(2,1)S(1)} %get-tuple-element.94), channel_id=1, source_target_pairs={{0,8},{4,12},{8,0},{12,4},{16,24},{20,28},{24,16},{28,20},{1,9},{5... | collective-permute-start | bytes 196616 | tf_op jit(solution)/shard_map/finish/ppermute | solution.py:429

commit v7 on v6

--- a/solution.py
+++ b/solution.py
@@ -355,14 +355,14 @@
 def finish_kernel(at, plan_ref, tokens_ref, near_ref, got_ref, crossed_ref, *refs):
     out_hbm, done, sems = refs[-3:]
     rows = crossed_ref.shape[0]
-    half = rows // 2
+    size = rows // 4
     stores = []
-    for i in range(2):
-        here = pl.ds(i * half, half)
-        there = pl.ds(at + i * half, half)
+    for i in range(4):
+        here = pl.ds(i * size, size)
+        there = pl.ds(at + i * size, size)
         kept = near_ref[there, :].astype(F32) + got_ref[there, :].astype(F32)
         total = tokens_ref[there, :].astype(F32) + (kept + crossed_ref[here, :].astype(F32))
-        row = lax.broadcasted_iota(jnp.int32, total.shape, 0) + (at + i * half)
+        row = lax.broadcasted_iota(jnp.int32, total.shape, 0) + (at + i * size)
         done[here, :] = jnp.where(row < plan_ref[1], total, 0.0).astype(BF16)
         stores.append(pltpu.make_async_copy(done.at[here], out_hbm.at[there], sems.at[i]))
         stores[-1].start()
@@ -606,7 +606,7 @@
                 [SMEM] + [VMEM] * 4 + [HBM] * (at > 0),
                 (plan, own, near0, got0, over, *([mixed] if at else [])),
                 flops=4 * part * cols,
-                scratch=[pltpu.VMEM((part, cols), BF16), pltpu.SemaphoreType.DMA((2,))],
+                scratch=[pltpu.VMEM((part, cols), BF16), pltpu.SemaphoreType.DMA((4,))],
                 name="finish",
                 into={5: 0} if at else {},
             )

time: 61.4 us -> 61 us (level)
  Pallas kernels: 28.3 us -> 20.7 us
  starting transfers between devices: 16.1 us -> 23.6 us
    pallas_call x10, Pallas kernels: 28.3 us -> 20.7 us  [call(): pl.pallas_call(kernel, out_shape=out_shape, in_specs=in_specs, out_specs=...]
    ppermute x15, starting transfers between devices: 10.3 us -> 17.8 us  [swap(): return lax.ppermute(x, axis, [(i, i ^ bit) for i in range(size)])]
  transfers between devices with their start and end apart: 16 -> 16, of which waited for: 8 -> 10; matrix products, arithmetic and copies ran while one was open for 4% -> 4% of each run, Pallas kernels for 31% -> 25%
where the time goes in v7:
time: 61 us; the launch traced here: 60.8 us
  starting transfers between devices  23.6 us (39%)
  Pallas kernels  20.7 us (34%)
  waiting for transfers between devices  11.6 us (19%)
  other arithmetic  2.67 us (4%)
  between operations  2.21 us (4%)
    pallas_call x10, Pallas kernels, call(): pl.pallas_call(kernel, out_shape=out_shape, in_specs=in_specs, out_specs=...  20.7 us
    ppermute x15, starting transfers between devices, swap(): return lax.ppermute(x, axis, [(i, i ^ bit) for i in range(size)])  17.8 us
    ppermute x15, waiting for transfers between devices, swap(): return lax.ppermute(x, axis, [(i, i ^ bit) for i in range(size)])  9.37 us
    all_to_all x1, starting transfers between devices, exchange(): return lax.all_to_all(x, 'seq', split_axis=0, concat_axis=0, tiled=True)  5.81 us
    all_to_all x1, waiting for transfers between devices, exchange(): return lax.all_to_all(x, 'seq', split_axis=0, concat_axis=0, tiled=True)  2.26 us
  transfers between devices with their start and end apart: 16, of which 10 were waited for; matrix products, arithmetic and copies ran while one was open for 4% of the time, Pallas kernels for 25%

profile of v7, /device:TPU:0, one launch (start us, length us, event | category | flops | bytes accessed | tf_op | source)
XLA Modules:
  0.0 60.8 jit_solution(308494083104164411)
XLA Ops:
  0.6 3.0 %collective-permute-start = (bf16[512,512]{1,0:T(8,128)(2,1)}, bf16[512,512]{1,0:T(8,128)(2,1)S(1)}, u32[]{:S(2)}, u32[]{:S(2)}) collective-permute-start(bf16[512,512]{1,0:T(8,128)(2,1)} %param.10), channel_id=1, source_target_pairs={{0,2},{1,3},{2,0},{3,1},{4,6},{5,7},{6,4},{7,5},{8,10},{9,11},{10,... | collective-permute-start | bytes 1572872 | tf_op jit(solution)/shard_map/tokens_gather/ppermute | solution.py:429
  3.7 0.7 %broadcast_maximum_fusion.1 = f32[2048]{0:T(1024)S(1)} fusion(f32[2048]{0:T(1024)} %param.11), kind=kLoop, calls=%fused_computation.3 | loop fusion | flops 2048 | bytes 16384 | tf_op jit(solution)/shard_map/cache_gather/max | solution.py:441
  4.4 5.8 %all-to-all-start = ((bf16[8,64,256]{2,1,0:T(8,128)(2,1)}), bf16[8,64,256]{2,1,0:T(8,128)(2,1)S(1)}, u32[]{:S(2)}, u32[]{:S(2)}) async-start(bf16[8,64,256]{2,1,0:T(8,128)(2,1)} %param.19), calls=%async_computation | async-start | bytes 524288 | tf_op jit(solution)/shard_map/cache_gather/all_to_all | solution.py:432
  11.5 1.1 %broadcast_maximum_fusion.x0.tokens_ref = bf16[512,512]{1,0:T(8,128)(2,1)S(1)} fusion(bf16[512,512]{1,0:T(8,128)(2,1)} %param.10), kind=kLoop, calls=%fused_computation.2 | loop fusion | flops 262144 | bytes 1048576 | tf_op jit(solution)/shard_map/cache_gather/max | solution.py:444
  12.6 3.2 %collective-permute-done.x2 = bf16[512,512]{1,0:T(8,128)(2,1)S(1)} collective-permute-done((bf16[512,512]{1,0:T(8,128)(2,1)}, bf16[512,512]{1,0:T(8,128)(2,1)S(1)}, u32[]{:S(2)}, u32[]{:S(2)}) %collective-permute-start) | collective-permute-done | bytes 524320 | tf_op jit(solution)/shard_map/tokens_gather/ppermute | solution.py:429
  15.8 0.7 %pad_add_fusion.plan_ref = s32[18]{0:T(128)S(1)} fusion(s32[8]{0:T(128)} %bitcast.7, s32[8]{0:T(128)} %bitcast.8, s32[1]{0:T(128)S(6)} %copy.16, s32[1]{0:T(128)S(6)} %copy.17), kind=kLoop, calls=%fused_computation.4 | loop fusion | flops 54 | bytes 144 | tf_op jit(solution)/shard_map/cache_gather/concatenate | solution.py:448
  16.5 2.3 %all-to-all-done = bf16[8,64,256]{2,1,0:T(8,128)(2,1)S(1)} async-done(((bf16[8,64,256]{2,1,0:T(8,128)(2,1)}), bf16[8,64,256]{2,1,0:T(8,128)(2,1)S(1)}, u32[]{:S(2)}, u32[]{:S(2)}) %all-to-all-start) | async-done | bytes 262176 | tf_op jit(solution)/shard_map/cache_gather/all_to_all | solution.py:432
  20.7 4.1 %project.1 = (bf16[2048,128]{1,0:T(8,128)(2,1)S(1)}, bf16[512,256]{1,0:T(8,128)(2,1)S(1)}, bf16[512,256]{1,0:T(8,128)(2,1)S(1)}, f32[2,8,128]{2,1,0:T(8,128)S(1)}) custom-call(bf16[512,512]{1,0:T(8,128)(2,1)S(1)} %broadcast_maximum_fusion.x0.tokens_ref, bf16[512,512]{1,0:T(8,128)(2,1)S(1)} %collective-permute-done.1.x1, ...), custom_call_target="tpu_custom_call" | custom-call | flops 1610612736 | bytes 6307840 | tf_op jit(solution)/shard_map/project/project/pallas_call | solution.py:378
  24.8 1.2 %extend.1 = (bf16[4,64,256]{2,1,0:T(8,128)(2,1)S(1)}, bf16[4,64,256]{2,1,0:T(8,128)(2,1)S(1)}) custom-call(s32[18]{0:T(128)S(1)} %pad_add_fusion.plan_ref, bf16[512,256]{1,0:T(8,128)(2,1)S(1)} %get-tuple-element.63.kv_ref, bf16[512,256]{1,0:T(8,128)(2,1)S(1)} %bitcast.5), custom_call_target="tpu_custom_call" | custom-call | flops 268435456 | bytes 786504 | tf_op jit(solution)/shard_map/extend/extend/pallas_call | solution.py:378
  26.0 0.7 %collective-permute-done.4.refs_2_.refs_3_ = bf16[384,256]{1,0:T(8,128)(2,1)S(1)} collective-permute-done((bf16[384,256]{1,0:T(8,128)(2,1)S(1)}, bf16[384,256]{1,0:T(8,128)(2,1)S(1)}, u32[]{:S(2)}, u32[]{:S(2)}) %collective-permute-start.4) | collective-permute-done | bytes 196640 | tf_op jit(solution)/shard_map/cache_gather/ppermute | solution.py:429
  26.8 0.9 %early.1 = (bf16[1152,256]{1,0:T(8,128)(2,1)S(1)}, f32[8,128]{1,0:T(8,128)S(1)}) custom-call(s32[18]{0:T(128)S(1)} %pad_add_fusion.plan_ref, bf16[384,256]{1,0:T(8,128)(2,1)S(1)} %order.1.refs_0_.refs_1_, bf16[384,256]{1,0:T(8,128)(2,1)S(1)} %collective-permute-done.3.refs_1_.refs_2_, bf16[384,256]{1,0:T(8,128)(2,1)S(1)} %collective-permute-done.4.refs_2_.refs_3_), custom_call_target="tpu_custom_call" | custom-call | flops 1073741824 | bytes 1183816 | tf_op jit(solution)/shard_map/early/early/pallas_call | solution.py:378
  28.2 5.0 %attend.2 = (bf16[256,512]{1,0:T(8,128)(2,1)S(1)}, bf16[256,512]{1,0:T(8,128)(2,1)S(1)}, bf16[256,512]{1,0:T(8,128)(2,1)S(1)}, bf16[384,256]{1,0:T(8,128)(2,1)S(1)}, f32[8,128]{1,0:T(8,128)S(1)}) custom-call(s32[18]{0:T(128)S(1)} %pad_add_fusion.plan_ref, bf16[2048,128]{1,0:T(8,128)(2,1)S(1)} %get-tuple-element.74.q_ref, ...), custom_call_target="tpu_custom_call" | custom-call | flops 1476395008 | bytes 5521480 | tf_op jit(solution)/shard_map/attend/attend/pallas_call | solution.py:378
  33.4 1.4 %collective-permute-done.6 = bf16[256,512]{1,0:T(8,128)(2,1)S(1)} collective-permute-done((bf16[256,512]{1,0:T(8,128)(2,1)S(1)}, bf16[256,512]{1,0:T(8,128)(2,1)S(1)}, u32[]{:S(2)}, u32[]{:S(2)}) %collective-permute-start.6) | collective-permute-done | bytes 262176 | tf_op jit(solution)/shard_map/reduce/ppermute | solution.py:429
  35.4 1.4 %collective-permute-start.9 = (bf16[4,64,256]{2,1,0:T(8,128)(2,1)S(1)}, bf16[4,64,256]{2,1,0:T(8,128)(2,1)S(1)}, u32[]{:S(2)}, u32[]{:S(2)}) collective-permute-start(bf16[4,64,256]{2,1,0:T(8,128)(2,1)S(1)} %get-tuple-element.84), channel_id=1, source_target_pairs={{0,4},{4,0},{8,12},{12,8},{16,20},{20,16},{24,28},{28,24},{1,5},{5... | collective-permute-start | bytes 393224 | tf_op jit(solution)/shard_map/extend/ppermute | solution.py:429
  36.9 5.5 %attend.3 = (bf16[512,512]{1,0:T(8,128)(2,1)S(1)}, bf16[256,512]{1,0:T(8,128)(2,1)S(1)}, bf16[512,512]{1,0:T(8,128)(2,1)S(1)}, bf16[256,512]{1,0:T(8,128)(2,1)S(1)}) custom-call(s32[18]{0:T(128)S(1)} %pad_add_fusion.plan_ref, bf16[2048,128]{1,0:T(8,128)(2,1)S(1)} %get-tuple-element.74.q_ref, bf16[512,256]{1,0:T(8,128)(2,1)S(1)} %get-tuple-element.63.kv_ref, ...), custom_call_target="tpu_custom_call" | custom-call | flops 1610612736 | bytes 6570056 | tf_op jit(solution)/shard_map/attend/attend/pallas_call | solution.py:378
  43.3 0.7 %collective-permute-done.10 = bf16[256,512]{1,0:T(8,128)(2,1)S(1)} collective-permute-done((bf16[256,512]{1,0:T(8,128)(2,1)S(1)}, bf16[256,512]{1,0:T(8,128)(2,1)S(1)}, u32[]{:S(2)}, u32[]{:S(2)}) %collective-permute-start.10) | collective-permute-done | bytes 262176 | tf_op jit(solution)/shard_map/reduce/ppermute | solution.py:429
  44.1 1.6 %collective-permute-start.11 = (bf16[256,512]{1,0:T(8,128)(2,1)S(1)}, bf16[256,512]{1,0:T(8,128)(2,1)S(1)}, u32[]{:S(2)}, u32[]{:S(2)}) collective-permute-start(bf16[256,512]{1,0:T(8,128)(2,1)S(1)} %add_convert_fusion), channel_id=1, source_target_pairs={{0,2},{1,3},{2,0},{3,1},{4,6},{5,7},{6,4},{7,5},{8,10},{9,11},{10,... | collective-permute-start | bytes 786440 | tf_op jit(solution)/shard_map/reduce/ppermute | solution.py:429
  45.7 4.4 %collective-permute-start.13 = (bf16[2,64,256]{2,1,0:T(8,128)(2,1)S(1)}, bf16[2,64,256]{2,1,0:T(8,128)(2,1)S(1)}, u32[]{:S(2)}, u32[]{:S(2)}) collective-permute-start(bf16[2,64,256]{2,1,0:T(8,128)(2,1)S(1)} %get-tuple-element.95), channel_id=1, source_target_pairs={{0,16},{4,20},{8,24},{12,28},{16,0},{20,4},{24,8},{28,12},{1,17},{... | collective-permute-start | bytes 196616 | tf_op jit(solution)/shard_map/exchange/ppermute | solution.py:429
  50.1 5.2 %collective-permute-start.14 = (bf16[2,64,256]{2,1,0:T(8,128)(2,1)S(1)}, bf16[2,64,256]{2,1,0:T(8,128)(2,1)S(1)}, u32[]{:S(2)}, u32[]{:S(2)}) collective-permute-start(bf16[2,64,256]{2,1,0:T(8,128)(2,1)S(1)} %get-tuple-element.96), channel_id=1, source_target_pairs={{0,24},{4,28},{8,16},{12,20},{16,8},{20,12},{24,0},{28,4},{1,25},{... | collective-permute-start | bytes 196616 | tf_op jit(solution)/shard_map/exchange/ppermute | solution.py:429
  55.3 1.4 %finish.2.refs_0_ = bf16[512,512]{1,0:T(8,128)(2,1)} custom-call(s32[18]{0:T(128)S(1)} %pad_add_fusion.plan_ref, bf16[512,512]{1,0:T(8,128)(2,1)S(1)} %broadcast_maximum_fusion.x0.tokens_ref, bf16[512,512]{1,0:T(8,128)(2,1)S(1)} %get-tuple-element.78.near_ref, bf16[512,512]{1,0:T(8,128)(2,1)S(1)} %collective-permute-done.7.got_ref, ...), custom_call_target="tpu_custom_call" | custom-call | flops 524288 | bytes 2359368 | tf_op jit(solution)/shard_map/finish/finish/pallas_call | solution.py:378
  56.6 1.4 %finish.3 = bf16[512,512]{1,0:T(8,128)(2,1)} custom-call(s32[18]{0:T(128)S(1)} %pad_add_fusion.plan_ref, bf16[512,512]{1,0:T(8,128)(2,1)S(1)} %broadcast_maximum_fusion.x0.tokens_ref, bf16[512,512]{1,0:T(8,128)(2,1)S(1)} %get-tuple-element.78.near_ref, bf16[512,512]{1,0:T(8,128)(2,1)S(1)} %collective-permute-done.7.got_ref, ...), custom_call_target="tpu_custom_call", output_to_operand_aliasing={{}: (5, {})} | custom-call | flops 524288 | bytes 2883656 | tf_op jit(solution)/shard_map/finish/finish/pallas_call | solution.py:378
  58.0 1.2 %collective-permute-done.14.p3 = bf16[2,64,256]{2,1,0:T(8,128)(2,1)S(1)} collective-permute-done((bf16[2,64,256]{2,1,0:T(8,128)(2,1)S(1)}, bf16[2,64,256]{2,1,0:T(8,128)(2,1)S(1)}, u32[]{:S(2)}, u32[]{:S(2)}) %collective-permute-start.14) | collective-permute-done | bytes 65568 | tf_op jit(solution)/shard_map/exchange/ppermute | solution.py:429
  59.2 0.7 %collective-permute-done.12.p1 = bf16[2,64,256]{2,1,0:T(8,128)(2,1)S(1)} collective-permute-done((bf16[2,64,256]{2,1,0:T(8,128)(2,1)S(1)}, bf16[2,64,256]{2,1,0:T(8,128)(2,1)S(1)}, u32[]{:S(2)}, u32[]{:S(2)}) %collective-permute-start.12) | collective-permute-done | bytes 65568 | tf_op jit(solution)/shard_map/finish/ppermute | solution.py:429
  59.9 0.8 %place.1 = bf16[8,64,256]{2,1,0:T(8,128)(2,1)} custom-call(bf16[2,64,256]{2,1,0:T(8,128)(2,1)S(1)} %get-tuple-element.98.p0, bf16[2,64,256]{2,1,0:T(8,128)(2,1)S(1)} %collective-permute-done.12.p1, bf16[2,64,256]{2,1,0:T(8,128)(2,1)S(1)} %collective-permute-done.13.p2, bf16[2,64,256]{2,1,0:T(8,128)(2,1)S(1)} %collective-permute-done.14.p3), custom_call_target="tpu_custom_call" | custom-call | bytes 524288 | tf_op jit(solution)/shard_map/finish/place/pallas_call | solution.py:378
  (24 shorter events, 4.3 us)
Async XLA Ops:
  0.6 15.2 %collective-permute-start = (bf16[512,512]{1,0:T(8,128)(2,1)}, bf16[512,512]{1,0:T(8,128)(2,1)S(1)}, u32[]{:S(2)}, u32[]{:S(2)}) collective-permute-start(bf16[512,512]{1,0:T(8,128)(2,1)} %param.10), channel_id=1, source_target_pairs={{0,2},{1,3},{2,0},{3,1},{4,6},{5,7},{6,4},{7,5},{8,10},{9,11},{10,... | collective-permute-start | bytes 1572872 | tf_op jit(solution)/shard_map/tokens_gather/ppermute | solution.py:429
  4.4 14.4 %all-to-all-start = ((bf16[8,64,256]{2,1,0:T(8,128)(2,1)}), bf16[8,64,256]{2,1,0:T(8,128)(2,1)S(1)}, u32[]{:S(2)}, u32[]{:S(2)}) async-start(bf16[8,64,256]{2,1,0:T(8,128)(2,1)} %param.19), calls=%async_computation | async-start | bytes 524288 | tf_op jit(solution)/shard_map/cache_gather/all_to_all | solution.py:432
  10.2 10.0 %collective-permute-start.1 = (bf16[512,512]{1,0:T(8,128)(2,1)}, bf16[512,512]{1,0:T(8,128)(2,1)S(1)}, u32[]{:S(2)}, u32[]{:S(2)}) collective-permute-start(bf16[512,512]{1,0:T(8,128)(2,1)} %param.10), channel_id=1, source_target_pairs={{0,1},{1,0},{2,3},{3,2},{4,5},{5,4},{6,7},{7,6},{8,9},{9,8},{10,11... | collective-permute-start | bytes 1572872 | tf_op jit(solution)/shard_map/tokens_gather/ppermute | solution.py:429
  18.8 1.9 %collective-permute-start.2 = (bf16[512,512]{1,0:T(8,128)(2,1)S(1)}, bf16[512,512]{1,0:T(8,128)(2,1)S(1)}, u32[]{:S(2)}, u32[]{:S(2)}) collective-permute-start(bf16[512,512]{1,0:T(8,128)(2,1)S(1)} %collective-permute-done.x2), channel_id=1, source_target_pairs={{0,1},{1,0},{2,3},{3,2},{4,5},{5,4},{6,7},{7,6},{8,9},{9,8},{10,11... | collective-permute-start | bytes 1572872 | tf_op jit(solution)/shard_map/project/ppermute | solution.py:429
  19.4 7.4 %collective-permute-start.4 = (bf16[384,256]{1,0:T(8,128)(2,1)S(1)}, bf16[384,256]{1,0:T(8,128)(2,1)S(1)}, u32[]{:S(2)}, u32[]{:S(2)}) collective-permute-start(bf16[384,256]{1,0:T(8,128)(2,1)S(1)} %order.1.refs_0_.refs_1_), channel_id=1, source_target_pairs={{0,2},{1,3},{2,0},{3,1},{4,6},{5,7},{6,4},{7,5},{8,10},{9,11},{10,... | collective-permute-start | bytes 589832 | tf_op jit(solution)/shard_map/cache_gather/ppermute | solution.py:429
  19.9 6.8 %collective-permute-start.3 = (bf16[384,256]{1,0:T(8,128)(2,1)S(1)}, bf16[384,256]{1,0:T(8,128)(2,1)S(1)}, u32[]{:S(2)}, u32[]{:S(2)}) collective-permute-start(bf16[384,256]{1,0:T(8,128)(2,1)S(1)} %order.1.refs_0_.refs_1_), channel_id=1, source_target_pairs={{0,1},{1,0},{2,3},{3,2},{4,5},{5,4},{6,7},{7,6},{8,9},{9,8},{10,11... | collective-permute-start | bytes 589832 | tf_op jit(solution)/shard_map/cache_gather/ppermute | solution.py:429
  26.8 1.4 %collective-permute-start.5 = (bf16[384,256]{1,0:T(8,128)(2,1)S(1)}, bf16[384,256]{1,0:T(8,128)(2,1)S(1)}, u32[]{:S(2)}, u32[]{:S(2)}) collective-permute-start(bf16[384,256]{1,0:T(8,128)(2,1)S(1)} %collective-permute-done.4.refs_2_.refs_3_), channel_id=1, source_target_pairs={{0,1},{1,0},{2,3},{3,2},{4,5},{5,4},{6,7},{7,6},{8,9},{9,8},{10,11... | collective-permute-start | bytes 589832 | tf_op jit(solution)/shard_map/extend/ppermute | solution.py:429
  33.2 1.6 %collective-permute-start.6 = (bf16[256,512]{1,0:T(8,128)(2,1)S(1)}, bf16[256,512]{1,0:T(8,128)(2,1)S(1)}, u32[]{:S(2)}, u32[]{:S(2)}) collective-permute-start(bf16[256,512]{1,0:T(8,128)(2,1)S(1)} %get-tuple-element.73), channel_id=1, source_target_pairs={{0,1},{1,0},{2,3},{3,2},{4,5},{5,4},{6,7},{7,6},{8,9},{9,8},{10,11... | collective-permute-start | bytes 786440 | tf_op jit(solution)/shard_map/reduce/ppermute | solution.py:429
  34.8 8.4 %collective-permute-start.8 = (bf16[256,512]{1,0:T(8,128)(2,1)S(1)}, bf16[256,512]{1,0:T(8,128)(2,1)S(1)}, u32[]{:S(2)}, u32[]{:S(2)}) collective-permute-start(bf16[256,512]{1,0:T(8,128)(2,1)S(1)} %add_convert_fusion.1), channel_id=1, source_target_pairs={{0,2},{1,3},{2,0},{3,1},{4,6},{5,7},{6,4},{7,5},{8,10},{9,11},{10,... | collective-permute-start | bytes 786440 | tf_op jit(solution)/shard_map/reduce/ppermute | solution.py:429
  35.4 7.0 %collective-permute-start.9 = (bf16[4,64,256]{2,1,0:T(8,128)(2,1)S(1)}, bf16[4,64,256]{2,1,0:T(8,128)(2,1)S(1)}, u32[]{:S(2)}, u32[]{:S(2)}) collective-permute-start(bf16[4,64,256]{2,1,0:T(8,128)(2,1)S(1)} %get-tuple-element.84), channel_id=1, source_target_pairs={{0,4},{4,0},{8,12},{12,8},{16,20},{20,16},{24,28},{28,24},{1,5},{5... | collective-permute-start | bytes 393224 | tf_op jit(solution)/shard_map/extend/ppermute | solution.py:429
  42.4 1.6 %collective-permute-start.10 = (bf16[256,512]{1,0:T(8,128)(2,1)S(1)}, bf16[256,512]{1,0:T(8,128)(2,1)S(1)}, u32[]{:S(2)}, u32[]{:S(2)}) collective-permute-start(bf16[256,512]{1,0:T(8,128)(2,1)S(1)} %get-tuple-element.85), channel_id=1, source_target_pairs={{0,1},{1,0},{2,3},{3,2},{4,5},{5,4},{6,7},{7,6},{8,9},{9,8},{10,11... | collective-permute-start | bytes 786440 | tf_op jit(solution)/shard_map/reduce/ppermute | solution.py:429
  42.5 12.8 %collective-permute-start.7 = (bf16[512,512]{1,0:T(8,128)(2,1)S(1)}, bf16[512,512]{1,0:T(8,128)(2,1)S(1)}, u32[]{:S(2)}, u32[]{:S(2)}) collective-permute-start(bf16[512,512]{1,0:T(8,128)(2,1)S(1)} %get-tuple-element.79), channel_id=1, source_target_pairs={{0,1},{1,0},{2,3},{3,2},{4,5},{5,4},{6,7},{7,6},{8,9},{9,8},{10,11... | collective-permute-start | bytes 1572872 | tf_op jit(solution)/shard_map/finish/ppermute | solution.py:429
  44.1 12.6 %collective-permute-start.11 = (bf16[256,512]{1,0:T(8,128)(2,1)S(1)}, bf16[256,512]{1,0:T(8,128)(2,1)S(1)}, u32[]{:S(2)}, u32[]{:S(2)}) collective-permute-start(bf16[256,512]{1,0:T(8,128)(2,1)S(1)} %add_convert_fusion), channel_id=1, source_target_pairs={{0,2},{1,3},{2,0},{3,1},{4,6},{5,7},{6,4},{7,5},{8,10},{9,11},{10,... | collective-permute-start | bytes 786440 | tf_op jit(solution)/shard_map/reduce/ppermute | solution.py:429
  45.7 12.3 %collective-permute-start.13 = (bf16[2,64,256]{2,1,0:T(8,128)(2,1)S(1)}, bf16[2,64,256]{2,1,0:T(8,128)(2,1)S(1)}, u32[]{:S(2)}, u32[]{:S(2)}) collective-permute-start(bf16[2,64,256]{2,1,0:T(8,128)(2,1)S(1)} %get-tuple-element.95), channel_id=1, source_target_pairs={{0,16},{4,20},{8,24},{12,28},{16,0},{20,4},{24,8},{28,12},{1,17},{... | collective-permute-start | bytes 196616 | tf_op jit(solution)/shard_map/exchange/ppermute | solution.py:429
  50.1 9.1 %collective-permute-start.14 = (bf16[2,64,256]{2,1,0:T(8,128)(2,1)S(1)}, bf16[2,64,256]{2,1,0:T(8,128)(2,1)S(1)}, u32[]{:S(2)}, u32[]{:S(2)}) collective-permute-start(bf16[2,64,256]{2,1,0:T(8,128)(2,1)S(1)} %get-tuple-element.96), channel_id=1, source_target_pairs={{0,24},{4,28},{8,16},{12,20},{16,8},{20,12},{24,0},{28,4},{1,25},{... | collective-permute-start | bytes 196616 | tf_op jit(solution)/shard_map/exchange/ppermute | solution.py:429
  55.3 4.6 %collective-permute-start.12 = (bf16[2,64,256]{2,1,0:T(8,128)(2,1)S(1)}, bf16[2,64,256]{2,1,0:T(8,128)(2,1)S(1)}, u32[]{:S(2)}, u32[]{:S(2)}) collective-permute-start(bf16[2,64,256]{2,1,0:T(8,128)(2,1)S(1)} %get-tuple-element.94), channel_id=1, source_target_pairs={{0,8},{4,12},{8,0},{12,4},{16,24},{20,28},{24,16},{28,20},{1,9},{5... | collective-permute-start | bytes 196616 | tf_op jit(solution)/shard_map/finish/ppermute | solution.py:429
